TPU v7x, 128 devices: a whole 4x4x4 slice. The times are simulated.
128 devices in a mesh: seq: 16 (over z, x), head: 8 (over y, core).
Axes of the slice: x: 4, y: 4, z: 4, core: 2. Of those that a mesh axis runs over, the one named last changes fastest.
Arguments:
- scaled_input: bfloat16 [16384, 16384], P('seq', 'head'), may hold values from -0.059814453 to 0.059814453
- out_grad: bfloat16 [16384, 16384], P('seq', 'head'), may hold values from -1.796875 to 1.796875
- write_proj: bfloat16 [16384, 128], P('seq'), may hold values from -0.5 to 0.5
- read_proj: bfloat16 [16384, 128], P('seq'), may hold values from -0.5 to 0.5
- log_decay: float32 [256, 16384], P('head', 'seq'), may hold values from -0.8 to 0, as said below
Outputs:
- grad_input: bfloat16 [16384, 16384], P('seq', 'head')
- grad_write: bfloat16 [16384, 128], P(('seq', 'head'))
- grad_read: bfloat16 [16384, 128], P(('seq', 'head'))
Inputs may be any that keep to these rules, and one draw needn't show every extreme that they name: `log_decay`: logarithms of the per-token decays of each head.
All inputs are finite; a program needn't handle non-finite values.
Results may differ from a plain program's by a relative error of at most 0.0045.
Values sent between devices are 32-bit elements; how exact they have to be, the bound alone decides.
No kernel may reach another device: no remote copies, remote signals or barrier semaphores. Data moves between devices by JAX's collectives and lax.ppermute only.
A program may use at most 192 MiB of HBM per device.

v0:
```python
import jax
import jax.numpy as jnp
from jax import lax
from jax.sharding import PartitionSpec as P

BLOCK = 256


precise = lax.Precision.HIGH


def block_terms(
    inputs, grads, writes, reads, cumulative, scaled_in, scaled_grad, to_end, entering, leaving
):
    length = cumulative.shape[1]
    token_positions = jnp.arange(length)
    upper = token_positions[None, :] >= token_positions[:, None]
    spread = cumulative[:, None, :] - cumulative[:, :, None]
    decay_mat = jnp.exp(jnp.where(upper[None], spread, -jnp.inf))
    pairs = jnp.dot(writes, reads.T, preferred_element_type=jnp.float32)
    weights_x = (decay_mat * pairs[None]).astype(jnp.bfloat16)
    intra = jnp.einsum("hij,jhp->ihp", weights_x, grads, preferred_element_type=jnp.float32)
    inter = to_end.T[:, :, None] * jnp.einsum(
        "in,hnp->ihp", writes.astype(jnp.float32), leaving, precision=precise
    )
    grad_input = (intra + inter).astype(jnp.bfloat16).reshape(length, -1)
    cross = jnp.einsum("ihp,jhp->hij", inputs, grads, preferred_element_type=jnp.float32)
    weights_w = (decay_mat * cross).astype(jnp.bfloat16)
    part_write = jnp.einsum(
        "hij,jn->in", weights_w, reads, preferred_element_type=jnp.float32
    ) + jnp.einsum("ihp,hnp->in", scaled_in, leaving, precision=precise)
    part_read = jnp.einsum(
        "hij,in->jn", weights_w, writes, preferred_element_type=jnp.float32
    ) + jnp.einsum("jhp,hnp->jn", scaled_grad, entering, precision=precise)
    return (grad_input, part_write, part_read)


def body(scaled_input, out_grad, write_proj, read_proj, log_decay):
    tokens_here, width = scaled_input.shape
    heads_here = log_decay.shape[0]
    head_size = width // heads_here
    state_size = write_proj.shape[1]
    count = tokens_here // BLOCK
    inputs = scaled_input.reshape(count, BLOCK, heads_here, head_size)
    grads = out_grad.reshape(count, BLOCK, heads_here, head_size)
    writes = write_proj.reshape(count, BLOCK, state_size)
    reads = read_proj.reshape(count, BLOCK, state_size)
    cumulative = jnp.cumsum(log_decay.reshape(heads_here, count, BLOCK), axis=2)
    to_end = jnp.exp(cumulative[:, :, -1:] - cumulative)
    from_start = jnp.exp(cumulative)
    block_decay = from_start[:, :, -1]
    scaled_ins = []
    scaled_grads = []
    local_writes = []
    local_reads = []
    for number in range(count):
        scaled_in = to_end[:, number].T[:, :, None] * inputs[number].astype(jnp.float32)
        scaled_grad = from_start[:, number].T[:, :, None] * grads[number].astype(jnp.float32)
        scaled_ins.append(scaled_in)
        scaled_grads.append(scaled_grad)
        local_writes.append(
            jnp.einsum(
                "in,ihp->hnp", writes[number].astype(jnp.float32), scaled_in, precision=precise
            )
        )
        local_reads.append(
            jnp.einsum(
                "in,ihp->hnp", reads[number].astype(jnp.float32), scaled_grad, precision=precise
            )
        )
    zero_state = jnp.zeros((heads_here, state_size, head_size), jnp.float32)
    write_summary = zero_state
    for number in range(count):
        write_summary = block_decay[:, number][:, None, None] * write_summary + local_writes[number]
    read_summary = zero_state
    for number in reversed(range(count)):
        read_summary = block_decay[:, number][:, None, None] * read_summary + local_reads[number]
    device_decay = jnp.prod(block_decay, axis=1)
    every_decay, every_write, every_read = (
        lax.all_gather(device_decay[None], "seq", axis=0, tiled=True),
        lax.all_gather(write_summary[None], "seq", axis=0, tiled=True),
        lax.all_gather(read_summary[None], "seq", axis=0, tiled=True),
    )
    position = lax.axis_index("seq")
    shards = lax.axis_size("seq")

    def forward_step(number, carried):
        updated = every_decay[number][:, None, None] * carried + every_write[number]
        return jnp.where(number < position, updated, carried)

    def backward_step(number, carried):
        which = shards - 1 - number
        updated = every_decay[which][:, None, None] * carried + every_read[which]
        return jnp.where(which > position, updated, carried)

    entering_dev = lax.fori_loop(0, shards, forward_step, zero_state)
    leaving_dev = lax.fori_loop(0, shards, backward_step, zero_state)
    entering_blocks = []
    carried = entering_dev
    for number in range(count):
        entering_blocks.append(carried)
        carried = block_decay[:, number][:, None, None] * carried + local_writes[number]
    leaving_blocks = [zero_state] * count
    carried = leaving_dev
    for number in reversed(range(count)):
        leaving_blocks[number] = carried
        carried = block_decay[:, number][:, None, None] * carried + local_reads[number]
    input_parts = []
    write_parts = []
    read_parts = []
    for number in range(count):
        grad_block, write_block, read_block = block_terms(
            inputs[number],
            grads[number],
            writes[number],
            reads[number],
            cumulative[:, number],
            scaled_ins[number],
            scaled_grads[number],
            to_end[:, number],
            entering_blocks[number],
            leaving_blocks[number],
        )
        input_parts.append(grad_block)
        write_parts.append(write_block)
        read_parts.append(read_block)
    grad_input = jnp.concatenate(input_parts, axis=0)
    part_write = jnp.concatenate(write_parts, axis=0)
    part_read = jnp.concatenate(read_parts, axis=0)
    shared_write, shared_read = (
        lax.psum_scatter(part_write, "head", scatter_dimension=0, tiled=True),
        lax.psum_scatter(part_read, "head", scatter_dimension=0, tiled=True),
    )
    return (grad_input, shared_write.astype(jnp.bfloat16), shared_read.astype(jnp.bfloat16))


def solution(mesh):
    return jax.shard_map(
        body,
        mesh=mesh,
        in_specs=(
            P("seq", "head"),
            P("seq", "head"),
            P("seq", None),
            P("seq", None),
            P("head", "seq"),
        ),
        out_specs=(P("seq", "head"), P(("seq", "head"), None), P(("seq", "head"), None)),
        check_vma=False,
    )
```

profile of v0, /device:TPU:1, one launch (start us, length us, event | category | flops | bytes accessed | tf_op | source)
XLA Modules:
  0.0 431.8 jit_solution(6072827228808040339)
XLA Ops:
  12.4 3.9 fusion.141
  28.7 4.4 %fusion.140 = (bf16[256,2048]{1,0:T(8,128)(2,1)}, bf16[256,2048]{1,0:T(8,128)(2,1)}, bf16[256,2048]{1,0:T(8,128)(2,1)}, bf16[256,2048]{1,0:T(8,128)(2,1)}) fusion(bf16[1024,2048]{1,0:T(8,128)(2,1)} %param.9), kind=kLoop, calls=%fused_computation.216 | loop fusion | bytes 8388608 | tf_op jit(solution)/shard_map/slice | solution.py:113
  51.2 37.0 %all-reduce = f32[512]{0:T(512)} all-reduce(f32[512]{0:T(512)S(1)} %dynamic-update-slice), channel_id=2, replica_groups=mesh['seq'=16,'head'=8] {'seq'}, use_global_device_ids=true, to_apply=%add | all-reduce | flops 512 | bytes 4096
  96.0 4.8 %convert_reduce_fusion = bf16[256,256]{1,0:T(8,128)(2,1)} fusion(f32[32,256]{1,0:T(8,128)S(1)} %get-tuple-element.345, pred[256,256]{1,0:T(8,128)(4,1)S(1)} %iota_compare_fusion, bf16[256,32,64]{0,2,1:T(8,128)(2,1)S(1)} %bitcast.231, bf16[256,32,64]{0,2,1:T(8,128)(2,1)} %bitcast.241), kind=kOutput, calls=%fused_computation.8 | convolution fusion | flops 280952832 | bytes 2326528 | tf_op jit(solution)/shard_map/ihp,jhp->hij/dot_general | solution.py:27
  100.8 3.7 convert_reduce_fusion.1
  104.5 3.7 convert_reduce_fusion.2
  111.2 32.6 %all-gather.6.cloned.1.call-done = f32[512,128,64]{1,2,0:T(8,128)} async-done(((f32[32,128,64]{1,2,0:T(8,128)}), f32[512,128,64]{1,2,0:T(8,128)}) %all-gather.6.cloned.1.call-update) | async-done | bytes 16777232 | tf_op jit(solution)/shard_map/all_gather | solution.py:82
  143.8 83.0 %while.30 = (s32[]{:T(128)}, f32[32,128,64]{2,1,0:T(8,128)}, s32[]{:T(128)}, f32[16,32]{1,0:T(8,128)S(1)}, f32[16,32,128,64]{2,3,1,0:T(8,128)}, /*index=5*/s32[]{:T(128)}, s32[]{:T(128)}, s32[]{:T(128)}, s32[]{:T(128)}) while((s32[]{:T(128)}, f32[32,128,64]{2,1,0:T(8,128)}, s32[]{:T(128)}, f32[16,32]{1,0:T(8,128)S(1)}, ...), condition=%wide.region_4.5_spmd.clone, body=%wide.region_3.4_spmd.clone.sunk | while | flops 1048584 | bytes 7340591 | solution.py:97
  149.3 3.2 fusion.174
  154.5 3.5 fusion.174
  160.0 3.2 fusion.174
  165.2 3.3 fusion.174
  170.4 3.3 fusion.174
  175.6 3.2 fusion.174
  180.8 3.2 fusion.174
  186.0 3.9 fusion.174
  197.1 3.3 fusion.174
  202.3 3.3 fusion.174
  207.6 3.3 fusion.174
  212.9 3.3 fusion.174
  218.2 3.3 fusion.174
  223.4 3.3 fusion.174
  235.4 4.1 fusion.67
  248.8 7.9 %all-gather.8.cloned.1.call-done = f32[512,128,64]{1,2,0:T(8,128)} async-done(((f32[32,128,64]{1,2,0:T(8,128)}), f32[512,128,64]{1,2,0:T(8,128)}) %all-gather.8.cloned.1.call-update) | async-done | bytes 16777232 | tf_op jit(solution)/shard_map/all_gather | solution.py:81
  256.7 89.1 %while.31 = (s32[]{:T(128)}, f32[32,128,64]{2,1,0:T(8,128)}, s32[]{:T(128)}, f32[16,32]{1,0:T(8,128)S(1)}, f32[16,32,128,64]{2,3,1,0:T(8,128)}, /*index=5*/s32[]{:T(128)}, s32[]{:T(128)}) while((s32[]{:T(128)}, f32[32,128,64]{2,1,0:T(8,128)}, s32[]{:T(128)}, f32[16,32]{1,0:T(8,128)S(1)}, f32[16,32,128,64]{2,3,1,0:T(8,128)}, ...), condition=%wide.region_11.12_spmd.clone, body=%wide.region_10.11_spmd.clone.sunk | while | flops 1048580 | bytes 7340529 | solution.py:96
  357.8 4.1 fusion.63
  365.5 5.7 %fusion.27 = bf16[256,32,64]{0,2,1:T(8,128)(2,1)} fusion(f32[32,64,256]{2,1,0:T(8,128)} %fusion.89, bf16[256,32,64]{0,2,1:T(8,128)(2,1)S(1)} %bitcast.244, f32[256,256]{1,0:T(8,128)} %fusion.112, f32[32,256]{1,0:T(8,128)} %copy-done.83, pred[256,256]{1,0:T(8,128)(4,1)} %copy-done.75, f32[256,32]{0,1:T(8,128)} %get-tuple-element.361), kind=kOutput, calls=%fused_computation.51 | convolution fusion | flops 278396928 | bytes 4587520 | tf_op jit(solution)/shard_map/hij,jhp->ihp/dot_general | solution.py:22
  372.1 5.4 %fusion.29 = bf16[256,32,64]{0,2,1:T(8,128)(2,1)} fusion(f32[32,64,256]{2,1,0:T(8,128)} %fusion.92, bf16[256,32,64]{0,2,1:T(8,128)(2,1)S(1)} %bitcast.240, f32[256,256]{1,0:T(8,128)} %fusion.108, f32[32,256]{1,0:T(8,128)S(1)} %copy-done.82, pred[256,256]{1,0:T(8,128)(4,1)S(1)} %copy-done.76, f32[256,32]{0,1:T(8,128)S(1)} %copy-done.63), kind=kOutput, calls=%fused_computation.54 | convolution fusion | flops 278396928 | bytes 4587520 | tf_op jit(solution)/shard_map/hij,jhp->ihp/dot_general | solution.py:22
  377.6 3.7 fusion.31
  388.7 5.1 %fusion.33 = bf16[256,32,64]{0,2,1:T(8,128)(2,1)} fusion(f32[32,64,256]{2,1,0:T(8,128)} %fusion.87, bf16[256,32,64]{0,2,1:T(8,128)(2,1)S(1)} %bitcast.229, f32[256,256]{1,0:T(8,128)S(1)} %copy-done.73, f32[32,256]{1,0:T(8,128)S(1)} %copy-done.78, pred[256,256]{1,0:T(8,128)(4,1)S(1)} %copy-done.76, f32[256,32]{0,1:T(8,128)S(1)} %copy-done.58), kind=kOutput, calls=%fused_computation.60 | convolution fusion | flops 278396928 | bytes 4587520 | tf_op jit(solution)/shard_map/hij,jhp->ihp/dot_general | solution.py:22
  396.2 3.3 pad_maximum_fusion
  401.0 22.6 %reduce-scatter.5.cloned.1.call-done = f32[128,128]{1,0:T(8,128)} async-done(((f32[1024,128]{1,0:T(8,128)}), f32[128,128]{1,0:T(8,128)}) %reduce-scatter.5.cloned.1.call-update) | async-done | bytes 65552 | tf_op jit(solution)/shard_map/reduce_scatter | solution.py:132
  (373 shorter events, 208.5 us)
Async XLA Ops:
  7.2 136.6 %all-gather.6.cloned.1.call-start = ((), (), s32[]{:S(2)}) async-start(), calls=%async_computation.4 | async-start | bytes 17825792 | tf_op jit(solution)/shard_map/all_gather | solution.py:82
  12.4 13.4 %copy-start.84 = (f32[32]{0:T(128)}, f32[32]{0:T(128)S(1)}, u32[]{:S(2)}) copy-start(f32[32]{0:T(128)S(1)} %get-tuple-element.356) | copy-start | bytes 388
  12.4 33.2 %copy-start.86 = (f32[32]{0:T(128)}, f32[32]{0:T(128)S(1)}, u32[]{:S(2)}) copy-start(f32[32]{0:T(128)S(1)} %get-tuple-element.355) | copy-start | bytes 388
  16.9 91.3 %copy-start.9 = (bf16[256,2048]{0,1:T(8,128)(2,1)}, bf16[256,2048]{0,1:T(8,128)(2,1)S(1)}, u32[]{:S(2)}) copy-start(bf16[256,2048]{0,1:T(8,128)(2,1)S(1)} %copy.88) | copy-start | bytes 3145732
  18.1 86.4 %copy-start.19 = (bf16[256,2048]{0,1:T(8,128)(2,1)}, bf16[256,2048]{0,1:T(8,128)(2,1)S(1)}, u32[]{:S(2)}) copy-start(bf16[256,2048]{0,1:T(8,128)(2,1)S(1)} %copy.91) | copy-start | bytes 3145732
  28.6 228.1 %all-gather.8.cloned.1.call-start = ((), (), s32[]{:S(2)}) async-start(), calls=%async_computation.5 | async-start | bytes 17825792 | tf_op jit(solution)/shard_map/all_gather | solution.py:81
  34.5 61.5 %copy-start.13 = (bf16[256,2048]{0,1:T(8,128)(2,1)}, bf16[256,2048]{0,1:T(8,128)(2,1)S(1)}, u32[]{:S(2)}) copy-start(bf16[256,2048]{0,1:T(8,128)(2,1)S(1)} %copy.102) | copy-start | bytes 3145732
  48.5 351.1 %reduce-scatter.3.cloned.1.call-start = ((), (), s32[]{:S(2)}) async-start(), calls=%async_computation.2 | async-start | bytes 589824 | tf_op jit(solution)/shard_map/reduce_scatter | solution.py:131
  89.0 19.2 %copy-start.75 = (pred[256,256]{1,0:T(8,128)(4,1)}, pred[256,256]{1,0:T(8,128)(4,1)S(1)}, u32[]{:S(2)}) copy-start(pred[256,256]{1,0:T(8,128)(4,1)S(1)} %iota_compare_fusion) | copy-start | bytes 196612
  89.0 11.8 %copy-start.83 = (f32[32,256]{1,0:T(8,128)}, f32[32,256]{1,0:T(8,128)S(1)}, u32[]{:S(2)}) copy-start(f32[32,256]{1,0:T(8,128)S(1)} %get-tuple-element.345) | copy-start | bytes 98308
  89.0 11.8 %copy-start.81 = (f32[32,256]{1,0:T(8,128)}, f32[32,256]{1,0:T(8,128)S(1)}, u32[]{:S(2)}) copy-start(f32[32,256]{1,0:T(8,128)S(1)} %get-tuple-element.346) | copy-start | bytes 98308
  89.0 15.5 %copy-start.79 = (f32[32,256]{1,0:T(8,128)}, f32[32,256]{1,0:T(8,128)S(1)}, u32[]{:S(2)}) copy-start(f32[32,256]{1,0:T(8,128)S(1)} %get-tuple-element.344) | copy-start | bytes 98308
  89.0 19.2 %copy-start.77 = (f32[32,256]{1,0:T(8,128)}, f32[32,256]{1,0:T(8,128)S(1)}, u32[]{:S(2)}) copy-start(f32[32,256]{1,0:T(8,128)S(1)} %get-tuple-element.343) | copy-start | bytes 98308
  96.0 4.8 %copy-start.23 = (bf16[256,2048]{0,1:T(8,128)(2,1)S(1)}, bf16[256,2048]{0,1:T(8,128)(2,1)}, u32[]{:S(2)}) copy-start(bf16[256,2048]{0,1:T(8,128)(2,1)} %copy-done.22) | copy-start | bytes 3145732
  96.0 4.8 %copy-start.39 = (bf16[256,2048]{0,1:T(8,128)(2,1)S(1)}, bf16[256,2048]{0,1:T(8,128)(2,1)}, u32[]{:S(2)}) copy-start(bf16[256,2048]{0,1:T(8,128)(2,1)} %copy.101) | copy-start | bytes 3145732
  230.2 13.9 %copy-start.2 = (f32[32,128,64]{1,2,0:T(8,128)}, f32[32,128,64]{1,2,0:T(8,128)S(1)}, u32[]{:S(2)}) copy-start(f32[32,128,64]{1,2,0:T(8,128)S(1)} %get-tuple-element.329) | copy-start | bytes 3145732
  230.4 5.0 %copy-start = (f32[32,128,64]{2,1,0:T(8,128)S(1)}, f32[32,128,64]{2,1,0:T(8,128)}, u32[]{:S(2)}) copy-start(f32[32,128,64]{2,1,0:T(8,128)} %get-tuple-element.229) | copy-start | bytes 3145732
  230.4 5.0 %copy-start.14 = (bf16[256,2048]{0,1:T(8,128)(2,1)S(1)}, bf16[256,2048]{0,1:T(8,128)(2,1)}, u32[]{:S(2)}) copy-start(bf16[256,2048]{0,1:T(8,128)(2,1)} %copy-done.13) | copy-start | bytes 3145732
  230.4 5.0 %copy-start.65 = (f32[256,32]{0,1:T(8,128)S(1)}, f32[256,32]{0,1:T(8,128)}, u32[]{:S(2)}) copy-start(f32[256,32]{0,1:T(8,128)} %get-tuple-element.361) | copy-start | bytes 98308
  350.1 5.0 %copy-start.20 = (bf16[256,2048]{0,1:T(8,128)(2,1)S(1)}, bf16[256,2048]{0,1:T(8,128)(2,1)}, u32[]{:S(2)}) copy-start(bf16[256,2048]{0,1:T(8,128)(2,1)} %copy-done.19) | copy-start | bytes 3145732
  350.1 5.0 %copy-start.68 = (f32[256,32]{0,1:T(8,128)S(1)}, f32[256,32]{0,1:T(8,128)}, u32[]{:S(2)}) copy-start(f32[256,32]{0,1:T(8,128)} %get-tuple-element.351) | copy-start | bytes 98308
  357.7 4.7 %copy-start.51 = (f32[256,128]{1,0:T(8,128)S(1)}, f32[256,128]{1,0:T(8,128)}, u32[]{:S(2)}) copy-start(f32[256,128]{1,0:T(8,128)} %fusion.64) | copy-start | bytes 393220
  363.5 60.1 %reduce-scatter.5.cloned.1.call-start = ((), (), s32[]{:S(2)}) async-start(), calls=%async_computation.3 | async-start | bytes 589824 | tf_op jit(solution)/shard_map/reduce_scatter | solution.py:132
  365.4 6.6 %copy-start.25 = (bf16[256,2048]{0,1:T(8,128)(2,1)S(1)}, bf16[256,2048]{0,1:T(8,128)(2,1)}, u32[]{:S(2)}) copy-start(bf16[256,2048]{0,1:T(8,128)(2,1)} %copy-done.22) | copy-start | bytes 3145732
  365.4 6.6 %copy-start.63 = (f32[256,32]{0,1:T(8,128)S(1)}, f32[256,32]{0,1:T(8,128)}, u32[]{:S(2)}) copy-start(f32[256,32]{0,1:T(8,128)} %get-tuple-element.360) | copy-start | bytes 98308
  365.4 6.6 %copy-start.76 = (pred[256,256]{1,0:T(8,128)(4,1)S(1)}, pred[256,256]{1,0:T(8,128)(4,1)}, u32[]{:S(2)}) copy-start(pred[256,256]{1,0:T(8,128)(4,1)} %copy-done.75) | copy-start | bytes 196612
  365.5 6.6 %copy-start.82 = (f32[32,256]{1,0:T(8,128)S(1)}, f32[32,256]{1,0:T(8,128)}, u32[]{:S(2)}) copy-start(f32[32,256]{1,0:T(8,128)} %copy-done.81) | copy-start | bytes 98308
  372.0 5.5 %copy-start.21 = (bf16[256,2048]{0,1:T(8,128)(2,1)S(1)}, bf16[256,2048]{0,1:T(8,128)(2,1)}, u32[]{:S(2)}) copy-start(bf16[256,2048]{0,1:T(8,128)(2,1)} %copy-done.19) | copy-start | bytes 3145732
  372.0 5.5 %copy-start.45 = (f32[32,64,256]{2,1,0:T(8,128)S(1)}, f32[32,64,256]{2,1,0:T(8,128)}, u32[]{:S(2)}) copy-start(f32[32,64,256]{2,1,0:T(8,128)} %fusion.95) | copy-start | bytes 6291460
  372.0 5.5 %copy-start.61 = (f32[256,32]{0,1:T(8,128)S(1)}, f32[256,32]{0,1:T(8,128)}, u32[]{:S(2)}) copy-start(f32[256,32]{0,1:T(8,128)} %get-tuple-element.359) | copy-start | bytes 98308
  372.1 5.5 %copy-start.74 = (f32[256,256]{1,0:T(8,128)S(1)}, f32[256,256]{1,0:T(8,128)}, u32[]{:S(2)}) copy-start(f32[256,256]{1,0:T(8,128)} %fusion.104) | copy-start | bytes 786436
  372.1 5.5 %copy-start.80 = (f32[32,256]{1,0:T(8,128)S(1)}, f32[32,256]{1,0:T(8,128)}, u32[]{:S(2)}) copy-start(f32[32,256]{1,0:T(8,128)} %copy-done.79) | copy-start | bytes 98308
  (61 other events, 169.5 us)
Sparse Core Ops, SparseCore 0:
  28.8 114.9 all-gather.5
  145.9 110.7 all-gather.7
  363.6 27.7 reduce-scatter.2
  393.8 29.7 reduce-scatter.4
where the time goes:
time: 440 us; the launch traced here: 432 us
  other arithmetic  115 us (26%)
  local copies, waits for them, and re-layouts  105 us (24%)
  matrix products  86.9 us (20%)
  waiting for transfers between devices  63.2 us (14%)
  blocking collectives  37 us (8%)
  between operations  15.7 us (4%)
  loops' own time  8.67 us (2%)
    select_n x16, other arithmetic, backward_step(): return jnp.where(which > position, updated, carried)  51.9 us
    select_n x16, other arithmetic, forward_step(): return jnp.where(number < position, updated, carried)  50.3 us
    unnamed x1, blocking collectives  37 us
    all_gather x1, waiting for transfers between devices, body(): lax.all_gather(read_summary[None], 'seq', axis=0, tiled=True)  32.6 us
    dynamic_slice x32, local copies, waits for them, and re-layouts, backward_step(): updated = every_decay[which][:, None, None] * carried + every_read[which]  30.5 us
    dynamic_slice x32, local copies, waits for them, and re-layouts, forward_step(): updated = every_decay[number][:, None, None] * carried + every_write[number]  30.4 us
    reduce_scatter x1, waiting for transfers between devices, body(): lax.psum_scatter(part_read, 'head', scatter_dimension=0, tiled=True)  22.6 us
    dot_general x4, matrix products, block_terms(): jnp.einsum('hij,jhp->ihp', weights_x, grads, preferred_element_type=jnp.f...  20 us
  transfers between devices with their start and end apart: 4, of which 3 were waited for; matrix products, arithmetic and copies ran while one was open for 43% of the time, Pallas kernels for 0%

commit v1 on v0

v1 whole, which is shorter than its diff:
```python
import jax
import jax.numpy as jnp
from jax import lax
from jax.experimental import pallas as pl
from jax.experimental.pallas import tpu as pltpu
from jax.sharding import PartitionSpec as P

SUB = 128
LANES = 128
WIDE = 256
MIDDLE = SUB // 2 - 1
F32 = jnp.float32
BF16 = jnp.bfloat16


def dot(a, b, dims=((1,), (0,)), precision=None):
    return lax.dot_general(a, b, (dims, ((), ())), precision=precision, preferred_element_type=F32)


def running_sum(decays, start):
    rows = lax.broadcasted_iota(jnp.int32, (SUB, SUB), 0)
    columns = lax.broadcasted_iota(jnp.int32, (SUB, SUB), 1)
    lower = jnp.where(rows >= columns, 1.0, 0.0).astype(F32)
    return dot(lower, decays[:, start : start + SUB], ((1,), (1,)), lax.Precision.HIGHEST)


def two_terms(values, heads):
    lane = lax.broadcasted_iota(jnp.int32, values.shape, 1)
    high = values.astype(BF16).astype(F32)
    kept = jnp.where(lane < heads, high, jnp.where(lane < 2 * heads, values - high, 0.0))
    return kept.astype(BF16)


def spread_matrix(heads, head_size, first_head):
    row = lax.broadcasted_iota(jnp.int32, (LANES, WIDE), 0)
    column = lax.broadcasted_iota(jnp.int32, (LANES, WIDE), 1)
    same = lax.rem(row, heads) == first_head + column // head_size
    return jnp.where(same, 1.0, 0.0).astype(BF16)


def repeated(decays):
    return jnp.concatenate([decays] * (LANES // decays.shape[0]), axis=0)


def summary_kernel(x_ref, g_ref, w_ref, r_ref, ld_ref, out_ref, sums, fx, fg, total, wt, rt):
    heads, tokens = ld_ref.shape
    head_size = x_ref.shape[1] * pl.num_programs(0) // heads
    step = pl.program_id(0)

    @pl.when(step == 0)
    def _():
        decays = repeated(ld_ref[...])
        offset = jnp.zeros((1, LANES), F32)
        for start in range(0, tokens, SUB):
            part = running_sum(decays, start) + offset
            sums[start : start + SUB] = part
            offset = part[SUB - 1 :]
            wt[:, start : start + SUB] = w_ref[start : start + SUB].T
            rt[:, start : start + SUB] = r_ref[start : start + SUB].T
        total[...] = two_terms(jnp.broadcast_to(jnp.exp(offset), (16, LANES)), heads)
        for start in range(0, tokens, SUB):
            part = sums[start : start + SUB]
            fx[start : start + SUB] = two_terms(jnp.exp(offset - part), heads)
            fg[start : start + SUB] = two_terms(jnp.exp(part), heads)

    spread = spread_matrix(heads, head_size, step * (WIDE // head_size))
    scaled_x = (x_ref[...].astype(F32) * dot(fx[...], spread)).astype(BF16)
    scaled_g = (g_ref[...].astype(F32) * dot(fg[...], spread)).astype(BF16)
    written = dot(wt[...], scaled_x)
    collected = dot(rt[...], scaled_g)
    decay = dot(total[...], spread)[:8]
    state = written.shape[0]
    for pair in range(WIDE // LANES):
        lanes = slice(pair * LANES, (pair + 1) * LANES)
        out_ref[pair, :state] = written[:, lanes]
        out_ref[pair, state : 2 * state] = collected[:, lanes]
        out_ref[pair, 2 * state :] = decay[:, lanes]


def scan_kernel(in_ref, out_ref):
    shards = in_ref.shape[0]
    state = out_ref.shape[1] // 2
    carried = jnp.zeros((state, LANES), F32)
    for shard in range(shards):
        out_ref[shard, :state] = carried
        carried = in_ref[shard, 2 * state : 2 * state + 1] * carried + in_ref[shard, :state]
    carried = jnp.zeros((state, LANES), F32)
    for shard in reversed(range(shards)):
        out_ref[shard, state:] = carried
        carried = in_ref[shard, 2 * state : 2 * state + 1] * carried + in_ref[shard, state : 2 * state]


def grads_kernel(
    x_ref, g_ref, st_ref, w_ref, r_ref, ld_ref, gi_ref, out_ref, fa, fb, fuv, pw, wt, rt, acc, scale, right
):
    heads, tokens = ld_ref.shape
    head_size = x_ref.shape[1] * pl.num_programs(0) // heads
    state = w_ref.shape[1]
    count = tokens // SUB
    step = pl.program_id(0)
    rows = lax.broadcasted_iota(jnp.int32, (SUB, SUB), 0)
    columns = lax.broadcasted_iota(jnp.int32, (SUB, SUB), 1)
    upper = columns >= rows

    @pl.when(step == 0)
    def _():
        decays = repeated(ld_ref[...])
        middles = []
        afters = []
        for k in range(count):
            tok = slice(k * SUB, (k + 1) * SUB)
            part = running_sum(decays, k * SUB)
            middle = part[MIDDLE : MIDDLE + 1]
            fa[tok] = two_terms(jnp.exp(middle - part), heads)
            fb[tok] = two_terms(jnp.exp(part - middle), heads)
            middles.append(middle)
            afters.append(part[SUB - 1 :] - middle)
            write, read = w_ref[tok], r_ref[tok]
            pairs = jnp.where(upper, dot(write, read, ((1,), (1,))), 0.0).astype(BF16)
            pw[k] = jnp.concatenate([pairs, write], axis=1)
            wt[k] = write.T
            rt[k] = read.T
        into = [middles[0]] + [middles[k] + afters[k - 1] for k in range(1, count)]
        back = [afters[k] + middles[k + 1] for k in range(count - 1)] + [afters[count - 1]]
        fuv[...] = two_terms(jnp.exp(jnp.concatenate(into + back, axis=0)), heads)
        acc[...] = jnp.zeros_like(acc)

    spread = spread_matrix(heads, head_size, step * (WIDE // head_size))
    factor = dot(fuv[...], spread)
    entering = jnp.concatenate([st_ref[p, :state] for p in range(WIDE // LANES)], axis=1)
    leaving = jnp.concatenate([st_ref[p, state:] for p in range(WIDE // LANES)], axis=1)

    back = factor[2 * count - 1 : 2 * count] * leaving
    for k in reversed(range(count)):
        tok = slice(k * SUB, (k + 1) * SUB)
        scaled_g = (g_ref[tok].astype(F32) * dot(fb[tok], spread)).astype(BF16)
        stacked = jnp.concatenate([scaled_g, back.astype(BF16)], axis=0)
        right[k] = stacked
        factors = dot(fa[tok], spread)
        scale[tok] = factors
        gi_ref[tok] = (factors * dot(pw[k], stacked)).astype(BF16)
        if k:
            back = factor[count + k - 1 : count + k] * (back + dot(rt[k], scaled_g))

    into = factor[:1] * entering
    for k in range(count):
        tok = slice(k * SUB, (k + 1) * SUB)
        scaled_x = (x_ref[tok].astype(F32) * scale[tok]).astype(BF16)
        stacked = jnp.concatenate([scaled_x, into.astype(BF16)], axis=0)
        acc[k] += dot(stacked, right[k], ((1,), (1,)))
        if k + 1 < count:
            into = factor[k + 1 : k + 2] * (into + dot(wt[k], scaled_x))

    @pl.when(step == pl.num_programs(0) - 1)
    def _():
        for k in range(count):
            tok = slice(k * SUB, (k + 1) * SUB)
            weights = jnp.where(upper, acc[k, :SUB, :SUB], 0.0).astype(BF16)
            out_ref[k, :, :state] = dot(weights, r_ref[tok]) + acc[k, :SUB, SUB:]
            out_ref[k, :, state:] = (dot(wt[k], weights) + acc[k, SUB:, :SUB]).T


def body(scaled_input, out_grad, write_proj, read_proj, log_decay):
    tokens, width = scaled_input.shape
    heads = log_decay.shape[0]
    state = write_proj.shape[1]
    shards = lax.axis_size("seq")
    count = tokens // SUB
    steps = width // WIDE
    pairs = WIDE // LANES
    wide = pl.BlockSpec((tokens, WIDE), lambda i: (0, i))
    whole = pl.BlockSpec((tokens, state), lambda i: (0, 0))
    decays = pl.BlockSpec((heads, tokens), lambda i: (0, 0))
    params = pltpu.CompilerParams(vmem_limit_bytes=48 * 2**20, dimension_semantics=("arbitrary",))

    summary = pl.pallas_call(
        summary_kernel,
        grid=(steps,),
        in_specs=[wide, wide, whole, whole, decays],
        out_specs=pl.BlockSpec((pairs, 2 * state + 8, LANES), lambda i: (i, 0, 0)),
        out_shape=jax.ShapeDtypeStruct((width // LANES, 2 * state + 8, LANES), F32),
        scratch_shapes=[
            pltpu.VMEM((tokens, LANES), F32),
            pltpu.VMEM((tokens, LANES), BF16),
            pltpu.VMEM((tokens, LANES), BF16),
            pltpu.VMEM((16, LANES), BF16),
            pltpu.VMEM((state, tokens), BF16),
            pltpu.VMEM((state, tokens), BF16),
        ],
        compiler_params=params,
        name="summary",
    )(scaled_input, out_grad, write_proj, read_proj, log_decay)

    every = lax.all_to_all(summary, "seq", 0, 0, tiled=True)
    states = pl.pallas_call(
        scan_kernel,
        out_shape=jax.ShapeDtypeStruct((shards, 2 * state, LANES), F32),
        compiler_params=pltpu.CompilerParams(vmem_limit_bytes=48 * 2**20),
        name="scan",
    )(every)
    own = lax.all_to_all(states, "seq", 0, 0, tiled=True)

    grad_input, parts = pl.pallas_call(
        grads_kernel,
        grid=(steps,),
        in_specs=[
            wide,
            wide,
            pl.BlockSpec((pairs, 2 * state, LANES), lambda i: (i, 0, 0)),
            whole,
            whole,
            decays,
        ],
        out_specs=[wide, pl.BlockSpec((count, SUB, 2 * state), lambda i: (0, 0, 0))],
        out_shape=[
            jax.ShapeDtypeStruct((tokens, width), BF16),
            jax.ShapeDtypeStruct((count, SUB, 2 * state), F32),
        ],
        scratch_shapes=[
            pltpu.VMEM((tokens, LANES), BF16),
            pltpu.VMEM((tokens, LANES), BF16),
            pltpu.VMEM((2 * count, LANES), BF16),
            pltpu.VMEM((count, SUB, SUB + state), BF16),
            pltpu.VMEM((count, state, SUB), BF16),
            pltpu.VMEM((count, state, SUB), BF16),
            pltpu.VMEM((count, SUB + state, SUB + state), F32),
            pltpu.VMEM((tokens, WIDE), F32),
            pltpu.VMEM((count, SUB + state, WIDE), BF16),
        ],
        compiler_params=params,
        name="grads",
    )(scaled_input, out_grad, own, write_proj, read_proj, log_decay)

    shared = lax.all_to_all(parts, "head", 0, 0, tiled=True).sum(axis=0)
    return grad_input, shared[:, :state].astype(BF16), shared[:, state:].astype(BF16)


def solution(mesh):
    return jax.shard_map(
        body,
        mesh=mesh,
        in_specs=(
            P("seq", "head"),
            P("seq", "head"),
            P("seq", None),
            P("seq", None),
            P("head", "seq"),
        ),
        out_specs=(P("seq", "head"), P(("seq", "head"), None), P(("seq", "head"), None)),
        check_vma=False,
    )
```

time: 440 us -> 127 us (0.29); the launches traced: 432 us -> 126 us
  other arithmetic: 115 us -> 0.07 us
  local copies, waits for them, and re-layouts: 105 us -> 3.45 us
  matrix products: 86.9 us -> 0 us
  waiting for transfers between devices: 63.2 us -> 0 us
  blocking collectives: 37 us -> 89 us
  Pallas kernels: 0 us -> 32.9 us
  between operations: 15.7 us -> 0.68 us
  loops' own time: 8.67 us -> 0 us
    select_n x32 -> x0, other arithmetic: 102 us -> none  [the longest x16 51.9 us: backward_step(): return jnp.where(which > position, updated, carried)]
    all_to_all x0 -> x3, blocking collectives: none -> 89 us  [the longest x1 36.3 us: body(): every = lax.all_to_all(summary, 'seq', 0, 0, tiled=True)]
    dot_general x40 -> x0, matrix products: 86.9 us -> none  [the longest x4 20 us: block_terms(): jnp.einsum('hij,jhp->ihp', weights_x, grads, preferred_element_type=jnp.f...]
    dynamic_slice x64 -> x0, local copies, waits for them, and re-layouts: 60.8 us -> none  [the longest x32 30.5 us: backward_step(): updated = every_decay[which][:, None, None] * carried + every_read[which]]
    all_gather x2 -> x0, waiting for transfers between devices: 40.5 us -> none  [the longest x1 32.6 us: body(): lax.all_gather(read_summary[None], 'seq', axis=0, tiled=True)]
    unnamed x1 -> x0, blocking collectives: 37 us -> none
    pallas_call x0 -> x3, Pallas kernels: none -> 32.9 us  [the longest x1 23.4 us: body(): pl.pallas_call(grads_kernel, grid=(steps,), in_specs=[wide, wide, pl.Bloc...]
    reduce_scatter x2 -> x0, waiting for transfers between devices: 22.6 us -> none  [the longest x1 22.6 us: body(): lax.psum_scatter(part_read, 'head', scatter_dimension=0, tiled=True)]
  transfers between devices with their start and end apart: 4 -> 0, of which waited for: 3 -> 0; matrix products, arithmetic and copies ran while one was open for 43% -> 0% of each run, Pallas kernels for 0% -> 0%
where the time goes in v1:
time: 127 us; the launch traced here: 126 us
  blocking collectives  89 us (70%)
  Pallas kernels  32.9 us (26%)
  local copies, waits for them, and re-layouts  3.45 us (3%)
    all_to_all x1, blocking collectives, body(): every = lax.all_to_all(summary, 'seq', 0, 0, tiled=True)  36.3 us
    all_to_all x1, blocking collectives, body(): own = lax.all_to_all(states, 'seq', 0, 0, tiled=True)  30.1 us
    pallas_call x1, Pallas kernels, body(): pl.pallas_call(grads_kernel, grid=(steps,), in_specs=[wide, wide, pl.Bloc...  23.4 us
    all_to_all x1, blocking collectives, body(): shared = lax.all_to_all(parts, 'head', 0, 0, tiled=True).sum(axis=0)  22.5 us
    pallas_call x1, Pallas kernels, body(): pl.pallas_call(summary_kernel, grid=(steps,), in_specs=[wide, wide, whole...  9.4 us
    unnamed x12, local copies, waits for them, and re-layouts  2.82 us

profile of v1, /device:TPU:1, one launch (start us, length us, event | category | flops | bytes accessed | tf_op | source)
XLA Modules:
  0.0 126.1 jit_solution(12384294478590611474)
XLA Ops:
  0.6 0.0 copy-start
  0.6 0.9 copy-done
  1.6 0.0 copy-start.2
  1.6 0.9 copy-done.2
  2.5 0.0 copy-start.4
  2.5 0.9 copy-done.4
  3.4 9.4 %summary.1 = f32[16,264,128]{2,1,0:T(8,128)S(1)} custom-call(bf16[1024,2048]{1,0:T(8,128)(2,1)} %x_ref.3, bf16[1024,2048]{1,0:T(8,128)(2,1)} %g_ref.3, bf16[1024,128]{1,0:T(8,128)(2,1)S(1)} %copy-done, bf16[1024,128]{1,0:T(8,128)(2,1)S(1)} %copy-done.2, f32[32,1024]{1,0:T(8,128)S(1)} %copy-done.4), custom_call_target="tpu_custom_call" | custom-call | tf_op jit(solution)/shard_map/summary/pallas_call | solution.py:176
  12.8 36.3 %all_to_all.15.in_ref = f32[16,264,128]{2,1,0:T(8,128)S(1)} all-to-all(f32[16,264,128]{2,1,0:T(8,128)S(1)} %summary.1), channel_id=1, replica_groups=mesh['seq'=16,'head'=8] {'seq'}, dimensions={0} | all-to-all | bytes 4325376 | tf_op jit(solution)/shard_map/all_to_all | solution.py:194
  49.2 0.2 scan.1
  49.4 0.0 copy-start.1
  49.4 0.0 copy-start.3
  49.4 0.0 copy-start.5
  49.4 30.1 %all_to_all.16.st_ref = f32[16,256,128]{2,1,0:T(8,128)S(1)} all-to-all(f32[16,256,128]{2,1,0:T(8,128)S(1)} %scan.1), channel_id=1, replica_groups=mesh['seq'=16,'head'=8] {'seq'}, dimensions={0} | all-to-all | bytes 4194304 | tf_op jit(solution)/shard_map/all_to_all | solution.py:201
  79.5 0.0 copy-done.1
  79.5 0.0 copy-done.3
  79.5 0.0 copy-done.5
  79.5 23.4 %grads.1 = (bf16[1024,2048]{1,0:T(8,128)(2,1)}, f32[8,128,256]{2,1,0:T(8,128)S(1)}) custom-call(bf16[1024,2048]{1,0:T(8,128)(2,1)} %x_ref.3, bf16[1024,2048]{1,0:T(8,128)(2,1)} %g_ref.3, f32[16,256,128]{2,1,0:T(8,128)S(1)} %all_to_all.16.st_ref, bf16[1024,128]{1,0:T(8,128)(2,1)S(1)} %copy-done.1, bf16[1024,128]{1,0:T(8,128)(2,1)S(1)} %copy-done.3, ...), custom_call_target="tpu_custom_call" | custom-call | tf_op jit(solution)/shard_map/grads/pallas_call | solution.py:203
  102.9 22.5 %all_to_all.17 = f32[8,128,256]{2,1,0:T(8,128)S(1)} all-to-all(f32[8,128,256]{2,1,0:T(8,128)S(1)} %get-tuple-element.6), channel_id=1, replica_groups=mesh['seq'=16,'head'=8] {'head'}, dimensions={0} | all-to-all | bytes 2097152 | tf_op jit(solution)/shard_map/all_to_all | solution.py:234
  125.4 0.1 reduce_sum.9
  125.5 0.6 fusion
Async XLA Ops:
  0.6 1.0 copy-start
  1.6 0.9 copy-start.2
  2.5 0.9 copy-start.4
  49.4 30.1 %copy-start.1 = (bf16[1024,128]{1,0:T(8,128)(2,1)S(1)}, bf16[1024,128]{1,0:T(8,128)(2,1)}, u32[]{:S(2)}) copy-start(bf16[1024,128]{1,0:T(8,128)(2,1)} %w_ref.3) | copy-start | bytes 786436
  49.4 30.1 %copy-start.3 = (bf16[1024,128]{1,0:T(8,128)(2,1)S(1)}, bf16[1024,128]{1,0:T(8,128)(2,1)}, u32[]{:S(2)}) copy-start(bf16[1024,128]{1,0:T(8,128)(2,1)} %r_ref.3) | copy-start | bytes 786436
  49.4 30.1 %copy-start.5 = (f32[32,1024]{1,0:T(8,128)S(1)}, f32[32,1024]{1,0:T(8,128)}, u32[]{:S(2)}) copy-start(f32[32,1024]{1,0:T(8,128)} %ld_ref.3) | copy-start | bytes 393220

commit v2 on v1

v2 whole, which is shorter than its diff:
```python
import jax
import jax.numpy as jnp
from jax import lax
from jax.experimental import pallas as pl
from jax.experimental.pallas import tpu as pltpu
from jax.sharding import PartitionSpec as P

SUB = 128
LANES = 128
WIDE = 512
WIDE2 = 1024
MIDDLE = SUB // 2 - 1
F32 = jnp.float32
BF16 = jnp.bfloat16


def dot(a, b, dims=((1,), (0,))):
    return lax.dot_general(a, b, (dims, ((), ())), preferred_element_type=F32)


def running_sums(decays):
    rows = lax.broadcasted_iota(jnp.int32, (SUB, SUB), 0)
    columns = lax.broadcasted_iota(jnp.int32, (SUB, SUB), 1)
    lower = jnp.where(rows >= columns, 1.0, 0.0).astype(BF16)
    first = decays.astype(BF16)
    left = decays - first.astype(F32)
    second = left.astype(BF16)
    third = (left - second.astype(F32)).astype(BF16)
    sums = []
    for start in range(0, decays.shape[1], SUB):
        tok = slice(start, start + SUB)
        a, b, c = (dot(lower, term[:, tok], ((1,), (1,))) for term in (first, second, third))
        sums.append(a + (b + c))
    return sums


def two_terms(values, heads):
    lane = lax.broadcasted_iota(jnp.int32, values.shape, 1)
    high = values.astype(BF16).astype(F32)
    kept = jnp.where(lane < heads, high, jnp.where(lane < 2 * heads, values - high, 0.0))
    return kept.astype(BF16)


def spread_matrix(heads, head_size, wide, step):
    row = lax.broadcasted_iota(jnp.int32, (LANES, wide), 0)
    column = lax.broadcasted_iota(jnp.int32, (LANES, wide), 1)
    same = lax.rem(row, heads) == (step * wide + column) // head_size
    return jnp.where(same, 1.0, 0.0).astype(BF16)


def summary_kernel(
    x_hbm, g_hbm, w_hbm, r_hbm, ld_hbm, out_ref, xs_ref, gs_ref, fa, between, pw, wt, rt, fb, ends, xb, gb, w_ref, r_ref, ld_ref, sems
):
    heads, tokens = ld_ref.shape
    width = xs_ref.shape[1]
    head_size = width // heads
    state = w_ref.shape[1]
    count = tokens // SUB
    steps = width // WIDE

    small = [
        pltpu.make_async_copy(source, target, sems.at[2 * steps + n])
        for n, (source, target) in enumerate(((ld_hbm, ld_ref), (w_hbm, w_ref), (r_hbm, r_ref)))
    ]
    for copy in small:
        copy.start()

    def load(source, target, step, sem):
        columns = pl.ds(pl.multiple_of(step * WIDE, WIDE), WIDE)
        return pltpu.make_async_copy(source.at[:, columns], target.at[step], sems.at[sem])

    for step in range(steps):
        load(x_hbm, xb, step, step).start()
        load(g_hbm, gb, step, steps + step).start()
    for copy in small:
        copy.wait()

    decays = jnp.concatenate([ld_ref[...]] * (LANES // heads), axis=0)
    sums = running_sums(decays)
    rows = lax.broadcasted_iota(jnp.int32, (SUB, SUB), 0)
    columns = lax.broadcasted_iota(jnp.int32, (SUB, SUB), 1)
    before = jnp.zeros((1, LANES), F32)
    upto = []
    middles = []
    afters = []
    for k in range(count):
        tok = slice(k * SUB, (k + 1) * SUB)
        middle, end = sums[k][MIDDLE : MIDDLE + 1], sums[k][SUB - 1 :]
        fa[tok] = two_terms(jnp.exp(middle - sums[k]), heads)
        fb[tok] = two_terms(jnp.exp(sums[k] - middle), heads)
        upto.append(before + middle)
        before = before + end
        middles.append(middle)
        afters.append(end - middle)
        write, read = w_ref[tok], r_ref[tok]
        pairs = jnp.where(columns >= rows, dot(write, read, ((1,), (1,))), 0.0).astype(BF16)
        pw[k] = jnp.concatenate([pairs, write], axis=1)
        wt[k] = write.T
        rt[k] = read.T
    into = [middles[0]] + [middles[k] + afters[k - 1] for k in range(1, count)]
    back = [afters[k] + middles[k + 1] for k in range(count - 1)] + [afters[count - 1]]
    between[...] = two_terms(jnp.exp(jnp.concatenate(into + back, axis=0)), heads)
    to_end = [before - part for part in upto]
    whole = [before] * 16
    ends[...] = two_terms(jnp.exp(jnp.concatenate(to_end + upto + whole, axis=0)), heads)

    @pl.loop(0, steps)
    def _(step):
        load(x_hbm, xb, step, step).wait()
        load(g_hbm, gb, step, steps + step).wait()
        lanes = pl.ds(pl.multiple_of(step * WIDE, WIDE), WIDE)
        spread = spread_matrix(heads, head_size, WIDE, step)
        factor = dot(ends[...], spread)
        written = jnp.zeros((state, WIDE), F32)
        collected = jnp.zeros((state, WIDE), F32)
        xs_ref[:, lanes] = (xb[step].astype(F32) * dot(fa[...], spread)).astype(BF16)
        gs_ref[:, lanes] = (gb[step].astype(F32) * dot(fb[...], spread)).astype(BF16)
        for k in range(count):
            tok = slice(k * SUB, (k + 1) * SUB)
            written += factor[k : k + 1] * dot(wt[k], xs_ref[tok, lanes])
            collected += factor[count + k : count + k + 1] * dot(rt[k], gs_ref[tok, lanes])
        for pair in range(WIDE // LANES):
            part = slice(pair * LANES, (pair + 1) * LANES)
            to = step * (WIDE // LANES) + pair
            out_ref[to, :state] = written[:, part]
            out_ref[to, state : 2 * state] = collected[:, part]
            out_ref[to, 2 * state :] = factor[2 * count : 2 * count + 8, part]


def scan_kernel(in_ref, out_ref):
    shards = in_ref.shape[0]
    state = out_ref.shape[1] // 2
    carried = jnp.zeros((state, LANES), F32)
    for shard in range(shards):
        out_ref[shard, :state] = carried
        carried = in_ref[shard, 2 * state : 2 * state + 1] * carried + in_ref[shard, :state]
    carried = jnp.zeros((state, LANES), F32)
    for shard in reversed(range(shards)):
        out_ref[shard, state:] = carried
        carried = in_ref[shard, 2 * state : 2 * state + 1] * carried + in_ref[shard, state : 2 * state]


def grads_kernel(
    xs_ref, gs_ref, st_ref, r_ref, fa, between, pw, wt, rt, gi_hbm, out_ref, acc, wrote, took, into_s, back_s, gi, sems, *, heads
):
    width = xs_ref.shape[1]
    head_size = width // heads
    count, state, _ = wt.shape
    steps = width // WIDE2
    acc[...] = jnp.zeros_like(acc)

    def store(step):
        lanes = pl.ds(pl.multiple_of(step * WIDE2, WIDE2), WIDE2)
        return pltpu.make_async_copy(gi.at[step], gi_hbm.at[:, lanes], sems.at[step])

    @pl.loop(0, steps)
    def _(step):
        lanes = pl.ds(pl.multiple_of(step * WIDE2, WIDE2), WIDE2)
        first = step * (WIDE2 // LANES)
        spread = spread_matrix(heads, head_size, WIDE2, step)
        factor = dot(between[...], spread)
        for k in range(count):
            tok = slice(k * SUB, (k + 1) * SUB)
            took[k] = dot(rt[k], gs_ref[tok, lanes])
            wrote[k] = dot(wt[k], xs_ref[tok, lanes])

        entering = jnp.concatenate([st_ref[first + p, :state] for p in range(WIDE2 // LANES)], axis=1)
        leaving = jnp.concatenate([st_ref[first + p, state:] for p in range(WIDE2 // LANES)], axis=1)
        back = factor[2 * count - 1 : 2 * count] * leaving
        for k in reversed(range(count)):
            back_s[k] = back.astype(BF16)
            if k:
                back = factor[count + k - 1 : count + k] * (back + took[k])
        into = factor[:1] * entering
        for k in range(count):
            into_s[k] = into.astype(BF16)
            if k + 1 < count:
                into = factor[k + 1 : k + 2] * (into + wrote[k])

        for k in range(count):
            tok = slice(k * SUB, (k + 1) * SUB)
            right = jnp.concatenate([gs_ref[tok, lanes], back_s[k]], axis=0)
            left = jnp.concatenate([xs_ref[tok, lanes], into_s[k]], axis=0)
            gi[step, tok] = (dot(fa[tok], spread) * dot(pw[k], right)).astype(BF16)
            acc[k] += dot(left, right, ((1,), (1,)))
        store(step).start()

    rows = lax.broadcasted_iota(jnp.int32, (SUB, SUB), 0)
    columns = lax.broadcasted_iota(jnp.int32, (SUB, SUB), 1)
    for k in range(count):
        tok = slice(k * SUB, (k + 1) * SUB)
        weights = jnp.where(columns >= rows, acc[k, :SUB, :SUB], 0.0).astype(BF16)
        out_ref[k, :, :state] = dot(weights, r_ref[tok]) + acc[k, :SUB, SUB:]
        out_ref[k, :, state:] = (dot(wt[k], weights) + acc[k, SUB:, :SUB]).T
    for step in range(steps):
        store(step).wait()


PARAMS = pltpu.CompilerParams(vmem_limit_bytes=32 * 2**20)
HERE = pl.BlockSpec(memory_space=pltpu.VMEM)
THERE = pl.BlockSpec(memory_space=pltpu.HBM)


def summarise(x, g, w, r, ld):
    tokens, width = x.shape
    state = w.shape[1]
    count = tokens // SUB
    steps = width // WIDE
    return pl.pallas_call(
        summary_kernel,
        in_specs=[THERE] * 5,
        out_specs=[HERE] * 8,
        out_shape=[
            jax.ShapeDtypeStruct((width // LANES, 2 * state + 8, LANES), F32),
            jax.ShapeDtypeStruct((tokens, width), BF16),
            jax.ShapeDtypeStruct((tokens, width), BF16),
            jax.ShapeDtypeStruct((tokens, LANES), BF16),
            jax.ShapeDtypeStruct((2 * count, LANES), BF16),
            jax.ShapeDtypeStruct((count, SUB, SUB + state), BF16),
            jax.ShapeDtypeStruct((count, state, SUB), BF16),
            jax.ShapeDtypeStruct((count, state, SUB), BF16),
        ],
        scratch_shapes=[
            pltpu.VMEM((tokens, LANES), BF16),
            pltpu.VMEM((2 * count + 16, LANES), BF16),
            pltpu.VMEM((steps, tokens, WIDE), BF16),
            pltpu.VMEM((steps, tokens, WIDE), BF16),
            pltpu.VMEM((tokens, state), BF16),
            pltpu.VMEM((tokens, state), BF16),
            pltpu.VMEM(ld.shape, F32),
            pltpu.SemaphoreType.DMA((2 * steps + 3,)),
        ],
        compiler_params=pltpu.CompilerParams(vmem_limit_bytes=50 * 2**20),
        name="summary",
    )(x, g, w, r, ld)


def scan_shards(every):
    return pl.pallas_call(
        scan_kernel,
        in_specs=[HERE],
        out_specs=HERE,
        out_shape=jax.ShapeDtypeStruct((every.shape[0], every.shape[1] - 8, LANES), F32),
        compiler_params=PARAMS,
        name="scan",
    )(every)


def gradients(scaled_x, scaled_g, own, r, kept, heads):
    tokens, width = scaled_x.shape
    state = r.shape[1]
    count = tokens // SUB
    steps = width // WIDE2

    def kernel(*refs):
        grads_kernel(*refs, heads=heads)

    return pl.pallas_call(
        kernel,
        in_specs=[HERE] * (4 + len(kept)),
        out_specs=[THERE, HERE],
        out_shape=[
            jax.ShapeDtypeStruct((tokens, width), BF16),
            jax.ShapeDtypeStruct((count, SUB, 2 * state), F32),
        ],
        scratch_shapes=[
            pltpu.VMEM((count, SUB + state, SUB + state), F32),
            pltpu.VMEM((count, state, WIDE2), F32),
            pltpu.VMEM((count, state, WIDE2), F32),
            pltpu.VMEM((count, state, WIDE2), BF16),
            pltpu.VMEM((count, state, WIDE2), BF16),
            pltpu.VMEM((steps, tokens, WIDE2), BF16),
            pltpu.SemaphoreType.DMA((steps,)),
        ],
        compiler_params=pltpu.CompilerParams(vmem_limit_bytes=36 * 2**20),
        name="grads",
    )(scaled_x, scaled_g, own, r, *kept)


def body(scaled_input, out_grad, write_proj, read_proj, log_decay):
    heads = log_decay.shape[0]
    state = write_proj.shape[1]
    summary, scaled_x, scaled_g, *kept = summarise(scaled_input, out_grad, write_proj, read_proj, log_decay)
    every = lax.all_to_all(summary, "seq", 0, 0, tiled=True)
    own = lax.all_to_all(scan_shards(every), "seq", 0, 0, tiled=True)
    grad_input, parts = gradients(scaled_x, scaled_g, own, read_proj, kept, heads)
    shared = lax.all_to_all(parts, "head", 0, 0, tiled=True).sum(axis=0)
    return grad_input, shared[:, :state].astype(BF16), shared[:, state:].astype(BF16)


def solution(mesh):
    return jax.shard_map(
        body,
        mesh=mesh,
        in_specs=(
            P("seq", "head"),
            P("seq", "head"),
            P("seq", None),
            P("seq", None),
            P("head", "seq"),
        ),
        out_specs=(P("seq", "head"), P(("seq", "head"), None), P(("seq", "head"), None)),
        check_vma=False,
    )
```

time: 127 us -> 114 us (0.90)
  Pallas kernels: 32.9 us -> 20.2 us
    pallas_call x3, Pallas kernels: 32.9 us -> 20.2 us  [the longest x1 10.9 us: summarise(): pl.pallas_call(summary_kernel, in_specs=[THERE] * 5, out_specs=[HERE] * 8...]
    unnamed x12 -> x10, local copies, waits for them, and re-layouts: 2.82 us -> 2.8 us
where the time goes in v2:
time: 114 us
  blocking collectives  89.3 us (78%)
  Pallas kernels  20.2 us (18%)
  local copies, waits for them, and re-layouts  3.43 us (3%)
    all_to_all x1, blocking collectives, body(): every = lax.all_to_all(summary, 'seq', 0, 0, tiled=True)  36.6 us
    all_to_all x1, blocking collectives, body(): own = lax.all_to_all(scan_shards(every), 'seq', 0, 0, tiled=True)  30.4 us
    all_to_all x1, blocking collectives, body(): shared = lax.all_to_all(parts, 'head', 0, 0, tiled=True).sum(axis=0)  22.4 us
    pallas_call x1, Pallas kernels, summarise(): pl.pallas_call(summary_kernel, in_specs=[THERE] * 5, out_specs=[HERE] * 8...  10.9 us
    pallas_call x1, Pallas kernels, gradients(): pl.pallas_call(kernel, in_specs=[HERE] * (4 + len(kept)), out_specs=[THER...  9.2 us
    unnamed x10, local copies, waits for them, and re-layouts  2.8 us

profile of v2, /device:TPU:1, one launch (start us, length us, event | category | flops | bytes accessed | tf_op | source)
XLA Modules:
  0.0 113.8 jit_solution(3292433110198909620)
XLA Ops:
  0.6 0.0 copy-start.2
  0.6 0.9 copy-done.2
  1.6 0.0 copy-start.3
  1.6 0.9 copy-done.3
  2.5 0.0 copy-start.4
  2.5 0.9 copy-done.4
  3.4 10.9 %summary.1 = (f32[16,264,128]{2,1,0:T(8,128)}, bf16[1024,2048]{1,0:T(8,128)(2,1)}, bf16[1024,2048]{1,0:T(8,128)(2,1)}, bf16[1024,128]{1,0:T(8,128)(2,1)S(1)}, bf...) custom-call(bf16[1024,2048]{1,0:T(8,128)(2,1)} %x_hbm.1, ...), custom_call_target="tpu_custom_call" | custom-call | tf_op jit(solution)/shard_map/summary/pallas_call | solution.py:209
  14.3 36.6 %all_to_all.15.in_ref = f32[16,264,128]{2,1,0:T(8,128)S(1)} all-to-all(f32[16,264,128]{2,1,0:T(8,128)} %get-tuple-element.15), channel_id=1, replica_groups=mesh['seq'=16,'head'=8] {'seq'}, dimensions={0} | all-to-all | bytes 4325376 | tf_op jit(solution)/shard_map/all_to_all | solution.py:284
  50.9 0.0 copy-start
  50.9 0.0 copy-start.1
  50.9 0.2 scan.1
  51.1 30.4 %all_to_all.16.refs_2_ = f32[16,256,128]{2,1,0:T(8,128)S(1)} all-to-all(f32[16,256,128]{2,1,0:T(8,128)S(1)} %scan.1), channel_id=1, replica_groups=mesh['seq'=16,'head'=8] {'seq'}, dimensions={0} | all-to-all | bytes 4194304 | tf_op jit(solution)/shard_map/all_to_all | solution.py:285
  81.5 0.0 copy-done
  81.5 0.0 copy-done.1
  81.5 9.2 %grads.1 = (bf16[1024,2048]{1,0:T(8,128)(2,1)}, f32[8,128,256]{2,1,0:T(8,128)S(1)}) custom-call(bf16[1024,2048]{1,0:T(8,128)(2,1)S(1)} %copy-done, bf16[1024,2048]{1,0:T(8,128)(2,1)S(1)} %copy-done.1, f32[16,256,128]{2,1,0:T(8,128)S(1)} %all_to_all.16.refs_2_, bf16[1024,128]{1,0:T(8,128)(2,1)S(1)} %copy-done.2, ...), custom_call_target="tpu_custom_call" | custom-call | tf_op jit(solution)/shard_map/grads/pallas_call | solution.py:258
  90.7 22.4 %all_to_all.17 = f32[8,128,256]{2,1,0:T(8,128)S(1)} all-to-all(f32[8,128,256]{2,1,0:T(8,128)S(1)} %get-tuple-element.22), channel_id=1, replica_groups=mesh['seq'=16,'head'=8] {'head'}, dimensions={0} | all-to-all | bytes 2097152 | tf_op jit(solution)/shard_map/all_to_all | solution.py:287
  113.0 0.1 reduce_sum.9
  113.1 0.6 fusion
Async XLA Ops:
  0.6 1.0 copy-start.2
  1.6 0.9 copy-start.3
  2.5 0.9 copy-start.4
  50.9 30.6 %copy-start = (bf16[1024,2048]{1,0:T(8,128)(2,1)S(1)}, bf16[1024,2048]{1,0:T(8,128)(2,1)}, u32[]{:S(2)}) copy-start(bf16[1024,2048]{1,0:T(8,128)(2,1)} %get-tuple-element.13.refs_0_) | copy-start | bytes 12582916
  50.9 30.6 %copy-start.1 = (bf16[1024,2048]{1,0:T(8,128)(2,1)S(1)}, bf16[1024,2048]{1,0:T(8,128)(2,1)}, u32[]{:S(2)}) copy-start(bf16[1024,2048]{1,0:T(8,128)(2,1)} %get-tuple-element.14.refs_1_) | copy-start | bytes 12582916

commit v3 on v1

v3 whole, which is shorter than its diff:
```python
import jax
import jax.numpy as jnp
from jax import lax
from jax.experimental import pallas as pl
from jax.experimental.pallas import tpu as pltpu
from jax.sharding import PartitionSpec as P

SUB = 128
LANES = 128
WIDE = 512
MIDDLE = SUB // 2 - 1
F32 = jnp.float32
BF16 = jnp.bfloat16


def dot(a, b, dims=((1,), (0,))):
    return lax.dot_general(a, b, (dims, ((), ())), preferred_element_type=F32)


def running_sums(decays):
    rows = lax.broadcasted_iota(jnp.int32, (SUB, SUB), 0)
    columns = lax.broadcasted_iota(jnp.int32, (SUB, SUB), 1)
    lower = jnp.where(rows >= columns, 1.0, 0.0).astype(BF16)
    first = decays.astype(BF16)
    left = decays - first.astype(F32)
    second = left.astype(BF16)
    third = (left - second.astype(F32)).astype(BF16)
    sums = []
    for start in range(0, decays.shape[1], SUB):
        tok = slice(start, start + SUB)
        a, b, c = (dot(lower, term[:, tok], ((1,), (1,))) for term in (first, second, third))
        sums.append(a + (b + c))
    return sums


def two_terms(values, heads):
    lane = lax.broadcasted_iota(jnp.int32, values.shape, 1)
    high = values.astype(BF16).astype(F32)
    kept = jnp.where(lane < heads, high, jnp.where(lane < 2 * heads, values - high, 0.0))
    return kept.astype(BF16)


def spread_matrix(heads, head_size, wide, step):
    row = lax.broadcasted_iota(jnp.int32, (LANES, wide), 0)
    column = lax.broadcasted_iota(jnp.int32, (LANES, wide), 1)
    same = lax.rem(row, heads) == (step * wide + column) // head_size
    return jnp.where(same, 1.0, 0.0).astype(BF16)


def summary_kernel(x_ref, g_ref, w_ref, r_ref, ld_ref, out_ref, x1_ref, g1_ref, fx, fg, ends, wt, rt):
    heads, tokens = ld_ref.shape
    wide = x_ref.shape[1]
    head_size = wide * pl.num_programs(0) // heads
    state = w_ref.shape[1]
    step = pl.program_id(0)

    @pl.when(step == 0)
    def _():
        sums = running_sums(jnp.concatenate([ld_ref[...]] * (LANES // heads), axis=0))
        before = jnp.zeros((1, LANES), F32)
        for k in range(len(sums)):
            sums[k] = sums[k] + before
            before = sums[k][SUB - 1 :]
        for k in range(len(sums)):
            tok = slice(k * SUB, (k + 1) * SUB)
            fx[tok] = two_terms(jnp.exp(before - sums[k]), heads)
            fg[tok] = two_terms(jnp.exp(sums[k]), heads)
            wt[:, tok] = w_ref[tok].T
            rt[:, tok] = r_ref[tok].T
        ends[...] = two_terms(jnp.exp(jnp.broadcast_to(before, ends.shape)), heads)

    spread = spread_matrix(heads, head_size, wide, step)
    x1_ref[...] = (x_ref[...].astype(F32) * dot(fx[...], spread)).astype(BF16)
    g1_ref[...] = (g_ref[...].astype(F32) * dot(fg[...], spread)).astype(BF16)
    written = dot(wt[...], x1_ref[...])
    collected = dot(rt[...], g1_ref[...])
    decay = dot(ends[...], spread)[:8]
    for pair in range(wide // LANES):
        lanes = slice(pair * LANES, (pair + 1) * LANES)
        out_ref[pair, :state] = written[:, lanes]
        out_ref[pair, state : 2 * state] = collected[:, lanes]
        out_ref[pair, 2 * state :] = decay[:, lanes]


def scan_kernel(in_ref, out_ref):
    shards = in_ref.shape[0]
    state = out_ref.shape[1] // 2
    carried = jnp.zeros((state, LANES), F32)
    for shard in range(shards):
        out_ref[shard, :state] = carried
        carried = in_ref[shard, 2 * state : 2 * state + 1] * carried + in_ref[shard, :state]
    carried = jnp.zeros((state, LANES), F32)
    for shard in reversed(range(shards)):
        out_ref[shard, state:] = carried
        carried = in_ref[shard, 2 * state : 2 * state + 1] * carried + in_ref[shard, state : 2 * state]


def local_kernel(
    x_ref, g_ref, w_ref, r_ref, ld_ref, gi_ref, out_ref, fa, fb, between, pw, wt, rt, xs, gs, acc, wrote, took, into_s, back_s
):
    heads, tokens = ld_ref.shape
    wide = x_ref.shape[1]
    head_size = wide * pl.num_programs(0) // heads
    count, state, _ = wt.shape
    step = pl.program_id(0)
    rows = lax.broadcasted_iota(jnp.int32, (SUB, SUB), 0)
    columns = lax.broadcasted_iota(jnp.int32, (SUB, SUB), 1)
    upper = columns >= rows

    @pl.when(step == 0)
    def _():
        sums = running_sums(jnp.concatenate([ld_ref[...]] * (LANES // heads), axis=0))
        middles = []
        afters = []
        for k in range(count):
            tok = slice(k * SUB, (k + 1) * SUB)
            middle = sums[k][MIDDLE : MIDDLE + 1]
            fa[tok] = two_terms(jnp.exp(middle - sums[k]), heads)
            fb[tok] = two_terms(jnp.exp(sums[k] - middle), heads)
            middles.append(middle)
            afters.append(sums[k][SUB - 1 :] - middle)
            write, read = w_ref[tok], r_ref[tok]
            pairs = jnp.where(upper, dot(write, read, ((1,), (1,))), 0.0).astype(BF16)
            pw[k] = jnp.concatenate([pairs, write], axis=1)
            wt[k] = write.T
            rt[k] = read.T
        into = [middles[0]] + [middles[k] + afters[k - 1] for k in range(1, count)]
        back = [afters[k] + middles[k + 1] for k in range(count - 1)] + [afters[count - 1]]
        between[...] = two_terms(jnp.exp(jnp.concatenate(into + back, axis=0)), heads)
        acc[...] = jnp.zeros_like(acc)

    spread = spread_matrix(heads, head_size, wide, step)
    factor = dot(between[...], spread)
    xs[...] = (x_ref[...].astype(F32) * dot(fa[...], spread)).astype(BF16)
    gs[...] = (g_ref[...].astype(F32) * dot(fb[...], spread)).astype(BF16)
    for k in range(count):
        tok = slice(k * SUB, (k + 1) * SUB)
        took[k] = dot(rt[k], gs[tok])
        wrote[k] = dot(wt[k], xs[tok])

    back = jnp.zeros((state, wide), F32)
    for k in reversed(range(count)):
        back_s[k] = back.astype(BF16)
        if k:
            back = factor[count + k - 1 : count + k] * (back + took[k])
    into = jnp.zeros((state, wide), F32)
    for k in range(count):
        into_s[k] = into.astype(BF16)
        if k + 1 < count:
            into = factor[k + 1 : k + 2] * (into + wrote[k])

    for k in range(count):
        tok = slice(k * SUB, (k + 1) * SUB)
        right = jnp.concatenate([gs[tok], back_s[k]], axis=0)
        left = jnp.concatenate([xs[tok], into_s[k]], axis=0)
        gi_ref[tok] = dot(fa[tok], spread) * dot(pw[k], right)
        acc[k] += dot(left, right, ((1,), (1,)))

    @pl.when(step == pl.num_programs(0) - 1)
    def _():
        for k in range(count):
            tok = slice(k * SUB, (k + 1) * SUB)
            weights = jnp.where(upper, acc[k, :SUB, :SUB], 0.0).astype(BF16)
            out_ref[k, :, :state] = dot(weights, r_ref[tok]) + acc[k, :SUB, SUB:]
            out_ref[k, :, state:] = (dot(wt[k], weights) + acc[k, SUB:, :SUB]).T


def meet_kernel(core_ref, x1_ref, g1_ref, st_ref, part_ref, mine_ref, other_ref, states):
    state = st_ref.shape[1] // 2
    core = core_ref[0]
    for p in range(st_ref.shape[0]):
        states[:, p * LANES : (p + 1) * LANES] = st_ref[p].astype(BF16)
    for out_ref, which in ((other_ref, 1 - core), (mine_ref, core)):
        for chip in range(out_ref.shape[0]):
            k = 2 * chip + which
            tok = pl.ds(pl.multiple_of(k * SUB, SUB), SUB)
            out_ref[chip, :, :state] = part_ref[k, :, :state] + dot(x1_ref[tok], states[state:], ((1,), (1,)))
            out_ref[chip, :, state:] = part_ref[k, :, state:] + dot(g1_ref[tok], states[:state], ((1,), (1,)))


def finish_kernel(gi_ref, st_ref, w_ref, fx, out_ref, *, heads):
    wide = gi_ref.shape[1]
    head_size = wide * pl.num_programs(0) // heads
    state = w_ref.shape[1]
    spread = spread_matrix(heads, head_size, wide, pl.program_id(0))
    leaving = jnp.concatenate([st_ref[p, state:].astype(BF16) for p in range(wide // LANES)], axis=1)
    for start in range(0, w_ref.shape[0], WIDE):
        tok = slice(start, start + WIDE)
        out_ref[tok] = (gi_ref[tok] + dot(fx[tok], spread) * dot(w_ref[tok], leaving)).astype(BF16)


def params(mib):
    return pltpu.CompilerParams(vmem_limit_bytes=mib * 2**20)


HERE = pl.BlockSpec(memory_space=pltpu.VMEM)


def fixed(*shape):
    return pl.BlockSpec(shape, lambda i: (0,) * len(shape))


def summarise(x, g, w, r, ld):
    tokens, width = x.shape
    state = w.shape[1]
    pairs = WIDE // LANES
    wide = pl.BlockSpec((tokens, WIDE), lambda i: (0, i))
    return pl.pallas_call(
        summary_kernel,
        grid=(width // WIDE,),
        in_specs=[wide, wide, fixed(tokens, state), fixed(tokens, state), fixed(*ld.shape)],
        out_specs=[
            pl.BlockSpec((pairs, 2 * state + 8, LANES), lambda i: (i, 0, 0)),
            wide,
            wide,
            fixed(tokens, LANES),
        ],
        out_shape=[
            jax.ShapeDtypeStruct((width // LANES, 2 * state + 8, LANES), F32),
            jax.ShapeDtypeStruct((tokens, width), BF16),
            jax.ShapeDtypeStruct((tokens, width), BF16),
            jax.ShapeDtypeStruct((tokens, LANES), BF16),
        ],
        scratch_shapes=[
            pltpu.VMEM((tokens, LANES), BF16),
            pltpu.VMEM((16, LANES), BF16),
            pltpu.VMEM((state, tokens), BF16),
            pltpu.VMEM((state, tokens), BF16),
        ],
        compiler_params=params(60),
        name="summary",
    )(x, g, w, r, ld)


def scan_shards(every):
    return pl.pallas_call(
        scan_kernel,
        in_specs=[HERE],
        out_specs=HERE,
        out_shape=jax.ShapeDtypeStruct((every.shape[0], every.shape[1] - 8, LANES), F32),
        compiler_params=params(16),
        name="scan",
    )(every)


def local_gradients(x, g, w, r, ld):
    tokens, width = x.shape
    state = w.shape[1]
    count = tokens // SUB
    wide = pl.BlockSpec((tokens, WIDE), lambda i: (0, i))
    return pl.pallas_call(
        local_kernel,
        grid=(width // WIDE,),
        in_specs=[wide, wide, fixed(tokens, state), fixed(tokens, state), fixed(*ld.shape)],
        out_specs=[wide, fixed(count, SUB, 2 * state)],
        out_shape=[
            jax.ShapeDtypeStruct((tokens, width), F32),
            jax.ShapeDtypeStruct((count, SUB, 2 * state), F32),
        ],
        scratch_shapes=[
            pltpu.VMEM((tokens, LANES), BF16),
            pltpu.VMEM((tokens, LANES), BF16),
            pltpu.VMEM((2 * count, LANES), BF16),
            pltpu.VMEM((count, SUB, SUB + state), BF16),
            pltpu.VMEM((count, state, SUB), BF16),
            pltpu.VMEM((count, state, SUB), BF16),
            pltpu.VMEM((tokens, WIDE), BF16),
            pltpu.VMEM((tokens, WIDE), BF16),
            pltpu.VMEM((count, SUB + state, SUB + state), F32),
            pltpu.VMEM((count, state, WIDE), F32),
            pltpu.VMEM((count, state, WIDE), F32),
            pltpu.VMEM((count, state, WIDE), BF16),
            pltpu.VMEM((count, state, WIDE), BF16),
        ],
        compiler_params=params(36),
        cost_estimate=pl.CostEstimate(flops=8 * 10**9, bytes_accessed=17 * 10**6, transcendentals=0),
        name="local",
    )(x, g, w, r, ld)


def meet(core, x1, g1, own, parts):
    tokens, width = x1.shape
    count, _, both = parts.shape
    half = jax.ShapeDtypeStruct((count // 2, SUB, both), F32)
    return pl.pallas_call(
        meet_kernel,
        in_specs=[pl.BlockSpec(memory_space=pltpu.SMEM)] + [HERE] * 4,
        out_specs=[HERE, HERE],
        out_shape=[half, half],
        scratch_shapes=[pltpu.VMEM((both, width), BF16)],
        compiler_params=params(16),
        name="meet",
    )(core, x1, g1, own, parts)


def finish(gi, own, w, fx, heads):
    tokens, width = gi.shape
    state = w.shape[1]
    pairs = WIDE // LANES
    wide = pl.BlockSpec((tokens, WIDE), lambda i: (0, i))

    def kernel(*refs):
        finish_kernel(*refs, heads=heads)

    return pl.pallas_call(
        kernel,
        grid=(width // WIDE,),
        in_specs=[
            wide,
            pl.BlockSpec((pairs, 2 * state, LANES), lambda i: (i, 0, 0)),
            fixed(tokens, state),
            fixed(tokens, LANES),
        ],
        out_specs=wide,
        out_shape=jax.ShapeDtypeStruct((tokens, width), BF16),
        compiler_params=params(24),
        cost_estimate=pl.CostEstimate(flops=2 * 10**9, bytes_accessed=13 * 10**6, transcendentals=0),
        name="finish",
    )(gi, own, w, fx)


def body(scaled_input, out_grad, write_proj, read_proj, log_decay):
    heads = log_decay.shape[0]
    state = write_proj.shape[1]
    ranks = lax.axis_size("head")
    rank = lax.axis_index("head")
    summary, x1, g1, fx = summarise(scaled_input, out_grad, write_proj, read_proj, log_decay)
    every = lax.all_to_all(summary, "seq", 0, 0, tiled=True)
    gi, parts = local_gradients(scaled_input, out_grad, write_proj, read_proj, log_decay)
    own = lax.all_to_all(scan_shards(every), "seq", 0, 0, tiled=True)
    mine, other = meet((rank % 2).astype(jnp.int32).reshape(1), x1, g1, own, parts)
    chip = mine + lax.ppermute(other, "head", [(i, i ^ 1) for i in range(ranks)])
    groups = [list(range(core, ranks, 2)) for core in range(2)]
    shared = lax.all_to_all(chip, "head", 0, 0, axis_index_groups=groups, tiled=True).sum(axis=0)
    grad_input = finish(gi, own, write_proj, fx, heads)
    return grad_input, shared[:, :state].astype(BF16), shared[:, state:].astype(BF16)


def solution(mesh):
    return jax.shard_map(
        body,
        mesh=mesh,
        in_specs=(
            P("seq", "head"),
            P("seq", "head"),
            P("seq", None),
            P("seq", None),
            P("head", "seq"),
        ),
        out_specs=(P("seq", "head"), P(("seq", "head"), None), P(("seq", "head"), None)),
        check_vma=False,
    )
```

time: 127 us -> 107 us (0.84)
  blocking collectives: 89 us -> 36.5 us
  local copies, waits for them, and re-layouts: 3.45 us -> 19.2 us
  starting transfers between devices: 0 us -> 12.2 us
  waiting for transfers between devices: 0 us -> 7.41 us
  Pallas kernels: 32.9 us -> 29.4 us
    all_to_all x2 -> x0, blocking collectives: 52.6 us -> none  [the longest x1 30.1 us: body(): own = lax.all_to_all(states, 'seq', 0, 0, tiled=True)]
    unnamed x12 -> x22, local copies, waits for them, and re-layouts: 2.82 us -> 18.6 us
    all_to_all x0 -> x2, starting transfers between devices: none -> 7.9 us  [the longest x1 4.19 us: body(): lax.all_to_all(chip, 'head', 0, 0, axis_index_groups=groups, tiled=True)]
    all_to_all x0 -> x2, waiting for transfers between devices: none -> 5.87 us  [the longest x1 5.8 us: body(): own = lax.all_to_all(scan_shards(every), 'seq', 0, 0, tiled=True)]
    ppermute x0 -> x1, starting transfers between devices: none -> 4.31 us  [body(): lax.ppermute(other, 'head', [(i, i ^ 1) for i in range(ranks)])]
    pallas_call x3 -> x5, Pallas kernels: 32.9 us -> 29.4 us  [the longest x1 12.9 us: local_gradients(): pl.pallas_call(local_kernel, grid=(width // WIDE,), in_specs=[wide, wide,...]
    ppermute x0 -> x1, waiting for transfers between devices: none -> 1.54 us  [body(): lax.ppermute(other, 'head', [(i, i ^ 1) for i in range(ranks)])]
  transfers between devices with their start and end apart: 0 -> 3, of which waited for: 0 -> 3; matrix products, arithmetic and copies ran while one was open for 0% -> 0% of each run, Pallas kernels for 0% -> 16%
where the time goes in v3:
time: 107 us; the launch traced here: 106 us
  blocking collectives  36.5 us (34%)
  Pallas kernels  29.4 us (27%)
  local copies, waits for them, and re-layouts  19.2 us (18%)
  starting transfers between devices  12.2 us (11%)
  waiting for transfers between devices  7.41 us (7%)
    all_to_all x1, blocking collectives, body(): every = lax.all_to_all(summary, 'seq', 0, 0, tiled=True)  36.5 us
    unnamed x22, local copies, waits for them, and re-layouts  18.6 us
    pallas_call x1, Pallas kernels, local_gradients(): pl.pallas_call(local_kernel, grid=(width // WIDE,), in_specs=[wide, wide,...  12.9 us
    pallas_call x1, Pallas kernels, summarise(): pl.pallas_call(summary_kernel, grid=(width // WIDE,), in_specs=[wide, wid...  9.5 us
    all_to_all x1, waiting for transfers between devices, body(): own = lax.all_to_all(scan_shards(every), 'seq', 0, 0, tiled=True)  5.8 us
    pallas_call x1, Pallas kernels, finish(): pl.pallas_call(kernel, grid=(width // WIDE,), in_specs=[wide, pl.BlockSpe...  4.51 us
    ppermute x1, starting transfers between devices, body(): lax.ppermute(other, 'head', [(i, i ^ 1) for i in range(ranks)])  4.31 us
    all_to_all x1, starting transfers between devices, body(): lax.all_to_all(chip, 'head', 0, 0, axis_index_groups=groups, tiled=True)  4.19 us
  transfers between devices with their start and end apart: 3, of which 3 were waited for; matrix products, arithmetic and copies ran while one was open for 0% of the time, Pallas kernels for 16%

profile of v3, /device:TPU:1, one launch (start us, length us, event | category | flops | bytes accessed | tf_op | source)
XLA Modules:
  0.0 106.5 jit_solution(18132118985042459250)
XLA Ops:
  0.6 9.5 %summary.1 = (f32[16,264,128]{2,1,0:T(8,128)}, bf16[1024,2048]{1,0:T(8,128)(2,1)}, bf16[1024,2048]{1,0:T(8,128)(2,1)}, bf16[1024,128]{1,0:T(8,128)(2,1)}) custom-call(bf16[1024,2048]{1,0:T(8,128)(2,1)} %x_ref.3, bf16[1024,2048]{1,0:T(8,128)(2,1)} %g_ref.3, bf16[1024,128]{1,0:T(8,128)(2,1)} %refs_2_.1, bf16[1024,128]{1,0:T(8,128)(2,1)} %r_ref.3, ...), custom_call_target="tpu_custom_call" | custom-call | tf_op jit(solution)/shard_map/summary/pallas_call | solution.py:208
  10.1 36.5 %all_to_all.15.in_ref = f32[16,264,128]{2,1,0:T(8,128)S(1)} all-to-all(f32[16,264,128]{2,1,0:T(8,128)} %get-tuple-element.12), channel_id=1, replica_groups=mesh['seq'=16,'head'=8] {'seq'}, dimensions={0} | all-to-all | bytes 4325376 | tf_op jit(solution)/shard_map/all_to_all | solution.py:328
  46.7 0.0 copy-start.10
  46.7 0.2 scan.1
  46.8 0.0 copy-start.2
  46.9 1.3 %copy-done.2 = f32[16,256,128]{2,1,0:T(8,128)} copy-done((f32[16,256,128]{2,1,0:T(8,128)}, f32[16,256,128]{2,1,0:T(8,128)S(1)}, u32[]{:S(2)}) %copy-start.2) | copy-done | bytes 2097176
  48.2 3.7 %all-to-all-start.1 = ((f32[16,256,128]{2,1,0:T(8,128)}), f32[16,256,128]{2,1,0:T(8,128)S(1)}, u32[]{:S(2)}, u32[]{:S(2)}) async-start(f32[16,256,128]{2,1,0:T(8,128)} %copy-done.2), calls=%async_computation.1 | async-start | bytes 4194304 | tf_op jit(solution)/shard_map/all_to_all | solution.py:330
  51.9 0.0 copy-done.7
  51.9 0.0 copy-done.10
  51.9 0.0 copy-start.3
  52.0 2.2 %copy-done.3 = bf16[1024,2048]{1,0:T(8,128)(2,1)S(1)} copy-done((bf16[1024,2048]{1,0:T(8,128)(2,1)S(1)}, bf16[1024,2048]{1,0:T(8,128)(2,1)}, u32[]{:S(2)}) %copy-start.3) | copy-done | bytes 4194328
  54.1 0.0 copy-start.4
  54.1 2.2 %copy-done.4 = bf16[1024,2048]{1,0:T(8,128)(2,1)S(1)} copy-done((bf16[1024,2048]{1,0:T(8,128)(2,1)S(1)}, bf16[1024,2048]{1,0:T(8,128)(2,1)}, u32[]{:S(2)}) %copy-start.4) | copy-done | bytes 4194328
  56.3 0.0 copy-start.8
  56.3 0.9 copy-done.8
  57.3 12.9 %local.1 = (f32[1024,2048]{1,0:T(8,128)S(1)}, f32[8,128,256]{2,1,0:T(8,128)S(1)}) custom-call(bf16[1024,2048]{1,0:T(8,128)(2,1)S(1)} %copy-done.3, bf16[1024,2048]{1,0:T(8,128)(2,1)S(1)} %copy-done.4, bf16[1024,128]{1,0:T(8,128)(2,1)S(1)} %copy-done.7, bf16[1024,128]{1,0:T(8,128)(2,1)S(1)} %copy-done.8, f32[32,1024]{1,0:T(8,128)S(1)} %copy-done.10), custom_call_target="tpu_custom_call" | custom-call | flops 8000000000 | bytes 17000000 | tf_op jit(solution)/shard_map/local/pallas_call | solution.py:251
  70.2 0.0 copy-start
  70.2 3.2 %copy-done = f32[1024,2048]{1,0:T(8,128)} copy-done((f32[1024,2048]{1,0:T(8,128)}, f32[1024,2048]{1,0:T(8,128)S(1)}, u32[]{:S(2)}) %copy-start) | copy-done | bytes 8388632
  73.4 5.8 %all-to-all-done.1.refs_1_.st_ref = f32[16,256,128]{2,1,0:T(8,128)S(1)} async-done(((f32[16,256,128]{2,1,0:T(8,128)}), f32[16,256,128]{2,1,0:T(8,128)S(1)}, u32[]{:S(2)}, u32[]{:S(2)}) %all-to-all-start.1) | async-done | bytes 2097184 | tf_op jit(solution)/shard_map/all_to_all | solution.py:330
  79.2 0.0 copy-start.5
  79.2 2.2 %copy-done.5 = bf16[1024,2048]{1,0:T(8,128)(2,1)S(1)} copy-done((bf16[1024,2048]{1,0:T(8,128)(2,1)S(1)}, bf16[1024,2048]{1,0:T(8,128)(2,1)}, u32[]{:S(2)}) %copy-start.5) | copy-done | bytes 4194328
  81.4 2.2 %copy-done.6 = bf16[1024,2048]{1,0:T(8,128)(2,1)S(1)} copy-done((bf16[1024,2048]{1,0:T(8,128)(2,1)S(1)}, bf16[1024,2048]{1,0:T(8,128)(2,1)}, u32[]{:S(2)}) %copy-start.6) | copy-done | bytes 4194328
  83.6 2.4 %meet.1 = (f32[4,128,256]{2,1,0:T(8,128)S(1)}, f32[4,128,256]{2,1,0:T(8,128)S(1)}) custom-call(s32[1]{0:T(128)} %bitcast.core_ref, bf16[1024,2048]{1,0:T(8,128)(2,1)S(1)} %copy-done.5, bf16[1024,2048]{1,0:T(8,128)(2,1)S(1)} %copy-done.6, f32[16,256,128]{2,1,0:T(8,128)S(1)} %all-to-all-done.1.refs_1_.st_ref, f32[8,128,256]{2,1,0:T(8,128)S(1)} %get-tuple-element.16.part_ref), custom_call_target="tpu_custom_call" | custom-call | tf_op jit(solution)/shard_map/meet/pallas_call | solution.py:285
  86.0 4.3 %collective-permute-start = (f32[4,128,256]{2,1,0:T(8,128)S(1)}, f32[4,128,256]{2,1,0:T(8,128)S(1)}, u32[]{:S(2)}, u32[]{:S(2)}) collective-permute-start(f32[4,128,256]{2,1,0:T(8,128)S(1)} %get-tuple-element.18), channel_id=1, source_target_pairs={{0,1},{1,0},{2,3},{3,2},{4,5},{5,4},{6,7},{7,6},{8,9},{9,8},{10,11... | collective-permute-start | bytes 1572872 | tf_op jit(solution)/shard_map/ppermute | solution.py:332
  90.3 1.5 %collective-permute-done = f32[4,128,256]{2,1,0:T(8,128)S(1)} collective-permute-done((f32[4,128,256]{2,1,0:T(8,128)S(1)}, f32[4,128,256]{2,1,0:T(8,128)S(1)}, u32[]{:S(2)}, u32[]{:S(2)}) %collective-permute-start) | collective-permute-done | bytes 524320 | tf_op jit(solution)/shard_map/ppermute | solution.py:332
  91.8 0.9 add.8
  92.7 4.2 %all-to-all-start.2 = ((f32[4,128,256]{2,1,0:T(8,128)}), f32[4,128,256]{2,1,0:T(8,128)S(1)}, u32[]{:S(2)}, u32[]{:S(2)}) async-start(f32[4,128,256]{2,1,0:T(8,128)} %add.8), calls=%async_computation.2 | async-start | bytes 1048576 | tf_op jit(solution)/shard_map/all_to_all | solution.py:334
  96.9 3.4 %copy-done.1 = f32[1024,2048]{1,0:T(8,128)S(1)} copy-done((f32[1024,2048]{1,0:T(8,128)S(1)}, f32[1024,2048]{1,0:T(8,128)}, u32[]{:S(2)}) %copy-start.1) | copy-done | bytes 8388632
  100.3 0.9 copy-done.9
  101.3 4.5 %finish.1 = bf16[1024,2048]{1,0:T(8,128)(2,1)} custom-call(f32[1024,2048]{1,0:T(8,128)S(1)} %copy-done.1, f32[16,256,128]{2,1,0:T(8,128)S(1)} %all-to-all-done.1.refs_1_.st_ref, bf16[1024,128]{1,0:T(8,128)(2,1)S(1)} %copy-done.7, bf16[1024,128]{1,0:T(8,128)(2,1)S(1)} %copy-done.9), custom_call_target="tpu_custom_call" | custom-call | flops 2000000000 | bytes 13000000 | tf_op jit(solution)/shard_map/finish/pallas_call | solution.py:305
  105.8 0.1 all-to-all-done.2
  105.9 0.6 fusion
  (5 shorter events, 0.0 us)
Async XLA Ops:
  46.7 5.3 %copy-start.7 = (bf16[1024,128]{1,0:T(8,128)(2,1)S(1)}, bf16[1024,128]{1,0:T(8,128)(2,1)}, u32[]{:S(2)}) copy-start(bf16[1024,128]{1,0:T(8,128)(2,1)} %refs_2_.1) | copy-start | bytes 786436
  46.7 5.3 %copy-start.10 = (f32[32,1024]{1,0:T(8,128)S(1)}, f32[32,1024]{1,0:T(8,128)}, u32[]{:S(2)}) copy-start(f32[32,1024]{1,0:T(8,128)} %ld_ref.3) | copy-start | bytes 393220
  46.8 1.3 %copy-start.2 = (f32[16,256,128]{2,1,0:T(8,128)}, f32[16,256,128]{2,1,0:T(8,128)S(1)}, u32[]{:S(2)}) copy-start(f32[16,256,128]{2,1,0:T(8,128)S(1)} %scan.1) | copy-start | bytes 6291460
  48.2 31.0 %all-to-all-start.1 = ((f32[16,256,128]{2,1,0:T(8,128)}), f32[16,256,128]{2,1,0:T(8,128)S(1)}, u32[]{:S(2)}, u32[]{:S(2)}) async-start(f32[16,256,128]{2,1,0:T(8,128)} %copy-done.2), calls=%async_computation.1 | async-start | bytes 4194304 | tf_op jit(solution)/shard_map/all_to_all | solution.py:330
  51.9 2.2 %copy-start.3 = (bf16[1024,2048]{1,0:T(8,128)(2,1)S(1)}, bf16[1024,2048]{1,0:T(8,128)(2,1)}, u32[]{:S(2)}) copy-start(bf16[1024,2048]{1,0:T(8,128)(2,1)} %x_ref.3) | copy-start | bytes 12582916
  54.1 2.2 %copy-start.4 = (bf16[1024,2048]{1,0:T(8,128)(2,1)S(1)}, bf16[1024,2048]{1,0:T(8,128)(2,1)}, u32[]{:S(2)}) copy-start(bf16[1024,2048]{1,0:T(8,128)(2,1)} %g_ref.3) | copy-start | bytes 12582916
  56.3 0.9 copy-start.8
  70.2 3.2 %copy-start = (f32[1024,2048]{1,0:T(8,128)}, f32[1024,2048]{1,0:T(8,128)S(1)}, u32[]{:S(2)}) copy-start(f32[1024,2048]{1,0:T(8,128)S(1)} %get-tuple-element.11.refs_0_) | copy-start | bytes 25165828
  79.2 2.2 %copy-start.5 = (bf16[1024,2048]{1,0:T(8,128)(2,1)S(1)}, bf16[1024,2048]{1,0:T(8,128)(2,1)}, u32[]{:S(2)}) copy-start(bf16[1024,2048]{1,0:T(8,128)(2,1)} %get-tuple-element.14.x1_ref) | copy-start | bytes 12582916
  81.4 2.2 %copy-start.6 = (bf16[1024,2048]{1,0:T(8,128)(2,1)S(1)}, bf16[1024,2048]{1,0:T(8,128)(2,1)}, u32[]{:S(2)}) copy-start(bf16[1024,2048]{1,0:T(8,128)(2,1)} %get-tuple-element.15.g1_ref) | copy-start | bytes 12582916
  86.0 5.8 %collective-permute-start = (f32[4,128,256]{2,1,0:T(8,128)S(1)}, f32[4,128,256]{2,1,0:T(8,128)S(1)}, u32[]{:S(2)}, u32[]{:S(2)}) collective-permute-start(f32[4,128,256]{2,1,0:T(8,128)S(1)} %get-tuple-element.18), channel_id=1, source_target_pairs={{0,1},{1,0},{2,3},{3,2},{4,5},{5,4},{6,7},{7,6},{8,9},{9,8},{10,11... | collective-permute-start | bytes 1572872 | tf_op jit(solution)/shard_map/ppermute | solution.py:332
  92.7 13.1 %all-to-all-start.2 = ((f32[4,128,256]{2,1,0:T(8,128)}), f32[4,128,256]{2,1,0:T(8,128)S(1)}, u32[]{:S(2)}, u32[]{:S(2)}) async-start(f32[4,128,256]{2,1,0:T(8,128)} %add.8), calls=%async_computation.2 | async-start | bytes 1048576 | tf_op jit(solution)/shard_map/all_to_all | solution.py:334
  96.9 3.4 %copy-start.1 = (f32[1024,2048]{1,0:T(8,128)S(1)}, f32[1024,2048]{1,0:T(8,128)}, u32[]{:S(2)}) copy-start(f32[1024,2048]{1,0:T(8,128)} %copy-done) | copy-start | bytes 25165828
  100.3 0.9 copy-start.9

commit v4 on v3

v4 whole, which is shorter than its diff:
```python
import jax
import jax.numpy as jnp
from jax import lax
from jax.experimental import pallas as pl
from jax.experimental.pallas import tpu as pltpu
from jax.sharding import PartitionSpec as P

SUB = 128
LANES = 128
WIDE = 512
FIRST = 1024
MIDDLE = SUB // 2 - 1
F32 = jnp.float32
BF16 = jnp.bfloat16


def dot(a, b, dims=((1,), (0,))):
    return lax.dot_general(a, b, (dims, ((), ())), preferred_element_type=F32)


def running_sums(decays):
    rows = lax.broadcasted_iota(jnp.int32, (SUB, SUB), 0)
    columns = lax.broadcasted_iota(jnp.int32, (SUB, SUB), 1)
    lower = jnp.where(rows >= columns, 1.0, 0.0).astype(BF16)
    first = decays.astype(BF16)
    left = decays - first.astype(F32)
    second = left.astype(BF16)
    third = (left - second.astype(F32)).astype(BF16)
    sums = []
    for start in range(0, decays.shape[1], SUB):
        tok = slice(start, start + SUB)
        a, b, c = (dot(lower, term[:, tok], ((1,), (1,))) for term in (first, second, third))
        sums.append(a + (b + c))
    return sums


def two_terms(values, heads):
    lane = lax.broadcasted_iota(jnp.int32, values.shape, 1)
    high = values.astype(BF16).astype(F32)
    kept = jnp.where(lane < heads, high, jnp.where(lane < 2 * heads, values - high, 0.0))
    return kept.astype(BF16)


def spread_matrix(heads, head_size, wide, step):
    row = lax.broadcasted_iota(jnp.int32, (LANES, wide), 0)
    column = lax.broadcasted_iota(jnp.int32, (LANES, wide), 1)
    same = lax.rem(row, heads) == (step * wide + column) // head_size
    return jnp.where(same, 1.0, 0.0).astype(BF16)


def summary_kernel(x_hbm, g_hbm, w_hbm, r_hbm, ld_hbm, out_hbm, fx, fg, ends, wt, rt, xb, gb, w_ref, r_ref, ld_ref, out_ref, sems):
    heads, tokens = ld_ref.shape
    steps, _, wide = xb.shape
    head_size = wide * steps // heads
    state = w_ref.shape[1]
    pairs = wide // LANES

    def load(source, target, step, sem):
        columns = pl.ds(pl.multiple_of(step * wide, wide), wide)
        return pltpu.make_async_copy(source.at[:, columns], target.at[step], sems.at[sem])

    def save(step):
        slots = pl.ds(step * pairs, pairs)
        return pltpu.make_async_copy(out_ref.at[slots], out_hbm.at[slots], sems.at[2 * steps + step])

    small = [
        pltpu.make_async_copy(source, target, sems.at[3 * steps + n])
        for n, (source, target) in enumerate(((ld_hbm, ld_ref), (w_hbm, w_ref), (r_hbm, r_ref)))
    ]
    for copy in small:
        copy.start()
    for step in range(steps):
        load(x_hbm, xb, step, step).start()
        load(g_hbm, gb, step, steps + step).start()

    small[0].wait()
    sums = running_sums(jnp.concatenate([ld_ref[...]] * (LANES // heads), axis=0))
    before = jnp.zeros((1, LANES), F32)
    for k in range(len(sums)):
        sums[k] = sums[k] + before
        before = sums[k][SUB - 1 :]
    for k in range(len(sums)):
        tok = slice(k * SUB, (k + 1) * SUB)
        fx[tok] = two_terms(jnp.exp(before - sums[k]), heads)
        fg[tok] = two_terms(jnp.exp(sums[k]), heads)
    ends[...] = two_terms(jnp.exp(jnp.broadcast_to(before, ends.shape)), heads)
    small[1].wait()
    small[2].wait()
    for start in range(0, tokens, SUB):
        tok = slice(start, start + SUB)
        wt[:, tok] = w_ref[tok].T
        rt[:, tok] = r_ref[tok].T

    for step in range(steps):
        spread = spread_matrix(heads, head_size, wide, step)
        load(x_hbm, xb, step, step).wait()
        written = dot(wt[...], (xb[step].astype(F32) * dot(fx[...], spread)).astype(BF16))
        load(g_hbm, gb, step, steps + step).wait()
        collected = dot(rt[...], (gb[step].astype(F32) * dot(fg[...], spread)).astype(BF16))
        decay = dot(ends[...], spread)[:8]
        for pair in range(pairs):
            lanes = slice(pair * LANES, (pair + 1) * LANES)
            out_ref[step * pairs + pair, :state] = written[:, lanes]
            out_ref[step * pairs + pair, state : 2 * state] = collected[:, lanes]
            out_ref[step * pairs + pair, 2 * state :] = decay[:, lanes]
        save(step).start()
    for step in range(steps):
        save(step).wait()


def scan_kernel(in_ref, out_hbm, out_ref, sems):
    shards = in_ref.shape[0]
    state = out_ref.shape[1] // 2
    carried = jnp.zeros((state, LANES), F32)
    for shard in range(shards):
        out_ref[shard, :state] = carried
        carried = in_ref[shard, 2 * state : 2 * state + 1] * carried + in_ref[shard, :state]
    carried = jnp.zeros((state, LANES), F32)
    copies = []
    for shard in reversed(range(shards)):
        out_ref[shard, state:] = carried
        carried = in_ref[shard, 2 * state : 2 * state + 1] * carried + in_ref[shard, state : 2 * state]
        copies.append(pltpu.make_async_copy(out_ref.at[shard], out_hbm.at[shard], sems.at[shard]))
        copies[-1].start()
    for copy in copies:
        copy.wait()


def local_kernel(
    x_ref, g_ref, w_ref, r_ref, ld_ref, gi_ref, out_ref, x1_ref, g1_ref, fx, fa, fb, fg, between, pw, wt, rt, xs, gs, acc, wrote, took, into_s, back_s
):
    heads, tokens = ld_ref.shape
    wide = x_ref.shape[1]
    head_size = wide * pl.num_programs(0) // heads
    count, state, _ = wt.shape
    step = pl.program_id(0)
    rows = lax.broadcasted_iota(jnp.int32, (SUB, SUB), 0)
    columns = lax.broadcasted_iota(jnp.int32, (SUB, SUB), 1)
    upper = columns >= rows

    @pl.when(step == 0)
    def _():
        sums = running_sums(jnp.concatenate([ld_ref[...]] * (LANES // heads), axis=0))
        before = jnp.zeros((1, LANES), F32)
        middles = []
        afters = []
        for k in range(count):
            tok = slice(k * SUB, (k + 1) * SUB)
            middle = sums[k][MIDDLE : MIDDLE + 1]
            fa[tok] = two_terms(jnp.exp(middle - sums[k]), heads)
            fb[tok] = two_terms(jnp.exp(sums[k] - middle), heads)
            middles.append(middle)
            afters.append(sums[k][SUB - 1 :] - middle)
            sums[k] = sums[k] + before
            before = sums[k][SUB - 1 :]
            write, read = w_ref[tok], r_ref[tok]
            pairs = jnp.where(upper, dot(write, read, ((1,), (1,))), 0.0).astype(BF16)
            pw[k] = jnp.concatenate([pairs, write], axis=1)
            wt[k] = write.T
            rt[k] = read.T
        into = [middles[0]] + [middles[k] + afters[k - 1] for k in range(1, count)]
        back = [afters[k] + middles[k + 1] for k in range(count - 1)] + [afters[count - 1]]
        between[...] = two_terms(jnp.exp(jnp.concatenate(into + back, axis=0)), heads)
        for k in range(count):
            tok = slice(k * SUB, (k + 1) * SUB)
            fx[tok] = two_terms(jnp.exp(before - sums[k]), heads)
            fg[tok] = two_terms(jnp.exp(sums[k]), heads)
        acc[...] = jnp.zeros_like(acc)

    spread = spread_matrix(heads, head_size, wide, step)
    factor = dot(between[...], spread)
    x1_ref[...] = (x_ref[...].astype(F32) * dot(fx[...], spread)).astype(BF16)
    g1_ref[...] = (g_ref[...].astype(F32) * dot(fg[...], spread)).astype(BF16)
    xs[...] = (x_ref[...].astype(F32) * dot(fa[...], spread)).astype(BF16)
    gs[...] = (g_ref[...].astype(F32) * dot(fb[...], spread)).astype(BF16)
    for k in range(count):
        tok = slice(k * SUB, (k + 1) * SUB)
        took[k] = dot(rt[k], gs[tok])
        wrote[k] = dot(wt[k], xs[tok])

    back = jnp.zeros((state, wide), F32)
    for k in reversed(range(count)):
        back_s[k] = back.astype(BF16)
        if k:
            back = factor[count + k - 1 : count + k] * (back + took[k])
    into = jnp.zeros((state, wide), F32)
    for k in range(count):
        into_s[k] = into.astype(BF16)
        if k + 1 < count:
            into = factor[k + 1 : k + 2] * (into + wrote[k])

    for k in range(count):
        tok = slice(k * SUB, (k + 1) * SUB)
        right = jnp.concatenate([gs[tok], back_s[k]], axis=0)
        left = jnp.concatenate([xs[tok], into_s[k]], axis=0)
        gi_ref[tok] = dot(fa[tok], spread) * dot(pw[k], right)
        acc[k] += dot(left, right, ((1,), (1,)))

    @pl.when(step == pl.num_programs(0) - 1)
    def _():
        for k in range(count):
            tok = slice(k * SUB, (k + 1) * SUB)
            weights = jnp.where(upper, acc[k, :SUB, :SUB], 0.0).astype(BF16)
            out_ref[k, :, :state] = dot(weights, r_ref[tok]) + acc[k, :SUB, SUB:]
            out_ref[k, :, state:] = (dot(wt[k], weights) + acc[k, SUB:, :SUB]).T


def meet_kernel(core_ref, x1_hbm, g1_hbm, part_hbm, st_ref, out_ref, *rest, first):
    states = rest[0] if first else st_ref
    x1, g1, part, sems = rest[-4:]
    chips = out_ref.shape[0]
    state = states.shape[0] // 2
    which = 1 - core_ref[0] if first else core_ref[0]

    def load(chip):
        k = 2 * chip + which
        tok = pl.ds(pl.multiple_of(k * SUB, SUB), SUB)
        return (
            pltpu.make_async_copy(x1_hbm.at[tok], x1.at[chip], sems.at[chip]),
            pltpu.make_async_copy(g1_hbm.at[tok], g1.at[chip], sems.at[chips + chip]),
            pltpu.make_async_copy(part_hbm.at[k], part.at[chip], sems.at[2 * chips + chip]),
        )

    for chip in range(chips):
        for copy in load(chip):
            copy.start()
    if first:
        for p in range(st_ref.shape[0]):
            states[:, p * LANES : (p + 1) * LANES] = st_ref[p].astype(BF16)
    for chip in range(chips):
        for copy in load(chip):
            copy.wait()
        out_ref[chip, :, :state] = part[chip, :, :state] + dot(x1[chip], states[state:], ((1,), (1,)))
        out_ref[chip, :, state:] = part[chip, :, state:] + dot(g1[chip], states[:state], ((1,), (1,)))


def finish_kernel(gi_ref, st_ref, w_ref, fx, out_ref, *, heads):
    wide = gi_ref.shape[1]
    head_size = wide * pl.num_programs(0) // heads
    state = w_ref.shape[1]
    spread = spread_matrix(heads, head_size, wide, pl.program_id(0))
    leaving = jnp.concatenate([st_ref[p, state:].astype(BF16) for p in range(wide // LANES)], axis=1)
    for start in range(0, w_ref.shape[0], WIDE):
        tok = slice(start, start + WIDE)
        out_ref[tok] = (gi_ref[tok] + dot(fx[tok], spread) * dot(w_ref[tok], leaving)).astype(BF16)


def params(mib):
    return pltpu.CompilerParams(vmem_limit_bytes=mib * 2**20)


def in_hbm(array):
    return pltpu.with_memory_space_constraint(array, pltpu.HBM)


HERE = pl.BlockSpec(memory_space=pltpu.VMEM)


def fixed(*shape):
    return pl.BlockSpec(shape, lambda i: (0,) * len(shape))


def summarise(x, g, w, r, ld):
    tokens, width = x.shape
    state = w.shape[1]
    steps = width // FIRST
    there = pl.BlockSpec(memory_space=pltpu.HBM)
    payload = (width // LANES, 2 * state + 8, LANES)
    return pl.pallas_call(
        summary_kernel,
        in_specs=[there] * 5,
        out_specs=there,
        out_shape=jax.ShapeDtypeStruct(payload, F32),
        scratch_shapes=[
            pltpu.VMEM((tokens, LANES), BF16),
            pltpu.VMEM((tokens, LANES), BF16),
            pltpu.VMEM((16, LANES), BF16),
            pltpu.VMEM((state, tokens), BF16),
            pltpu.VMEM((state, tokens), BF16),
            pltpu.VMEM((steps, tokens, FIRST), BF16),
            pltpu.VMEM((steps, tokens, FIRST), BF16),
            pltpu.VMEM((tokens, state), BF16),
            pltpu.VMEM((tokens, state), BF16),
            pltpu.VMEM(ld.shape, F32),
            pltpu.VMEM(payload, F32),
            pltpu.SemaphoreType.DMA((3 * steps + 3,)),
        ],
        compiler_params=params(60),
        name="summary",
    )(x, g, w, r, ld)


def scan_shards(every):
    shards = every.shape[0]
    shape = (shards, every.shape[1] - 8, LANES)
    return pl.pallas_call(
        scan_kernel,
        in_specs=[HERE],
        out_specs=pl.BlockSpec(memory_space=pltpu.HBM),
        out_shape=pltpu.HBM(shape, F32),
        scratch_shapes=[pltpu.VMEM(shape, F32), pltpu.SemaphoreType.DMA((shards,))],
        compiler_params=params(16),
        name="scan",
    )(every)


def local_gradients(x, g, w, r, ld):
    tokens, width = x.shape
    state = w.shape[1]
    count = tokens // SUB
    wide = pl.BlockSpec((tokens, WIDE), lambda i: (0, i))
    return pl.pallas_call(
        local_kernel,
        grid=(width // WIDE,),
        in_specs=[wide, wide, fixed(tokens, state), fixed(tokens, state), fixed(*ld.shape)],
        out_specs=[wide, fixed(count, SUB, 2 * state), wide, wide, fixed(tokens, LANES)],
        out_shape=[
            pltpu.HBM((tokens, width), F32),
            pltpu.HBM((count, SUB, 2 * state), F32),
            pltpu.HBM((tokens, width), BF16),
            pltpu.HBM((tokens, width), BF16),
            pltpu.HBM((tokens, LANES), BF16),
        ],
        scratch_shapes=[
            pltpu.VMEM((tokens, LANES), BF16),
            pltpu.VMEM((tokens, LANES), BF16),
            pltpu.VMEM((tokens, LANES), BF16),
            pltpu.VMEM((2 * count, LANES), BF16),
            pltpu.VMEM((count, SUB, SUB + state), BF16),
            pltpu.VMEM((count, state, SUB), BF16),
            pltpu.VMEM((count, state, SUB), BF16),
            pltpu.VMEM((tokens, WIDE), BF16),
            pltpu.VMEM((tokens, WIDE), BF16),
            pltpu.VMEM((count, SUB + state, SUB + state), F32),
            pltpu.VMEM((count, state, WIDE), F32),
            pltpu.VMEM((count, state, WIDE), F32),
            pltpu.VMEM((count, state, WIDE), BF16),
            pltpu.VMEM((count, state, WIDE), BF16),
        ],
        compiler_params=params(60),
        cost_estimate=pl.CostEstimate(flops=10**10, bytes_accessed=26 * 10**6, transcendentals=0),
        name="local",
    )(in_hbm(x), in_hbm(g), w, r, ld)


def meet(core, x1, g1, parts, states, first):
    tokens, width = x1.shape
    count, _, both = parts.shape
    chips = count // 2

    def kernel(*refs):
        meet_kernel(*refs, first=first)

    return pl.pallas_call(
        kernel,
        in_specs=[pl.BlockSpec(memory_space=pltpu.SMEM)] + [pl.BlockSpec(memory_space=pltpu.HBM)] * 3 + [HERE],
        out_specs=[HERE] * (1 + first),
        out_shape=[
            jax.ShapeDtypeStruct((chips, SUB, both), F32),
            jax.ShapeDtypeStruct((both, width), BF16),
        ][: 1 + first],
        scratch_shapes=[
            pltpu.VMEM((chips, SUB, width), BF16),
            pltpu.VMEM((chips, SUB, width), BF16),
            pltpu.VMEM((chips, SUB, both), F32),
            pltpu.SemaphoreType.DMA((3 * chips,)),
        ],
        compiler_params=params(24),
        cost_estimate=pl.CostEstimate(flops=10**9, bytes_accessed=4 * 10**6, transcendentals=0),
        name="meet_other" if first else "meet_mine",
    )(core, in_hbm(x1), in_hbm(g1), in_hbm(parts), states)


def finish(gi, own, w, fx, heads):
    tokens, width = gi.shape
    state = w.shape[1]
    pairs = WIDE // LANES
    wide = pl.BlockSpec((tokens, WIDE), lambda i: (0, i))

    def kernel(*refs):
        finish_kernel(*refs, heads=heads)

    return pl.pallas_call(
        kernel,
        grid=(width // WIDE,),
        in_specs=[
            wide,
            pl.BlockSpec((pairs, 2 * state, LANES), lambda i: (i, 0, 0)),
            fixed(tokens, state),
            fixed(tokens, LANES),
        ],
        out_specs=wide,
        out_shape=jax.ShapeDtypeStruct((tokens, width), BF16),
        compiler_params=params(40),
        cost_estimate=pl.CostEstimate(flops=2 * 10**9, bytes_accessed=13 * 10**6, transcendentals=0),
        name="finish",
    )(in_hbm(gi), own, w, fx)


def body(scaled_input, out_grad, write_proj, read_proj, log_decay):
    heads = log_decay.shape[0]
    state = write_proj.shape[1]
    ranks = lax.axis_size("head")
    core = (lax.axis_index("head") % 2).astype(jnp.int32).reshape(1)
    every = lax.all_to_all(
        summarise(scaled_input, out_grad, write_proj, read_proj, log_decay), "seq", 0, 0, tiled=True
    )
    gi, parts, x1, g1, fx = local_gradients(scaled_input, out_grad, write_proj, read_proj, log_decay)
    own = lax.all_to_all(scan_shards(every), "seq", 0, 0, tiled=True)
    other, states = meet(core, x1, g1, parts, own, True)
    arrived = lax.ppermute(other, "head", [(i, i ^ 1) for i in range(ranks)])
    (mine,) = meet(core, x1, g1, parts, states, False)
    groups = [list(range(first, ranks, 2)) for first in range(2)]
    shared = lax.all_to_all(mine + arrived, "head", 0, 0, axis_index_groups=groups, tiled=True).sum(axis=0)
    grad_input = finish(gi, own, write_proj, fx, heads)
    return grad_input, shared[:, :state].astype(BF16), shared[:, state:].astype(BF16)


def solution(mesh):
    return jax.shard_map(
        body,
        mesh=mesh,
        in_specs=(
            P("seq", "head"),
            P("seq", "head"),
            P("seq", None),
            P("seq", None),
            P("head", "seq"),
        ),
        out_specs=(P("seq", "head"), P(("seq", "head"), None), P(("seq", "head"), None)),
        check_vma=False,
    )
```

time: 107 us -> 103 us (0.963)
  local copies, waits for them, and re-layouts: 19.2 us -> 0.64 us
  Pallas kernels: 29.4 us -> 40.2 us
  waiting for transfers between devices: 7.41 us -> 11.2 us
    unnamed x22 -> x4, local copies, waits for them, and re-layouts: 18.6 us -> 0.01 us
    pallas_call x1, Pallas kernels: 12.9 us -> 18.3 us  [local_gradients(): pl.pallas_call(local_kernel, grid=(width // WIDE,), in_specs=[wide, wide,...]
    all_to_all x1, waiting for transfers between devices: 5.8 us -> 8.95 us  [body(): own = lax.all_to_all(scan_shards(every), 'seq', 0, 0, tiled=True)]
    pallas_call x3 -> x4, Pallas kernels: 12 us -> 14.8 us  [the longest x1 6.95 us: summarise(): pl.pallas_call(summary_kernel, in_specs=[there] * 5, out_specs=there, out...]
    pallas_call x1, Pallas kernels: 4.51 us -> 7.07 us  [finish(): pl.pallas_call(kernel, grid=(width // WIDE,), in_specs=[wide, pl.BlockSpe...]
    all_to_all x1, waiting for transfers between devices: 0.07 us -> 2.22 us  [body(): lax.all_to_all(mine + arrived, 'head', 0, 0, axis_index_groups=groups, ti...]
    ppermute x1, waiting for transfers between devices: 1.54 us -> 0.01 us  [body(): arrived = lax.ppermute(other, 'head', [(i, i ^ 1) for i in range(ranks)])]
  transfers between devices with their start and end apart: 3 -> 3, of which waited for: 3 -> 2; matrix products, arithmetic and copies ran while one was open for 0% -> 0% of each run, Pallas kernels for 16% -> 28%
where the time goes in v4:
time: 103 us; the launch traced here: 102 us
  Pallas kernels  40.2 us (39%)
  blocking collectives  36.6 us (36%)
  starting transfers between devices  12.2 us (12%)
  waiting for transfers between devices  11.2 us (11%)
    all_to_all x1, blocking collectives, body(): lax.all_to_all(summarise(scaled_input, out_grad, write_proj, read_proj, l...  36.6 us
    pallas_call x1, Pallas kernels, local_gradients(): pl.pallas_call(local_kernel, grid=(width // WIDE,), in_specs=[wide, wide,...  18.3 us
    all_to_all x1, waiting for transfers between devices, body(): own = lax.all_to_all(scan_shards(every), 'seq', 0, 0, tiled=True)  8.95 us
    pallas_call x1, Pallas kernels, finish(): pl.pallas_call(kernel, grid=(width // WIDE,), in_specs=[wide, pl.BlockSpe...  7.07 us
    pallas_call x1, Pallas kernels, summarise(): pl.pallas_call(summary_kernel, in_specs=[there] * 5, out_specs=there, out...  6.95 us
    pallas_call x2, Pallas kernels, meet(): pl.pallas_call(kernel, in_specs=[pl.BlockSpec(memory_space=pltpu.SMEM)] +...  6.26 us
    ppermute x1, starting transfers between devices, body(): arrived = lax.ppermute(other, 'head', [(i, i ^ 1) for i in range(ranks)])  4.31 us
    all_to_all x1, starting transfers between devices, body(): lax.all_to_all(mine + arrived, 'head', 0, 0, axis_index_groups=groups, ti...  4.18 us
  transfers between devices with their start and end apart: 3, of which 2 were waited for; matrix products, arithmetic and copies ran while one was open for 0% of the time, Pallas kernels for 28%

profile of v4, /device:TPU:1, one launch (start us, length us, event | category | flops | bytes accessed | tf_op | source)
XLA Modules:
  0.0 102.4 jit_solution(8607852203860511143)
XLA Ops:
  0.6 7.0 %summary.1 = f32[16,264,128]{2,1,0:T(8,128)} custom-call(bf16[1024,2048]{1,0:T(8,128)(2,1)} %x_hbm.1, bf16[1024,2048]{1,0:T(8,128)(2,1)} %g_hbm.1, bf16[1024,128]{1,0:T(8,128)(2,1)} %refs_2_.1, bf16[1024,128]{1,0:T(8,128)(2,1)} %r_hbm.1, f32[32,1024]{1,0:T(8,128)} %ld_hbm.1), custom_call_target="tpu_custom_call" | custom-call | tf_op jit(solution)/shard_map/summary/pallas_call | solution.py:269
  7.6 36.6 %all_to_all.15.in_ref = f32[16,264,128]{2,1,0:T(8,128)S(1)} all-to-all(f32[16,264,128]{2,1,0:T(8,128)} %summary.1), channel_id=1, replica_groups=mesh['seq'=16,'head'=8] {'seq'}, dimensions={0} | all-to-all | bytes 4325376 | tf_op jit(solution)/shard_map/all_to_all | solution.py:405
  44.2 1.6 %scan.1 = f32[16,256,128]{2,1,0:T(8,128)} custom-call(f32[16,264,128]{2,1,0:T(8,128)S(1)} %all_to_all.15.in_ref), custom_call_target="tpu_custom_call" | custom-call | tf_op jit(solution)/shard_map/scan/pallas_call | solution.py:296
  45.7 3.7 %all-to-all-start.1 = ((f32[16,256,128]{2,1,0:T(8,128)}), f32[16,256,128]{2,1,0:T(8,128)S(1)}, u32[]{:S(2)}, u32[]{:S(2)}) async-start(f32[16,256,128]{2,1,0:T(8,128)} %scan.1), calls=%async_computation.1 | async-start | bytes 4194304 | tf_op jit(solution)/shard_map/all_to_all | solution.py:409
  49.5 18.3 %local.1 = (f32[1024,2048]{1,0:T(8,128)}, f32[8,128,256]{2,1,0:T(8,128)}, bf16[1024,2048]{1,0:T(8,128)(2,1)}, bf16[1024,2048]{1,0:T(8,128)(2,1)}, bf16[1024,128]{1,0:T(8,128)(2,1)}) custom-call(bf16[1024,2048]{1,0:T(8,128)(2,1)} %x_hbm.1, bf16[1024,2048]{1,0:T(8,128)(2,1)} %g_hbm.1, bf16[1024,128]{1,0:T(8,128)(2,1)} %refs_2_.1, bf16[1024,128]{1,0:T(8,128)(2,1)} %r_hbm.1, ...), custom_call_target="tpu_custom_call" | custom-call | flops 10000000000 | bytes 26000000 | tf_op jit(solution)/shard_map/local/pallas_call | solution.py:312
  67.8 9.0 %all-to-all-done.1.refs_1_.refs_4_ = f32[16,256,128]{2,1,0:T(8,128)S(1)} async-done(((f32[16,256,128]{2,1,0:T(8,128)}), f32[16,256,128]{2,1,0:T(8,128)S(1)}, u32[]{:S(2)}, u32[]{:S(2)}) %all-to-all-start.1) | async-done | bytes 2097184 | tf_op jit(solution)/shard_map/all_to_all | solution.py:409
  76.8 3.1 %meet_other.1 = (f32[4,128,256]{2,1,0:T(8,128)S(1)}, bf16[256,2048]{1,0:T(8,128)(2,1)S(1)}) custom-call(s32[1]{0:T(128)} %bitcast.refs_0_, bf16[1024,2048]{1,0:T(8,128)(2,1)} %get-tuple-element.12.refs_1_, bf16[1024,2048]{1,0:T(8,128)(2,1)} %get-tuple-element.13.refs_2_, f32[8,128,256]{2,1,0:T(8,128)} %get-tuple-element.14.refs_3_, ...), custom_call_target="tpu_custom_call" | custom-call | flops 1000000000 | bytes 4000000 | tf_op jit(solution)/shard_map/meet_other/pallas_call | solution.py:354
  79.9 4.3 %collective-permute-start = (f32[4,128,256]{2,1,0:T(8,128)S(1)}, f32[4,128,256]{2,1,0:T(8,128)S(1)}, u32[]{:S(2)}, u32[]{:S(2)}) collective-permute-start(f32[4,128,256]{2,1,0:T(8,128)S(1)} %get-tuple-element.16), channel_id=1, source_target_pairs={{0,1},{1,0},{2,3},{3,2},{4,5},{5,4},{6,7},{7,6},{8,9},{9,8},{10,11... | collective-permute-start | bytes 1572872 | tf_op jit(solution)/shard_map/ppermute | solution.py:411
  84.2 0.0 copy-start
  84.2 0.0 copy-start.1
  84.2 3.2 %meet_mine.1 = f32[4,128,256]{2,1,0:T(8,128)S(1)} custom-call(s32[1]{0:T(128)} %bitcast.refs_0_, bf16[1024,2048]{1,0:T(8,128)(2,1)} %get-tuple-element.12.refs_1_, bf16[1024,2048]{1,0:T(8,128)(2,1)} %get-tuple-element.13.refs_2_, f32[8,128,256]{2,1,0:T(8,128)} %get-tuple-element.14.refs_3_, bf16[256,2048]{1,0:T(8,128)(2,1)S(1)} %get-tuple-element.15.refs_4_), custom_call_target="tpu_custom_call" | custom-call | flops 1000000000 | bytes 4000000 | tf_op jit(solution)/shard_map/meet_mine/pallas_call | solution.py:354
  87.4 0.0 collective-permute-done
  87.4 0.9 add.8
  88.3 4.2 %all-to-all-start.2 = ((f32[4,128,256]{2,1,0:T(8,128)}), f32[4,128,256]{2,1,0:T(8,128)S(1)}, u32[]{:S(2)}, u32[]{:S(2)}) async-start(f32[4,128,256]{2,1,0:T(8,128)} %add.8), calls=%async_computation.2 | async-start | bytes 1048576 | tf_op jit(solution)/shard_map/all_to_all | solution.py:414
  92.5 0.0 copy-done
  92.5 0.0 copy-done.1
  92.5 7.1 %finish.1 = bf16[1024,2048]{1,0:T(8,128)(2,1)} custom-call(f32[1024,2048]{1,0:T(8,128)} %get-tuple-element.10.refs_0_, f32[16,256,128]{2,1,0:T(8,128)S(1)} %all-to-all-done.1.refs_1_.refs_4_, bf16[1024,128]{1,0:T(8,128)(2,1)S(1)} %copy-done, bf16[1024,128]{1,0:T(8,128)(2,1)S(1)} %copy-done.1), custom_call_target="tpu_custom_call" | custom-call | flops 2000000000 | bytes 13000000 | tf_op jit(solution)/shard_map/finish/pallas_call | solution.py:383
  99.6 2.2 %all-to-all-done.2 = f32[4,128,256]{2,1,0:T(8,128)S(1)} async-done(((f32[4,128,256]{2,1,0:T(8,128)}), f32[4,128,256]{2,1,0:T(8,128)S(1)}, u32[]{:S(2)}, u32[]{:S(2)}) %all-to-all-start.2) | async-done | bytes 524320 | tf_op jit(solution)/shard_map/all_to_all | solution.py:414
  101.8 0.6 fusion
  (1 shorter events, 0.0 us)
Async XLA Ops:
  45.7 31.1 %all-to-all-start.1 = ((f32[16,256,128]{2,1,0:T(8,128)}), f32[16,256,128]{2,1,0:T(8,128)S(1)}, u32[]{:S(2)}, u32[]{:S(2)}) async-start(f32[16,256,128]{2,1,0:T(8,128)} %scan.1), calls=%async_computation.1 | async-start | bytes 4194304 | tf_op jit(solution)/shard_map/all_to_all | solution.py:409
  79.9 7.5 %collective-permute-start = (f32[4,128,256]{2,1,0:T(8,128)S(1)}, f32[4,128,256]{2,1,0:T(8,128)S(1)}, u32[]{:S(2)}, u32[]{:S(2)}) collective-permute-start(f32[4,128,256]{2,1,0:T(8,128)S(1)} %get-tuple-element.16), channel_id=1, source_target_pairs={{0,1},{1,0},{2,3},{3,2},{4,5},{5,4},{6,7},{7,6},{8,9},{9,8},{10,11... | collective-permute-start | bytes 1572872 | tf_op jit(solution)/shard_map/ppermute | solution.py:411
  84.2 8.3 %copy-start = (bf16[1024,128]{1,0:T(8,128)(2,1)S(1)}, bf16[1024,128]{1,0:T(8,128)(2,1)}, u32[]{:S(2)}) copy-start(bf16[1024,128]{1,0:T(8,128)(2,1)} %refs_2_.1) | copy-start | bytes 786436
  84.2 8.3 %copy-start.1 = (bf16[1024,128]{1,0:T(8,128)(2,1)S(1)}, bf16[1024,128]{1,0:T(8,128)(2,1)}, u32[]{:S(2)}) copy-start(bf16[1024,128]{1,0:T(8,128)(2,1)} %get-tuple-element.11.refs_3_) | copy-start | bytes 786436
  88.3 13.5 %all-to-all-start.2 = ((f32[4,128,256]{2,1,0:T(8,128)}), f32[4,128,256]{2,1,0:T(8,128)S(1)}, u32[]{:S(2)}, u32[]{:S(2)}) async-start(f32[4,128,256]{2,1,0:T(8,128)} %add.8), calls=%async_computation.2 | async-start | bytes 1048576 | tf_op jit(solution)/shard_map/all_to_all | solution.py:414

commit v5 on v4

--- a/solution.py
+++ b/solution.py
@@ -108,7 +108,7 @@
         save(step).wait()
 
 
-def scan_kernel(in_ref, out_hbm, out_ref, sems):
+def scan_kernel(in_ref, out_ref):
     shards = in_ref.shape[0]
     state = out_ref.shape[1] // 2
     carried = jnp.zeros((state, LANES), F32)
@@ -116,14 +116,9 @@
         out_ref[shard, :state] = carried
         carried = in_ref[shard, 2 * state : 2 * state + 1] * carried + in_ref[shard, :state]
     carried = jnp.zeros((state, LANES), F32)
-    copies = []
     for shard in reversed(range(shards)):
         out_ref[shard, state:] = carried
         carried = in_ref[shard, 2 * state : 2 * state + 1] * carried + in_ref[shard, state : 2 * state]
-        copies.append(pltpu.make_async_copy(out_ref.at[shard], out_hbm.at[shard], sems.at[shard]))
-        copies[-1].start()
-    for copy in copies:
-        copy.wait()
 
 
 def local_kernel(
@@ -205,33 +200,25 @@
             out_ref[k, :, state:] = (dot(wt[k], weights) + acc[k, SUB:, :SUB]).T
 
 
-def meet_kernel(core_ref, x1_hbm, g1_hbm, part_hbm, st_ref, out_ref, *rest, first):
-    states = rest[0] if first else st_ref
-    x1, g1, part, sems = rest[-4:]
+def meet_half(place_ref, away, x1_ref, g1_ref, states, part_ref, out_ref):
+    state = states.shape[0] // 2
     chips = out_ref.shape[0]
-    state = states.shape[0] // 2
-    which = 1 - core_ref[0] if first else core_ref[0]
-
-    def load(chip):
-        k = 2 * chip + which
+    core = 1 - place_ref[1] if away else place_ref[1]
+    for slot in range(chips):
+        k = 2 * lax.rem(place_ref[0] + slot, chips) + core
         tok = pl.ds(pl.multiple_of(k * SUB, SUB), SUB)
-        return (
-            pltpu.make_async_copy(x1_hbm.at[tok], x1.at[chip], sems.at[chip]),
-            pltpu.make_async_copy(g1_hbm.at[tok], g1.at[chip], sems.at[chips + chip]),
-            pltpu.make_async_copy(part_hbm.at[k], part.at[chip], sems.at[2 * chips + chip]),
-        )
-
-    for chip in range(chips):
-        for copy in load(chip):
-            copy.start()
-    if first:
-        for p in range(st_ref.shape[0]):
-            states[:, p * LANES : (p + 1) * LANES] = st_ref[p].astype(BF16)
-    for chip in range(chips):
-        for copy in load(chip):
-            copy.wait()
-        out_ref[chip, :, :state] = part[chip, :, :state] + dot(x1[chip], states[state:], ((1,), (1,)))
-        out_ref[chip, :, state:] = part[chip, :, state:] + dot(g1[chip], states[:state], ((1,), (1,)))
+        out_ref[slot, :, :state] = part_ref[k, :, :state] + dot(x1_ref[tok], states[state:], ((1,), (1,)))
+        out_ref[slot, :, state:] = part_ref[k, :, state:] + dot(g1_ref[tok], states[:state], ((1,), (1,)))
+
+
+def meet_other_kernel(place_ref, x1_ref, g1_ref, st_ref, part_ref, out_ref, states):
+    for p in range(st_ref.shape[0]):
+        states[:, p * LANES : (p + 1) * LANES] = st_ref[p].astype(BF16)
+    meet_half(place_ref, True, x1_ref, g1_ref, states, part_ref, out_ref)
+
+
+def meet_mine_kernel(place_ref, x1_ref, g1_ref, states, part_ref, out_ref):
+    meet_half(place_ref, False, x1_ref, g1_ref, states, part_ref, out_ref)
 
 
 def finish_kernel(gi_ref, st_ref, w_ref, fx, out_ref, *, heads):
@@ -291,14 +278,11 @@
 
 
 def scan_shards(every):
-    shards = every.shape[0]
-    shape = (shards, every.shape[1] - 8, LANES)
     return pl.pallas_call(
         scan_kernel,
         in_specs=[HERE],
-        out_specs=pl.BlockSpec(memory_space=pltpu.HBM),
-        out_shape=pltpu.HBM(shape, F32),
-        scratch_shapes=[pltpu.VMEM(shape, F32), pltpu.SemaphoreType.DMA((shards,))],
+        out_specs=HERE,
+        out_shape=jax.ShapeDtypeStruct((every.shape[0], every.shape[1] - 8, LANES), F32),
         compiler_params=params(16),
         name="scan",
     )(every)
@@ -343,32 +327,21 @@
     )(in_hbm(x), in_hbm(g), w, r, ld)
 
 
-def meet(core, x1, g1, parts, states, first):
+def meet(kernel, place, x1, g1, states, parts, keep):
     tokens, width = x1.shape
     count, _, both = parts.shape
-    chips = count // 2
-
-    def kernel(*refs):
-        meet_kernel(*refs, first=first)
-
     return pl.pallas_call(
         kernel,
-        in_specs=[pl.BlockSpec(memory_space=pltpu.SMEM)] + [pl.BlockSpec(memory_space=pltpu.HBM)] * 3 + [HERE],
-        out_specs=[HERE] * (1 + first),
+        in_specs=[pl.BlockSpec(memory_space=pltpu.SMEM)] + [HERE] * 4,
+        out_specs=[HERE] * (1 + keep),
         out_shape=[
-            jax.ShapeDtypeStruct((chips, SUB, both), F32),
+            jax.ShapeDtypeStruct((count // 2, SUB, both), F32),
             jax.ShapeDtypeStruct((both, width), BF16),
-        ][: 1 + first],
-        scratch_shapes=[
-            pltpu.VMEM((chips, SUB, width), BF16),
-            pltpu.VMEM((chips, SUB, width), BF16),
-            pltpu.VMEM((chips, SUB, both), F32),
-            pltpu.SemaphoreType.DMA((3 * chips,)),
-        ],
-        compiler_params=params(24),
+        ][: 1 + keep],
+        compiler_params=params(16),
         cost_estimate=pl.CostEstimate(flops=10**9, bytes_accessed=4 * 10**6, transcendentals=0),
-        name="meet_other" if first else "meet_mine",
-    )(core, in_hbm(x1), in_hbm(g1), in_hbm(parts), states)
+        name="meet_other" if keep else "meet_mine",
+    )(place, x1, g1, states, parts)
 
 
 def finish(gi, own, w, fx, heads):
@@ -397,21 +370,31 @@
     )(in_hbm(gi), own, w, fx)
 
 
+def over_chips(terms):
+    ranks = lax.axis_size("head")
+    arrived = [
+        lax.ppermute(terms[d], "head", [(i, (i + 2 * d) % ranks) for i in range(ranks)])
+        for d in range(1, terms.shape[0])
+    ]
+    return sum(arrived, terms[0])
+
+
 def body(scaled_input, out_grad, write_proj, read_proj, log_decay):
     heads = log_decay.shape[0]
     state = write_proj.shape[1]
     ranks = lax.axis_size("head")
-    core = (lax.axis_index("head") % 2).astype(jnp.int32).reshape(1)
+    rank = lax.axis_index("head")
+    place = jnp.stack([rank // 2, rank % 2]).astype(jnp.int32)
     every = lax.all_to_all(
         summarise(scaled_input, out_grad, write_proj, read_proj, log_decay), "seq", 0, 0, tiled=True
     )
-    gi, parts, x1, g1, fx = local_gradients(scaled_input, out_grad, write_proj, read_proj, log_decay)
+    local = local_gradients(scaled_input, out_grad, write_proj, read_proj, log_decay)
+    every, place, gi, parts, x1, g1, fx = lax.optimization_barrier((every, place, *local))
     own = lax.all_to_all(scan_shards(every), "seq", 0, 0, tiled=True)
-    other, states = meet(core, x1, g1, parts, own, True)
+    other, states = meet(meet_other_kernel, place, x1, g1, own, parts, True)
     arrived = lax.ppermute(other, "head", [(i, i ^ 1) for i in range(ranks)])
-    (mine,) = meet(core, x1, g1, parts, states, False)
-    groups = [list(range(first, ranks, 2)) for first in range(2)]
-    shared = lax.all_to_all(mine + arrived, "head", 0, 0, axis_index_groups=groups, tiled=True).sum(axis=0)
+    (mine,) = meet(meet_mine_kernel, place, x1, g1, states, parts, False)
+    shared = over_chips(mine + arrived)
     grad_input = finish(gi, own, write_proj, fx, heads)
     return grad_input, shared[:, :state].astype(BF16), shared[:, state:].astype(BF16)
 

time: 103 us -> 99.6 us (0.967)
  blocking collectives: 36.6 us -> 30.9 us
  Pallas kernels: 40.2 us -> 36.1 us
  starting transfers between devices: 12.2 us -> 16.2 us
  waiting for transfers between devices: 11.2 us -> 13.3 us
  local copies, waits for them, and re-layouts: 0.64 us -> 1.9 us
    all_to_all x1, blocking collectives: 36.6 us -> 30.9 us  [body(): own = lax.all_to_all(scan_shards(every), 'seq', 0, 0, tiled=True)]
    ppermute x0 -> x3, starting transfers between devices: none -> 5.06 us  [over_chips(): lax.ppermute(terms[d], 'head', [(i, (i + 2 * d) % ranks) for i in range(r...]
    pallas_call x2, Pallas kernels: 6.26 us -> 3.61 us  [meet(): pl.pallas_call(kernel, in_specs=[pl.BlockSpec(memory_space=pltpu.SMEM)] +...]
    all_to_all x2 -> x1, waiting for transfers between devices: 11.2 us -> 13.3 us  [body(): lax.all_to_all(summarise(scaled_input, out_grad, write_proj, read_proj, l...]
    ppermute x1, starting transfers between devices: 4.31 us -> 2.68 us  [body(): arrived = lax.ppermute(other, 'head', [(i, i ^ 1) for i in range(ranks)])]
    pallas_call x1, Pallas kernels: 1.58 us -> 0.16 us  [scan_shards(): pl.pallas_call(scan_kernel, in_specs=[HERE], out_specs=HERE, out_shape=ja...]
    unnamed x4 -> x10, local copies, waits for them, and re-layouts: 0.01 us -> 1.24 us
    all_to_all x2 -> x1, starting transfers between devices: 7.91 us -> 8.44 us  [body(): lax.all_to_all(summarise(scaled_input, out_grad, write_proj, read_proj, l...]
  transfers between devices with their start and end apart: 3 -> 5, of which waited for: 2 -> 1; matrix products, arithmetic and copies ran while one was open for 0% -> 0% of each run, Pallas kernels for 28% -> 27%
where the time goes in v5:
time: 99.6 us; the launch traced here: 99.4 us
  Pallas kernels  36.1 us (36%)
  blocking collectives  30.9 us (31%)
  starting transfers between devices  16.2 us (16%)
  waiting for transfers between devices  13.3 us (13%)
  local copies, waits for them, and re-layouts  1.9 us (2%)
    all_to_all x1, blocking collectives, body(): own = lax.all_to_all(scan_shards(every), 'seq', 0, 0, tiled=True)  30.9 us
    pallas_call x1, Pallas kernels, local_gradients(): pl.pallas_call(local_kernel, grid=(width // WIDE,), in_specs=[wide, wide,...  18.3 us
    all_to_all x1, waiting for transfers between devices, body(): lax.all_to_all(summarise(scaled_input, out_grad, write_proj, read_proj, l...  13.3 us
    all_to_all x1, starting transfers between devices, body(): lax.all_to_all(summarise(scaled_input, out_grad, write_proj, read_proj, l...  8.44 us
    pallas_call x1, Pallas kernels, finish(): pl.pallas_call(kernel, grid=(width // WIDE,), in_specs=[wide, pl.BlockSpe...  7.07 us
    pallas_call x1, Pallas kernels, summarise(): pl.pallas_call(summary_kernel, in_specs=[there] * 5, out_specs=there, out...  6.95 us
    ppermute x3, starting transfers between devices, over_chips(): lax.ppermute(terms[d], 'head', [(i, (i + 2 * d) % ranks) for i in range(r...  5.06 us
    pallas_call x2, Pallas kernels, meet(): pl.pallas_call(kernel, in_specs=[pl.BlockSpec(memory_space=pltpu.SMEM)] +...  3.61 us
  transfers between devices with their start and end apart: 5, of which 1 were waited for; matrix products, arithmetic and copies ran while one was open for 0% of the time, Pallas kernels for 27%

profile of v5, /device:TPU:1, one launch (start us, length us, event | category | flops | bytes accessed | tf_op | source)
XLA Modules:
  0.0 99.4 jit_solution(17898146143738628541)
XLA Ops:
  0.6 7.0 %summary.1 = f32[16,264,128]{2,1,0:T(8,128)} custom-call(bf16[1024,2048]{1,0:T(8,128)(2,1)} %x_ref.1, bf16[1024,2048]{1,0:T(8,128)(2,1)} %g_ref.1, bf16[1024,128]{1,0:T(8,128)(2,1)} %refs_2_.1, bf16[1024,128]{1,0:T(8,128)(2,1)} %r_ref.1, f32[32,1024]{1,0:T(8,128)} %ld_ref.1), custom_call_target="tpu_custom_call" | custom-call | tf_op jit(solution)/shard_map/summary/pallas_call | solution.py:256
  7.6 8.4 %all-to-all-start = ((f32[16,264,128]{2,1,0:T(8,128)}), f32[16,264,128]{2,1,0:T(8,128)S(1)}, u32[]{:S(2)}, u32[]{:S(2)}) async-start(f32[16,264,128]{2,1,0:T(8,128)} %summary.1), calls=%async_computation | async-start | bytes 4325376 | tf_op jit(solution)/shard_map/all_to_all | solution.py:388
  16.1 0.1 pad_add_fusion.place_ref
  16.1 18.3 %local.1 = (f32[1024,2048]{1,0:T(8,128)}, f32[8,128,256]{2,1,0:T(8,128)}, bf16[1024,2048]{1,0:T(8,128)(2,1)}, bf16[1024,2048]{1,0:T(8,128)(2,1)}, bf16[1024,128]{1,0:T(8,128)(2,1)}) custom-call(bf16[1024,2048]{1,0:T(8,128)(2,1)} %x_ref.1, bf16[1024,2048]{1,0:T(8,128)(2,1)} %g_ref.1, bf16[1024,128]{1,0:T(8,128)(2,1)} %refs_2_.1, bf16[1024,128]{1,0:T(8,128)(2,1)} %r_ref.1, ...), custom_call_target="tpu_custom_call" | custom-call | flops 10000000000 | bytes 26000000 | tf_op jit(solution)/shard_map/local/pallas_call | solution.py:296
  34.5 13.3 %all-to-all-done.in_ref = f32[16,264,128]{2,1,0:T(8,128)S(1)} async-done(((f32[16,264,128]{2,1,0:T(8,128)}), f32[16,264,128]{2,1,0:T(8,128)S(1)}, u32[]{:S(2)}, u32[]{:S(2)}) %all-to-all-start) | async-done | bytes 2162720 | tf_op jit(solution)/shard_map/all_to_all | solution.py:388
  47.8 0.0 copy-start
  47.8 0.0 copy-start.1
  47.8 0.2 scan.1
  47.9 30.9 %all_to_all.10.refs_1_.st_ref = f32[16,256,128]{2,1,0:T(8,128)S(1)} all-to-all(f32[16,256,128]{2,1,0:T(8,128)S(1)} %scan.1), channel_id=1, replica_groups=mesh['seq'=16,'head'=8] {'seq'}, dimensions={0} | all-to-all | bytes 4194304 | tf_op jit(solution)/shard_map/all_to_all | solution.py:393
  78.9 0.0 copy-done
  78.9 0.0 copy-done.1
  78.9 0.0 copy-start.2
  78.9 1.2 %copy-done.2 = f32[8,128,256]{2,1,0:T(8,128)S(1)} copy-done((f32[8,128,256]{2,1,0:T(8,128)S(1)}, f32[8,128,256]{2,1,0:T(8,128)}, u32[]{:S(2)}) %copy-start.2) | copy-done | bytes 1048600
  80.1 1.8 %meet_other.1 = (f32[4,128,256]{2,1,0:T(8,128)S(1)}, bf16[256,2048]{1,0:T(8,128)(2,1)S(1)}) custom-call(s32[2]{0:T(128)S(1)} %pad_add_fusion.place_ref, bf16[1024,2048]{1,0:T(8,128)(2,1)S(1)} %copy-done, bf16[1024,2048]{1,0:T(8,128)(2,1)S(1)} %copy-done.1, f32[16,256,128]{2,1,0:T(8,128)S(1)} %all_to_all.10.refs_1_.st_ref, f32[8,128,256]{2,1,0:T(8,128)S(1)} %copy-done.2), custom_call_target="tpu_custom_call" | custom-call | flops 1000000000 | bytes 4000000 | tf_op jit(solution)/shard_map/meet_other/pallas_call | solution.py:333
  81.9 2.7 %collective-permute-start = (f32[4,128,256]{2,1,0:T(8,128)S(1)}, f32[4,128,256]{2,1,0:T(8,128)S(1)}, u32[]{:S(2)}, u32[]{:S(2)}) collective-permute-start(f32[4,128,256]{2,1,0:T(8,128)S(1)} %get-tuple-element.30), channel_id=1, source_target_pairs={{0,1},{1,0},{2,3},{3,2},{4,5},{5,4},{6,7},{7,6},{8,9},{9,8},{10,11... | collective-permute-start | bytes 1572872 | tf_op jit(solution)/shard_map/ppermute | solution.py:395
  84.6 0.0 copy-start.3
  84.6 0.0 copy-start.4
  84.6 1.8 %meet_mine.1 = f32[4,128,256]{2,1,0:T(8,128)S(1)} custom-call(s32[2]{0:T(128)S(1)} %pad_add_fusion.place_ref, bf16[1024,2048]{1,0:T(8,128)(2,1)S(1)} %copy-done, bf16[1024,2048]{1,0:T(8,128)(2,1)S(1)} %copy-done.1, bf16[256,2048]{1,0:T(8,128)(2,1)S(1)} %get-tuple-element.29.states, f32[8,128,256]{2,1,0:T(8,128)S(1)} %copy-done.2), custom_call_target="tpu_custom_call" | custom-call | flops 1000000000 | bytes 4000000 | tf_op jit(solution)/shard_map/meet_mine/pallas_call | solution.py:333
  86.4 0.0 collective-permute-done
  86.4 0.1 add.18
  86.6 1.4 %collective-permute-start.1 = (f32[128,256]{1,0:T(8,128)S(1)}, f32[128,256]{1,0:T(8,128)S(1)}, u32[]{:S(2)}, u32[]{:S(2)}) collective-permute-start(f32[128,256]{1,0:T(8,128)S(1)} %get-tuple-element.31), channel_id=1, source_target_pairs={{0,2},{1,3},{2,4},{3,5},{4,6},{5,7},{6,0},{7,1},{8,10},{9,11},{10,... | collective-permute-start | bytes 393224 | tf_op jit(solution)/shard_map/ppermute | solution.py:376
  87.9 2.6 %collective-permute-start.2 = (f32[128,256]{1,0:T(8,128)S(1)}, f32[128,256]{1,0:T(8,128)S(1)}, u32[]{:S(2)}, u32[]{:S(2)}) collective-permute-start(f32[128,256]{1,0:T(8,128)S(1)} %get-tuple-element.33), channel_id=1, source_target_pairs={{0,4},{1,5},{2,6},{3,7},{4,0},{5,1},{6,2},{7,3},{8,12},{9,13},{10,... | collective-permute-start | bytes 393224 | tf_op jit(solution)/shard_map/ppermute | solution.py:376
  90.6 1.1 %collective-permute-start.3 = (f32[128,256]{1,0:T(8,128)S(1)}, f32[128,256]{1,0:T(8,128)S(1)}, u32[]{:S(2)}, u32[]{:S(2)}) collective-permute-start(f32[128,256]{1,0:T(8,128)S(1)} %get-tuple-element.32), channel_id=1, source_target_pairs={{0,6},{1,7},{2,0},{3,1},{4,2},{5,3},{6,4},{7,5},{8,14},{9,15},{10,... | collective-permute-start | bytes 393224 | tf_op jit(solution)/shard_map/ppermute | solution.py:376
  91.6 0.0 copy-done.3
  91.6 0.0 copy-done.4
  91.6 7.1 %finish.1 = bf16[1024,2048]{1,0:T(8,128)(2,1)} custom-call(f32[1024,2048]{1,0:T(8,128)} %get-tuple-element.22.refs_0_, f32[16,256,128]{2,1,0:T(8,128)S(1)} %all_to_all.10.refs_1_.st_ref, bf16[1024,128]{1,0:T(8,128)(2,1)S(1)} %copy-done.3, bf16[1024,128]{1,0:T(8,128)(2,1)S(1)} %copy-done.4), custom_call_target="tpu_custom_call" | custom-call | flops 2000000000 | bytes 13000000 | tf_op jit(solution)/shard_map/finish/pallas_call | solution.py:356
  98.7 0.0 collective-permute-done.1
  98.7 0.0 collective-permute-done.2
  98.7 0.0 collective-permute-done.3
  98.7 0.6 fusion.4
  (2 shorter events, 0.1 us)
Async XLA Ops:
  7.6 40.2 %all-to-all-start = ((f32[16,264,128]{2,1,0:T(8,128)}), f32[16,264,128]{2,1,0:T(8,128)S(1)}, u32[]{:S(2)}, u32[]{:S(2)}) async-start(f32[16,264,128]{2,1,0:T(8,128)} %summary.1), calls=%async_computation | async-start | bytes 4325376 | tf_op jit(solution)/shard_map/all_to_all | solution.py:388
  47.8 31.1 %copy-start = (bf16[1024,2048]{1,0:T(8,128)(2,1)S(1)}, bf16[1024,2048]{1,0:T(8,128)(2,1)}, u32[]{:S(2)}) copy-start(bf16[1024,2048]{1,0:T(8,128)(2,1)} %get-tuple-element.26.x1_ref) | copy-start | bytes 12582916
  47.8 31.1 %copy-start.1 = (bf16[1024,2048]{1,0:T(8,128)(2,1)S(1)}, bf16[1024,2048]{1,0:T(8,128)(2,1)}, u32[]{:S(2)}) copy-start(bf16[1024,2048]{1,0:T(8,128)(2,1)} %get-tuple-element.27.g1_ref) | copy-start | bytes 12582916
  78.9 1.2 %copy-start.2 = (f32[8,128,256]{2,1,0:T(8,128)S(1)}, f32[8,128,256]{2,1,0:T(8,128)}, u32[]{:S(2)}) copy-start(f32[8,128,256]{2,1,0:T(8,128)} %get-tuple-element.28.part_ref) | copy-start | bytes 3145732
  81.9 4.5 %collective-permute-start = (f32[4,128,256]{2,1,0:T(8,128)S(1)}, f32[4,128,256]{2,1,0:T(8,128)S(1)}, u32[]{:S(2)}, u32[]{:S(2)}) collective-permute-start(f32[4,128,256]{2,1,0:T(8,128)S(1)} %get-tuple-element.30), channel_id=1, source_target_pairs={{0,1},{1,0},{2,3},{3,2},{4,5},{5,4},{6,7},{7,6},{8,9},{9,8},{10,11... | collective-permute-start | bytes 1572872 | tf_op jit(solution)/shard_map/ppermute | solution.py:395
  84.6 7.0 %copy-start.3 = (bf16[1024,128]{1,0:T(8,128)(2,1)S(1)}, bf16[1024,128]{1,0:T(8,128)(2,1)}, u32[]{:S(2)}) copy-start(bf16[1024,128]{1,0:T(8,128)(2,1)} %refs_2_.1) | copy-start | bytes 786436
  84.6 7.0 %copy-start.4 = (bf16[1024,128]{1,0:T(8,128)(2,1)S(1)}, bf16[1024,128]{1,0:T(8,128)(2,1)}, u32[]{:S(2)}) copy-start(bf16[1024,128]{1,0:T(8,128)(2,1)} %get-tuple-element.24.refs_3_) | copy-start | bytes 786436
  86.6 12.1 %collective-permute-start.1 = (f32[128,256]{1,0:T(8,128)S(1)}, f32[128,256]{1,0:T(8,128)S(1)}, u32[]{:S(2)}, u32[]{:S(2)}) collective-permute-start(f32[128,256]{1,0:T(8,128)S(1)} %get-tuple-element.31), channel_id=1, source_target_pairs={{0,2},{1,3},{2,4},{3,5},{4,6},{5,7},{6,0},{7,1},{8,10},{9,11},{10,... | collective-permute-start | bytes 393224 | tf_op jit(solution)/shard_map/ppermute | solution.py:376
  87.9 10.8 %collective-permute-start.2 = (f32[128,256]{1,0:T(8,128)S(1)}, f32[128,256]{1,0:T(8,128)S(1)}, u32[]{:S(2)}, u32[]{:S(2)}) collective-permute-start(f32[128,256]{1,0:T(8,128)S(1)} %get-tuple-element.33), channel_id=1, source_target_pairs={{0,4},{1,5},{2,6},{3,7},{4,0},{5,1},{6,2},{7,3},{8,12},{9,13},{10,... | collective-permute-start | bytes 393224 | tf_op jit(solution)/shard_map/ppermute | solution.py:376
  90.6 8.1 %collective-permute-start.3 = (f32[128,256]{1,0:T(8,128)S(1)}, f32[128,256]{1,0:T(8,128)S(1)}, u32[]{:S(2)}, u32[]{:S(2)}) collective-permute-start(f32[128,256]{1,0:T(8,128)S(1)} %get-tuple-element.32), channel_id=1, source_target_pairs={{0,6},{1,7},{2,0},{3,1},{4,2},{5,3},{6,4},{7,5},{8,14},{9,15},{10,... | collective-permute-start | bytes 393224 | tf_op jit(solution)/shard_map/ppermute | solution.py:376

commit v6 on v5

--- a/solution.py
+++ b/solution.py
@@ -200,36 +200,60 @@
             out_ref[k, :, state:] = (dot(wt[k], weights) + acc[k, SUB:, :SUB]).T
 
 
-def meet_half(place_ref, away, x1_ref, g1_ref, states, part_ref, out_ref):
+def meet_half(place_ref, away, x1_ref, g1_ref, part_hbm, states, out_ref, part, sems, prepare=None):
     state = states.shape[0] // 2
     chips = out_ref.shape[0]
     core = 1 - place_ref[1] if away else place_ref[1]
+    blocks = [2 * lax.rem(place_ref[0] + slot, chips) + core for slot in range(chips)]
+
+    def load(slot):
+        return pltpu.make_async_copy(part_hbm.at[blocks[slot]], part.at[slot], sems.at[slot])
+
     for slot in range(chips):
-        k = 2 * lax.rem(place_ref[0] + slot, chips) + core
-        tok = pl.ds(pl.multiple_of(k * SUB, SUB), SUB)
-        out_ref[slot, :, :state] = part_ref[k, :, :state] + dot(x1_ref[tok], states[state:], ((1,), (1,)))
-        out_ref[slot, :, state:] = part_ref[k, :, state:] + dot(g1_ref[tok], states[:state], ((1,), (1,)))
-
-
-def meet_other_kernel(place_ref, x1_ref, g1_ref, st_ref, part_ref, out_ref, states):
-    for p in range(st_ref.shape[0]):
-        states[:, p * LANES : (p + 1) * LANES] = st_ref[p].astype(BF16)
-    meet_half(place_ref, True, x1_ref, g1_ref, states, part_ref, out_ref)
-
-
-def meet_mine_kernel(place_ref, x1_ref, g1_ref, states, part_ref, out_ref):
-    meet_half(place_ref, False, x1_ref, g1_ref, states, part_ref, out_ref)
-
-
-def finish_kernel(gi_ref, st_ref, w_ref, fx, out_ref, *, heads):
-    wide = gi_ref.shape[1]
-    head_size = wide * pl.num_programs(0) // heads
+        load(slot).start()
+    if prepare:
+        prepare()
+    for slot in range(chips):
+        tok = pl.ds(pl.multiple_of(blocks[slot] * SUB, SUB), SUB)
+        to_write = dot(x1_ref[tok], states[state:], ((1,), (1,)))
+        to_read = dot(g1_ref[tok], states[:state], ((1,), (1,)))
+        load(slot).wait()
+        out_ref[slot, :, :state] = part[slot, :, :state] + to_write
+        out_ref[slot, :, state:] = part[slot, :, state:] + to_read
+
+
+def meet_other_kernel(place_ref, x1_ref, g1_ref, part_hbm, st_ref, out_ref, states, part, sems):
+    def prepare():
+        for p in range(st_ref.shape[0]):
+            states[:, p * LANES : (p + 1) * LANES] = st_ref[p].astype(BF16)
+
+    meet_half(place_ref, True, x1_ref, g1_ref, part_hbm, states, out_ref, part, sems, prepare)
+
+
+def meet_mine_kernel(place_ref, x1_ref, g1_ref, part_hbm, states, out_ref, part, sems):
+    meet_half(place_ref, False, x1_ref, g1_ref, part_hbm, states, out_ref, part, sems)
+
+
+def finish_kernel(gi_ref, st_ref, w_ref, fx, out_hbm, out, sems, *, heads):
+    tokens, width = gi_ref.shape
+    head_size = width // heads
     state = w_ref.shape[1]
-    spread = spread_matrix(heads, head_size, wide, pl.program_id(0))
-    leaving = jnp.concatenate([st_ref[p, state:].astype(BF16) for p in range(wide // LANES)], axis=1)
-    for start in range(0, w_ref.shape[0], WIDE):
-        tok = slice(start, start + WIDE)
-        out_ref[tok] = (gi_ref[tok] + dot(fx[tok], spread) * dot(w_ref[tok], leaving)).astype(BF16)
+    steps, _, wide = out.shape
+
+    def store(step):
+        return pltpu.make_async_copy(out.at[step], out_hbm.at[:, pl.ds(step * wide, wide)], sems.at[step])
+
+    for step in range(steps):
+        lanes = slice(step * wide, (step + 1) * wide)
+        spread = spread_matrix(heads, head_size, wide, step)
+        pairs = range(step * (wide // LANES), (step + 1) * (wide // LANES))
+        leaving = jnp.concatenate([st_ref[p, state:].astype(BF16) for p in pairs], axis=1)
+        for start in range(0, tokens, WIDE):
+            tok = slice(start, start + WIDE)
+            out[step, tok] = (gi_ref[tok, lanes] + dot(fx[tok], spread) * dot(w_ref[tok], leaving)).astype(BF16)
+        store(step).start()
+    for step in range(steps):
+        store(step).wait()
 
 
 def params(mib):
@@ -327,47 +351,41 @@
     )(in_hbm(x), in_hbm(g), w, r, ld)
 
 
-def meet(kernel, place, x1, g1, states, parts, keep):
+def meet(kernel, place, x1, g1, parts, states, keep):
     tokens, width = x1.shape
     count, _, both = parts.shape
     return pl.pallas_call(
         kernel,
-        in_specs=[pl.BlockSpec(memory_space=pltpu.SMEM)] + [HERE] * 4,
+        in_specs=[pl.BlockSpec(memory_space=pltpu.SMEM), HERE, HERE, pl.BlockSpec(memory_space=pltpu.HBM), HERE],
         out_specs=[HERE] * (1 + keep),
         out_shape=[
             jax.ShapeDtypeStruct((count // 2, SUB, both), F32),
             jax.ShapeDtypeStruct((both, width), BF16),
         ][: 1 + keep],
+        scratch_shapes=[pltpu.VMEM((count // 2, SUB, both), F32), pltpu.SemaphoreType.DMA((count // 2,))],
         compiler_params=params(16),
         cost_estimate=pl.CostEstimate(flops=10**9, bytes_accessed=4 * 10**6, transcendentals=0),
         name="meet_other" if keep else "meet_mine",
-    )(place, x1, g1, states, parts)
+    )(place, x1, g1, in_hbm(parts), states)
 
 
 def finish(gi, own, w, fx, heads):
     tokens, width = gi.shape
-    state = w.shape[1]
-    pairs = WIDE // LANES
-    wide = pl.BlockSpec((tokens, WIDE), lambda i: (0, i))
+    steps = width // WIDE
 
     def kernel(*refs):
         finish_kernel(*refs, heads=heads)
 
     return pl.pallas_call(
         kernel,
-        grid=(width // WIDE,),
-        in_specs=[
-            wide,
-            pl.BlockSpec((pairs, 2 * state, LANES), lambda i: (i, 0, 0)),
-            fixed(tokens, state),
-            fixed(tokens, LANES),
-        ],
-        out_specs=wide,
+        in_specs=[HERE] * 4,
+        out_specs=pl.BlockSpec(memory_space=pltpu.HBM),
         out_shape=jax.ShapeDtypeStruct((tokens, width), BF16),
-        compiler_params=params(40),
+        scratch_shapes=[pltpu.VMEM((steps, tokens, WIDE), BF16), pltpu.SemaphoreType.DMA((steps,))],
+        compiler_params=params(16),
         cost_estimate=pl.CostEstimate(flops=2 * 10**9, bytes_accessed=13 * 10**6, transcendentals=0),
         name="finish",
-    )(in_hbm(gi), own, w, fx)
+    )(gi, own, w, fx)
 
 
 def over_chips(terms):
@@ -391,9 +409,9 @@
     local = local_gradients(scaled_input, out_grad, write_proj, read_proj, log_decay)
     every, place, gi, parts, x1, g1, fx = lax.optimization_barrier((every, place, *local))
     own = lax.all_to_all(scan_shards(every), "seq", 0, 0, tiled=True)
-    other, states = meet(meet_other_kernel, place, x1, g1, own, parts, True)
+    other, states = meet(meet_other_kernel, place, x1, g1, parts, own, True)
     arrived = lax.ppermute(other, "head", [(i, i ^ 1) for i in range(ranks)])
-    (mine,) = meet(meet_mine_kernel, place, x1, g1, states, parts, False)
+    (mine,) = meet(meet_mine_kernel, place, x1, g1, parts, states, False)
     shared = over_chips(mine + arrived)
     grad_input = finish(gi, own, write_proj, fx, heads)
     return grad_input, shared[:, :state].astype(BF16), shared[:, state:].astype(BF16)

time: 99.6 us -> 99.3 us (level)
  waiting for transfers between devices: 13.3 us -> 15.3 us
  local copies, waits for them, and re-layouts: 1.9 us -> 0.68 us
  Pallas kernels: 36.1 us -> 35.1 us
    ppermute x3, waiting for transfers between devices: 0.01 us -> 1.97 us  [over_chips(): lax.ppermute(terms[d], 'head', [(i, (i + 2 * d) % ranks) for i in range(r...]
    unnamed x10 -> x12, local copies, waits for them, and re-layouts: 1.24 us -> 0.02 us
    pallas_call x3, Pallas kernels: 10.7 us -> 9.65 us  [the longest x2 6.31 us: meet(): pl.pallas_call(kernel, in_specs=[pl.BlockSpec(memory_space=pltpu.SMEM), H...]
  transfers between devices with their start and end apart: 5 -> 5, of which waited for: 1 -> 2; matrix products, arithmetic and copies ran while one was open for 0% -> 0% of each run, Pallas kernels for 27% -> 25%
where the time goes in v6:
time: 99.3 us; the launch traced here: 99.1 us
  Pallas kernels  35.1 us (35%)
  blocking collectives  30.9 us (31%)
  starting transfers between devices  16.2 us (16%)
  waiting for transfers between devices  15.3 us (15%)
    all_to_all x1, blocking collectives, body(): own = lax.all_to_all(scan_shards(every), 'seq', 0, 0, tiled=True)  30.9 us
    pallas_call x1, Pallas kernels, local_gradients(): pl.pallas_call(local_kernel, grid=(width // WIDE,), in_specs=[wide, wide,...  18.3 us
    all_to_all x1, waiting for transfers between devices, body(): lax.all_to_all(summarise(scaled_input, out_grad, write_proj, read_proj, l...  13.3 us
    all_to_all x1, starting transfers between devices, body(): lax.all_to_all(summarise(scaled_input, out_grad, write_proj, read_proj, l...  8.44 us
    pallas_call x1, Pallas kernels, summarise(): pl.pallas_call(summary_kernel, in_specs=[there] * 5, out_specs=there, out...  6.97 us
    pallas_call x2, Pallas kernels, meet(): pl.pallas_call(kernel, in_specs=[pl.BlockSpec(memory_space=pltpu.SMEM), H...  6.31 us
    ppermute x3, starting transfers between devices, over_chips(): lax.ppermute(terms[d], 'head', [(i, (i + 2 * d) % ranks) for i in range(r...  5.06 us
    pallas_call x1, Pallas kernels, finish(): pl.pallas_call(kernel, in_specs=[HERE] * 4, out_specs=pl.BlockSpec(memory...  3.35 us
  transfers between devices with their start and end apart: 5, of which 2 were waited for; matrix products, arithmetic and copies ran while one was open for 0% of the time, Pallas kernels for 25%

profile of v6, /device:TPU:1, one launch (start us, length us, event | category | flops | bytes accessed | tf_op | source)
XLA Modules:
  0.0 99.1 jit_solution(3566485682950986736)
XLA Ops:
  0.6 7.0 %summary.1 = f32[16,264,128]{2,1,0:T(8,128)} custom-call(bf16[1024,2048]{1,0:T(8,128)(2,1)} %x_ref.1, bf16[1024,2048]{1,0:T(8,128)(2,1)} %g_ref.1, bf16[1024,128]{1,0:T(8,128)(2,1)} %refs_2_.1, bf16[1024,128]{1,0:T(8,128)(2,1)} %r_ref.1, f32[32,1024]{1,0:T(8,128)} %ld_ref.1), custom_call_target="tpu_custom_call" | custom-call | tf_op jit(solution)/shard_map/summary/pallas_call | solution.py:280
  7.6 8.4 %all-to-all-start = ((f32[16,264,128]{2,1,0:T(8,128)}), f32[16,264,128]{2,1,0:T(8,128)S(1)}, u32[]{:S(2)}, u32[]{:S(2)}) async-start(f32[16,264,128]{2,1,0:T(8,128)} %summary.1), calls=%async_computation | async-start | bytes 4325376 | tf_op jit(solution)/shard_map/all_to_all | solution.py:406
  16.1 0.1 pad_add_fusion.place_ref
  16.2 18.3 %local.1 = (f32[1024,2048]{1,0:T(8,128)}, f32[8,128,256]{2,1,0:T(8,128)}, bf16[1024,2048]{1,0:T(8,128)(2,1)}, bf16[1024,2048]{1,0:T(8,128)(2,1)}, bf16[1024,128]{1,0:T(8,128)(2,1)}) custom-call(bf16[1024,2048]{1,0:T(8,128)(2,1)} %x_ref.1, bf16[1024,2048]{1,0:T(8,128)(2,1)} %g_ref.1, bf16[1024,128]{1,0:T(8,128)(2,1)} %refs_2_.1, bf16[1024,128]{1,0:T(8,128)(2,1)} %r_ref.1, ...), custom_call_target="tpu_custom_call" | custom-call | flops 10000000000 | bytes 26000000 | tf_op jit(solution)/shard_map/local/pallas_call | solution.py:320
  34.5 13.3 %all-to-all-done.in_ref = f32[16,264,128]{2,1,0:T(8,128)S(1)} async-done(((f32[16,264,128]{2,1,0:T(8,128)}), f32[16,264,128]{2,1,0:T(8,128)S(1)}, u32[]{:S(2)}, u32[]{:S(2)}) %all-to-all-start) | async-done | bytes 2162720 | tf_op jit(solution)/shard_map/all_to_all | solution.py:406
  47.8 0.0 copy-start
  47.8 0.0 copy-start.1
  47.8 0.2 scan.1
  48.0 30.9 %all_to_all.10.refs_1_.st_ref = f32[16,256,128]{2,1,0:T(8,128)S(1)} all-to-all(f32[16,256,128]{2,1,0:T(8,128)S(1)} %scan.1), channel_id=1, replica_groups=mesh['seq'=16,'head'=8] {'seq'}, dimensions={0} | all-to-all | bytes 4194304 | tf_op jit(solution)/shard_map/all_to_all | solution.py:411
  78.9 0.0 copy-done
  78.9 0.0 copy-done.1
  78.9 0.0 slice-start
  78.9 3.2 %meet_other.1 = (f32[4,128,256]{2,1,0:T(8,128)S(1)}, bf16[256,2048]{1,0:T(8,128)(2,1)S(1)}) custom-call(s32[2]{0:T(128)S(1)} %pad_add_fusion.place_ref, bf16[1024,2048]{1,0:T(8,128)(2,1)S(1)} %copy-done, bf16[1024,2048]{1,0:T(8,128)(2,1)S(1)} %copy-done.1, f32[8,128,256]{2,1,0:T(8,128)} %get-tuple-element.28.part_hbm, ...), custom_call_target="tpu_custom_call" | custom-call | flops 1000000000 | bytes 4000000 | tf_op jit(solution)/shard_map/meet_other/pallas_call | solution.py:357
  82.1 2.7 %collective-permute-start = (f32[4,128,256]{2,1,0:T(8,128)S(1)}, f32[4,128,256]{2,1,0:T(8,128)S(1)}, u32[]{:S(2)}, u32[]{:S(2)}) collective-permute-start(f32[4,128,256]{2,1,0:T(8,128)S(1)} %get-tuple-element.30), channel_id=1, source_target_pairs={{0,1},{1,0},{2,3},{3,2},{4,5},{5,4},{6,7},{7,6},{8,9},{9,8},{10,11... | collective-permute-start | bytes 1572872 | tf_op jit(solution)/shard_map/ppermute | solution.py:413
  84.8 0.0 slice-start.1
  84.8 0.0 copy-start.2
  84.8 0.0 copy-start.3
  84.8 3.2 %meet_mine.1 = f32[4,128,256]{2,1,0:T(8,128)S(1)} custom-call(s32[2]{0:T(128)S(1)} %pad_add_fusion.place_ref, bf16[1024,2048]{1,0:T(8,128)(2,1)S(1)} %copy-done, bf16[1024,2048]{1,0:T(8,128)(2,1)S(1)} %copy-done.1, f32[8,128,256]{2,1,0:T(8,128)} %get-tuple-element.28.part_hbm, bf16[256,2048]{1,0:T(8,128)(2,1)S(1)} %get-tuple-element.29.states), custom_call_target="tpu_custom_call" | custom-call | flops 1000000000 | bytes 4000000 | tf_op jit(solution)/shard_map/meet_mine/pallas_call | solution.py:357
  87.9 0.0 collective-permute-done
  87.9 0.1 add.18
  88.0 1.4 %collective-permute-start.1 = (f32[128,256]{1,0:T(8,128)S(1)}, f32[128,256]{1,0:T(8,128)S(1)}, u32[]{:S(2)}, u32[]{:S(2)}) collective-permute-start(f32[128,256]{1,0:T(8,128)S(1)} %get-tuple-element.31), channel_id=1, source_target_pairs={{0,2},{1,3},{2,4},{3,5},{4,6},{5,7},{6,0},{7,1},{8,10},{9,11},{10,... | collective-permute-start | bytes 393224 | tf_op jit(solution)/shard_map/ppermute | solution.py:394
  89.4 2.6 %collective-permute-start.2 = (f32[128,256]{1,0:T(8,128)S(1)}, f32[128,256]{1,0:T(8,128)S(1)}, u32[]{:S(2)}, u32[]{:S(2)}) collective-permute-start(f32[128,256]{1,0:T(8,128)S(1)} %get-tuple-element.33), channel_id=1, source_target_pairs={{0,4},{1,5},{2,6},{3,7},{4,0},{5,1},{6,2},{7,3},{8,12},{9,13},{10,... | collective-permute-start | bytes 393224 | tf_op jit(solution)/shard_map/ppermute | solution.py:394
  92.0 1.1 %collective-permute-start.3 = (f32[128,256]{1,0:T(8,128)S(1)}, f32[128,256]{1,0:T(8,128)S(1)}, u32[]{:S(2)}, u32[]{:S(2)}) collective-permute-start(f32[128,256]{1,0:T(8,128)S(1)} %get-tuple-element.32), channel_id=1, source_target_pairs={{0,6},{1,7},{2,0},{3,1},{4,2},{5,3},{6,4},{7,5},{8,14},{9,15},{10,... | collective-permute-start | bytes 393224 | tf_op jit(solution)/shard_map/ppermute | solution.py:394
  93.1 0.0 slice-done
  93.1 0.0 slice-done.1
  93.1 0.0 copy-done.2
  93.1 0.0 copy-done.3
  93.1 3.3 %finish.1 = bf16[1024,2048]{1,0:T(8,128)(2,1)} custom-call(f32[1024,2048]{1,0:T(8,128)S(1)} %bitcast.19, f32[16,256,128]{2,1,0:T(8,128)S(1)} %all_to_all.10.refs_1_.st_ref, bf16[1024,128]{1,0:T(8,128)(2,1)S(1)} %copy-done.2, bf16[1024,128]{1,0:T(8,128)(2,1)S(1)} %copy-done.3), custom_call_target="tpu_custom_call" | custom-call | flops 2000000000 | bytes 13000000 | tf_op jit(solution)/shard_map/finish/pallas_call | solution.py:379
  96.5 0.0 collective-permute-done.1
  96.5 2.0 %collective-permute-done.2 = f32[128,256]{1,0:T(8,128)S(1)} collective-permute-done((f32[128,256]{1,0:T(8,128)S(1)}, f32[128,256]{1,0:T(8,128)S(1)}, u32[]{:S(2)}, u32[]{:S(2)}) %collective-permute-start.2) | collective-permute-done | bytes 131104 | tf_op jit(solution)/shard_map/ppermute | solution.py:394
  98.5 0.0 collective-permute-done.3
  98.5 0.6 fusion.4
  (3 shorter events, 0.1 us)
Async XLA Ops:
  7.6 40.2 %all-to-all-start = ((f32[16,264,128]{2,1,0:T(8,128)}), f32[16,264,128]{2,1,0:T(8,128)S(1)}, u32[]{:S(2)}, u32[]{:S(2)}) async-start(f32[16,264,128]{2,1,0:T(8,128)} %summary.1), calls=%async_computation | async-start | bytes 4325376 | tf_op jit(solution)/shard_map/all_to_all | solution.py:406
  47.8 31.1 %copy-start = (bf16[1024,2048]{1,0:T(8,128)(2,1)S(1)}, bf16[1024,2048]{1,0:T(8,128)(2,1)}, u32[]{:S(2)}) copy-start(bf16[1024,2048]{1,0:T(8,128)(2,1)} %get-tuple-element.26.x1_ref) | copy-start | bytes 12582916
  47.8 31.1 %copy-start.1 = (bf16[1024,2048]{1,0:T(8,128)(2,1)S(1)}, bf16[1024,2048]{1,0:T(8,128)(2,1)}, u32[]{:S(2)}) copy-start(bf16[1024,2048]{1,0:T(8,128)(2,1)} %get-tuple-element.27.g1_ref) | copy-start | bytes 12582916
  78.9 14.2 %slice-start = ((s8[8388608]{0:T(1024)(128)(4,1)}), s8[4194304]{0:T(1024)(128)(4,1)S(1)}, s32[]{:S(2)}) async-start(s8[8388608]{0:T(1024)(128)(4,1)} %bitcast.18), calls=%async_computation.2 | async-start | bytes 8388608
  82.1 5.8 %collective-permute-start = (f32[4,128,256]{2,1,0:T(8,128)S(1)}, f32[4,128,256]{2,1,0:T(8,128)S(1)}, u32[]{:S(2)}, u32[]{:S(2)}) collective-permute-start(f32[4,128,256]{2,1,0:T(8,128)S(1)} %get-tuple-element.30), channel_id=1, source_target_pairs={{0,1},{1,0},{2,3},{3,2},{4,5},{5,4},{6,7},{7,6},{8,9},{9,8},{10,11... | collective-permute-start | bytes 1572872 | tf_op jit(solution)/shard_map/ppermute | solution.py:413
  84.8 8.4 %slice-start.1 = ((s8[8388608]{0:T(1024)(128)(4,1)}), s8[4194304]{0:T(1024)(128)(4,1)S(1)}, s32[]{:S(2)}) async-start(s8[8388608]{0:T(1024)(128)(4,1)} %bitcast.18), calls=%async_computation.3 | async-start | bytes 8388608
  84.8 8.4 %copy-start.2 = (bf16[1024,128]{1,0:T(8,128)(2,1)S(1)}, bf16[1024,128]{1,0:T(8,128)(2,1)}, u32[]{:S(2)}) copy-start(bf16[1024,128]{1,0:T(8,128)(2,1)} %refs_2_.1) | copy-start | bytes 786436
  84.8 8.4 %copy-start.3 = (bf16[1024,128]{1,0:T(8,128)(2,1)S(1)}, bf16[1024,128]{1,0:T(8,128)(2,1)}, u32[]{:S(2)}) copy-start(bf16[1024,128]{1,0:T(8,128)(2,1)} %get-tuple-element.24.refs_3_) | copy-start | bytes 786436
  88.0 8.4 %collective-permute-start.1 = (f32[128,256]{1,0:T(8,128)S(1)}, f32[128,256]{1,0:T(8,128)S(1)}, u32[]{:S(2)}, u32[]{:S(2)}) collective-permute-start(f32[128,256]{1,0:T(8,128)S(1)} %get-tuple-element.31), channel_id=1, source_target_pairs={{0,2},{1,3},{2,4},{3,5},{4,6},{5,7},{6,0},{7,1},{8,10},{9,11},{10,... | collective-permute-start | bytes 393224 | tf_op jit(solution)/shard_map/ppermute | solution.py:394
  89.4 9.0 %collective-permute-start.2 = (f32[128,256]{1,0:T(8,128)S(1)}, f32[128,256]{1,0:T(8,128)S(1)}, u32[]{:S(2)}, u32[]{:S(2)}) collective-permute-start(f32[128,256]{1,0:T(8,128)S(1)} %get-tuple-element.33), channel_id=1, source_target_pairs={{0,4},{1,5},{2,6},{3,7},{4,0},{5,1},{6,2},{7,3},{8,12},{9,13},{10,... | collective-permute-start | bytes 393224 | tf_op jit(solution)/shard_map/ppermute | solution.py:394
  92.0 6.4 %collective-permute-start.3 = (f32[128,256]{1,0:T(8,128)S(1)}, f32[128,256]{1,0:T(8,128)S(1)}, u32[]{:S(2)}, u32[]{:S(2)}) collective-permute-start(f32[128,256]{1,0:T(8,128)S(1)} %get-tuple-element.32), channel_id=1, source_target_pairs={{0,6},{1,7},{2,0},{3,1},{4,2},{5,3},{6,4},{7,5},{8,14},{9,15},{10,... | collective-permute-start | bytes 393224 | tf_op jit(solution)/shard_map/ppermute | solution.py:394

commit v7 on v6

--- a/solution.py
+++ b/solution.py
@@ -121,8 +121,12 @@
         carried = in_ref[shard, 2 * state : 2 * state + 1] * carried + in_ref[shard, state : 2 * state]
 
 
+def block_of(place_ref, slot, chips, core):
+    return 2 * lax.rem(place_ref[0] + slot, chips) + core
+
+
 def local_kernel(
-    x_ref, g_ref, w_ref, r_ref, ld_ref, gi_ref, out_ref, x1_ref, g1_ref, fx, fa, fb, fg, between, pw, wt, rt, xs, gs, acc, wrote, took, into_s, back_s
+    place_ref, x_ref, g_ref, w_ref, r_ref, ld_ref, gi_ref, other_ref, mine_ref, x1_ref, g1_ref, fx, fa, fb, fg, between, pw, wt, rt, xs, gs, acc, wrote, took, into_s, back_s
 ):
     heads, tokens = ld_ref.shape
     wide = x_ref.shape[1]
@@ -193,45 +197,33 @@
 
     @pl.when(step == pl.num_programs(0) - 1)
     def _():
-        for k in range(count):
-            tok = slice(k * SUB, (k + 1) * SUB)
-            weights = jnp.where(upper, acc[k, :SUB, :SUB], 0.0).astype(BF16)
-            out_ref[k, :, :state] = dot(weights, r_ref[tok]) + acc[k, :SUB, SUB:]
-            out_ref[k, :, state:] = (dot(wt[k], weights) + acc[k, SUB:, :SUB]).T
-
-
-def meet_half(place_ref, away, x1_ref, g1_ref, part_hbm, states, out_ref, part, sems, prepare=None):
+        for out_ref, core in ((other_ref, 1 - place_ref[1]), (mine_ref, place_ref[1])):
+            for slot in range(count // 2):
+                k = block_of(place_ref, slot, count // 2, core)
+                tok = pl.ds(pl.multiple_of(k * SUB, SUB), SUB)
+                weights = jnp.where(upper, acc[k, :SUB, :SUB], 0.0).astype(BF16)
+                out_ref[slot, :, :state] = dot(weights, r_ref[tok]) + acc[k, :SUB, SUB:]
+                out_ref[slot, :, state:] = (dot(wt[k], weights) + acc[k, SUB:, :SUB]).T
+
+
+def meet_half(place_ref, away, x1_ref, g1_ref, states, out_ref):
     state = states.shape[0] // 2
     chips = out_ref.shape[0]
     core = 1 - place_ref[1] if away else place_ref[1]
-    blocks = [2 * lax.rem(place_ref[0] + slot, chips) + core for slot in range(chips)]
-
-    def load(slot):
-        return pltpu.make_async_copy(part_hbm.at[blocks[slot]], part.at[slot], sems.at[slot])
-
     for slot in range(chips):
-        load(slot).start()
-    if prepare:
-        prepare()
-    for slot in range(chips):
-        tok = pl.ds(pl.multiple_of(blocks[slot] * SUB, SUB), SUB)
-        to_write = dot(x1_ref[tok], states[state:], ((1,), (1,)))
-        to_read = dot(g1_ref[tok], states[:state], ((1,), (1,)))
-        load(slot).wait()
-        out_ref[slot, :, :state] = part[slot, :, :state] + to_write
-        out_ref[slot, :, state:] = part[slot, :, state:] + to_read
-
-
-def meet_other_kernel(place_ref, x1_ref, g1_ref, part_hbm, st_ref, out_ref, states, part, sems):
-    def prepare():
-        for p in range(st_ref.shape[0]):
-            states[:, p * LANES : (p + 1) * LANES] = st_ref[p].astype(BF16)
-
-    meet_half(place_ref, True, x1_ref, g1_ref, part_hbm, states, out_ref, part, sems, prepare)
-
-
-def meet_mine_kernel(place_ref, x1_ref, g1_ref, part_hbm, states, out_ref, part, sems):
-    meet_half(place_ref, False, x1_ref, g1_ref, part_hbm, states, out_ref, part, sems)
+        tok = pl.ds(pl.multiple_of(block_of(place_ref, slot, chips, core) * SUB, SUB), SUB)
+        out_ref[slot, :, :state] = dot(x1_ref[tok], states[state:], ((1,), (1,)))
+        out_ref[slot, :, state:] = dot(g1_ref[tok], states[:state], ((1,), (1,)))
+
+
+def meet_other_kernel(place_ref, x1_ref, g1_ref, st_ref, out_ref, states):
+    for p in range(st_ref.shape[0]):
+        states[:, p * LANES : (p + 1) * LANES] = st_ref[p].astype(BF16)
+    meet_half(place_ref, True, x1_ref, g1_ref, states, out_ref)
+
+
+def meet_mine_kernel(place_ref, x1_ref, g1_ref, states, out_ref):
+    meet_half(place_ref, False, x1_ref, g1_ref, states, out_ref)
 
 
 def finish_kernel(gi_ref, st_ref, w_ref, fx, out_hbm, out, sems, *, heads):
@@ -312,7 +304,7 @@
     )(every)
 
 
-def local_gradients(x, g, w, r, ld):
+def local_gradients(place, x, g, w, r, ld):
     tokens, width = x.shape
     state = w.shape[1]
     count = tokens // SUB
@@ -320,11 +312,12 @@
     return pl.pallas_call(
         local_kernel,
         grid=(width // WIDE,),
-        in_specs=[wide, wide, fixed(tokens, state), fixed(tokens, state), fixed(*ld.shape)],
-        out_specs=[wide, fixed(count, SUB, 2 * state), wide, wide, fixed(tokens, LANES)],
+        in_specs=[pl.BlockSpec(memory_space=pltpu.SMEM), wide, wide, fixed(tokens, state), fixed(tokens, state), fixed(*ld.shape)],
+        out_specs=[wide, *[fixed(count // 2, SUB, 2 * state)] * 2, wide, wide, fixed(tokens, LANES)],
         out_shape=[
             pltpu.HBM((tokens, width), F32),
-            pltpu.HBM((count, SUB, 2 * state), F32),
+            pltpu.HBM((count // 2, SUB, 2 * state), F32),
+            pltpu.HBM((count // 2, SUB, 2 * state), F32),
             pltpu.HBM((tokens, width), BF16),
             pltpu.HBM((tokens, width), BF16),
             pltpu.HBM((tokens, LANES), BF16),
@@ -348,25 +341,24 @@
         compiler_params=params(60),
         cost_estimate=pl.CostEstimate(flops=10**10, bytes_accessed=26 * 10**6, transcendentals=0),
         name="local",
-    )(in_hbm(x), in_hbm(g), w, r, ld)
-
-
-def meet(kernel, place, x1, g1, parts, states, keep):
+    )(place, in_hbm(x), in_hbm(g), w, r, ld)
+
+
+def meet(kernel, place, x1, g1, states, keep):
     tokens, width = x1.shape
-    count, _, both = parts.shape
+    both = 2 * LANES
     return pl.pallas_call(
         kernel,
-        in_specs=[pl.BlockSpec(memory_space=pltpu.SMEM), HERE, HERE, pl.BlockSpec(memory_space=pltpu.HBM), HERE],
+        in_specs=[pl.BlockSpec(memory_space=pltpu.SMEM)] + [HERE] * 3,
         out_specs=[HERE] * (1 + keep),
         out_shape=[
-            jax.ShapeDtypeStruct((count // 2, SUB, both), F32),
+            jax.ShapeDtypeStruct((tokens // SUB // 2, SUB, both), F32),
             jax.ShapeDtypeStruct((both, width), BF16),
         ][: 1 + keep],
-        scratch_shapes=[pltpu.VMEM((count // 2, SUB, both), F32), pltpu.SemaphoreType.DMA((count // 2,))],
         compiler_params=params(16),
         cost_estimate=pl.CostEstimate(flops=10**9, bytes_accessed=4 * 10**6, transcendentals=0),
         name="meet_other" if keep else "meet_mine",
-    )(place, x1, g1, in_hbm(parts), states)
+    )(place, x1, g1, states)
 
 
 def finish(gi, own, w, fx, heads):
@@ -388,31 +380,38 @@
     )(gi, own, w, fx)
 
 
-def over_chips(terms):
+def over_cores(other):
+    ranks = lax.axis_size("head")
+    return lax.ppermute(other, "head", [(i, i ^ 1) for i in range(ranks)])
+
+
+def over_chips(terms, start):
     ranks = lax.axis_size("head")
     arrived = [
         lax.ppermute(terms[d], "head", [(i, (i + 2 * d) % ranks) for i in range(ranks)])
         for d in range(1, terms.shape[0])
     ]
-    return sum(arrived, terms[0])
+    return sum(arrived, start + terms[0])
 
 
 def body(scaled_input, out_grad, write_proj, read_proj, log_decay):
     heads = log_decay.shape[0]
     state = write_proj.shape[1]
-    ranks = lax.axis_size("head")
     rank = lax.axis_index("head")
     place = jnp.stack([rank // 2, rank % 2]).astype(jnp.int32)
     every = lax.all_to_all(
         summarise(scaled_input, out_grad, write_proj, read_proj, log_decay), "seq", 0, 0, tiled=True
     )
-    local = local_gradients(scaled_input, out_grad, write_proj, read_proj, log_decay)
-    every, place, gi, parts, x1, g1, fx = lax.optimization_barrier((every, place, *local))
+    gi, other, mine, x1, g1, fx = local_gradients(
+        place, scaled_input, out_grad, write_proj, read_proj, log_decay
+    )
+    local = over_chips(mine + over_cores(other), 0.0)
+    every, place, local, gi, x1, g1, fx = lax.optimization_barrier((every, place, local, gi, x1, g1, fx))
     own = lax.all_to_all(scan_shards(every), "seq", 0, 0, tiled=True)
-    other, states = meet(meet_other_kernel, place, x1, g1, parts, own, True)
-    arrived = lax.ppermute(other, "head", [(i, i ^ 1) for i in range(ranks)])
-    (mine,) = meet(meet_mine_kernel, place, x1, g1, parts, states, False)
-    shared = over_chips(mine + arrived)
+    other, states = meet(meet_other_kernel, place, x1, g1, own, True)
+    arrived = over_cores(other)
+    (mine,) = meet(meet_mine_kernel, place, x1, g1, states, False)
+    shared = over_chips(mine + arrived, local)
     grad_input = finish(gi, own, write_proj, fx, heads)
     return grad_input, shared[:, :state].astype(BF16), shared[:, state:].astype(BF16)
 

time: 99.3 us -> 100 us (level)
  waiting for transfers between devices: 15.3 us -> 8.64 us
  starting transfers between devices: 16.2 us -> 21.2 us
  blocking collectives: 30.9 us -> 34.1 us
  Pallas kernels: 35.1 us -> 32.5 us
  other arithmetic: 0.18 us -> 1.86 us
    all_to_all x1, waiting for transfers between devices: 13.3 us -> 0.01 us  [body(): lax.all_to_all(summarise(scaled_input, out_grad, write_proj, read_proj, l...]
    ppermute x3 -> x6, waiting for transfers between devices: 1.97 us -> 6.89 us  [over_chips(): lax.ppermute(terms[d], 'head', [(i, (i + 2 * d) % ranks) for i in range(r...]
    ppermute x3 -> x6, starting transfers between devices: 5.06 us -> 9.32 us  [over_chips(): lax.ppermute(terms[d], 'head', [(i, (i + 2 * d) % ranks) for i in range(r...]
    all_to_all x1, blocking collectives: 30.9 us -> 34.1 us  [body(): own = lax.all_to_all(scan_shards(every), 'seq', 0, 0, tiled=True)]
    pallas_call x3, Pallas kernels: 24.6 us -> 22 us  [the longest x1 18.4 us: local_gradients(): pl.pallas_call(local_kernel, grid=(width // WIDE,), in_specs=[pl.BlockSpe...]
    ppermute x1 -> x2, waiting for transfers between devices: 0.01 us -> 1.75 us  [over_cores(): return lax.ppermute(other, 'head', [(i, i ^ 1) for i in range(ranks)])]
    add x1 -> x3, other arithmetic: 0.07 us -> 1.21 us  [the longest x1 1.11 us: body(): local = over_chips(mine + over_cores(other), 0.0)]
    ppermute x1 -> x2, starting transfers between devices: 2.68 us -> 3.42 us  [over_cores(): return lax.ppermute(other, 'head', [(i, i ^ 1) for i in range(ranks)])]
  transfers between devices with their start and end apart: 5 -> 9, of which waited for: 2 -> 4; matrix products, arithmetic and copies ran while one was open for 0% -> 2% of each run, Pallas kernels for 25% -> 24%
where the time goes in v7:
time: 100 us; the launch traced here: 99.8 us
  blocking collectives  34.1 us (34%)
  Pallas kernels  32.5 us (32%)
  starting transfers between devices  21.2 us (21%)
  waiting for transfers between devices  8.64 us (9%)
  other arithmetic  1.86 us (2%)
    all_to_all x1, blocking collectives, body(): own = lax.all_to_all(scan_shards(every), 'seq', 0, 0, tiled=True)  34.1 us
    pallas_call x1, Pallas kernels, local_gradients(): pl.pallas_call(local_kernel, grid=(width // WIDE,), in_specs=[pl.BlockSpe...  18.4 us
    ppermute x6, starting transfers between devices, over_chips(): lax.ppermute(terms[d], 'head', [(i, (i + 2 * d) % ranks) for i in range(r...  9.32 us
    all_to_all x1, starting transfers between devices, body(): lax.all_to_all(summarise(scaled_input, out_grad, write_proj, read_proj, l...  8.44 us
    pallas_call x1, Pallas kernels, summarise(): pl.pallas_call(summary_kernel, in_specs=[there] * 5, out_specs=there, out...  6.96 us
    ppermute x6, waiting for transfers between devices, over_chips(): lax.ppermute(terms[d], 'head', [(i, (i + 2 * d) % ranks) for i in range(r...  6.89 us
    pallas_call x2, Pallas kernels, meet(): pl.pallas_call(kernel, in_specs=[pl.BlockSpec(memory_space=pltpu.SMEM)] +...  3.61 us
    ppermute x2, starting transfers between devices, over_cores(): return lax.ppermute(other, 'head', [(i, i ^ 1) for i in range(ranks)])  3.42 us
  transfers between devices with their start and end apart: 9, of which 4 were waited for; matrix products, arithmetic and copies ran while one was open for 2% of the time, Pallas kernels for 24%

profile of v7, /device:TPU:1, one launch (start us, length us, event | category | flops | bytes accessed | tf_op | source)
XLA Modules:
  0.0 99.8 jit_solution(2679297955433948494)
XLA Ops:
  0.6 7.0 %summary.1 = f32[16,264,128]{2,1,0:T(8,128)} custom-call(bf16[1024,2048]{1,0:T(8,128)(2,1)} %x_ref.1, bf16[1024,2048]{1,0:T(8,128)(2,1)} %g_ref.1, bf16[1024,128]{1,0:T(8,128)(2,1)} %refs_2_.1, bf16[1024,128]{1,0:T(8,128)(2,1)} %r_ref.1, f32[32,1024]{1,0:T(8,128)} %ld_ref.1), custom_call_target="tpu_custom_call" | custom-call | tf_op jit(solution)/shard_map/summary/pallas_call | solution.py:272
  7.6 8.4 %all-to-all-start = ((f32[16,264,128]{2,1,0:T(8,128)}), f32[16,264,128]{2,1,0:T(8,128)S(1)}, u32[]{:S(2)}, u32[]{:S(2)}) async-start(f32[16,264,128]{2,1,0:T(8,128)} %summary.1), calls=%async_computation | async-start | bytes 4325376 | tf_op jit(solution)/shard_map/all_to_all | solution.py:402
  16.1 0.6 pad_add_fusion.place_ref
  16.7 18.4 %local.1 = (f32[1024,2048]{1,0:T(8,128)}, f32[4,128,256]{2,1,0:T(8,128)}, f32[4,128,256]{2,1,0:T(8,128)}, bf16[1024,2048]{1,0:T(8,128)(2,1)}, bf16[1024,2048]{1,0:T(8,128)(2,1)}, /*index=5*/bf16[1024,128]{1,0:T(8,128)(2,1)}) custom-call(s32[2]{0:T(128)} %pad_add_fusion.place_ref, bf16[1024,2048]{1,0:T(8,128)(2,1)} %x_ref.1, bf16[1024,2048]{1,0:T(8,128)(2,1)} %g_ref.1, ...), custom_call_target="tpu_custom_call" | custom-call | flops 10000000000 | bytes 26000000 | tf_op jit(solution)/shard_map/local/pallas_call | solution.py:312
  35.1 1.0 %collective-permute-start = (f32[4,128,256]{2,1,0:T(8,128)}, f32[4,128,256]{2,1,0:T(8,128)S(1)}, u32[]{:S(2)}, u32[]{:S(2)}) collective-permute-start(f32[4,128,256]{2,1,0:T(8,128)} %get-tuple-element.19), channel_id=1, source_target_pairs={{0,1},{1,0},{2,3},{3,2},{4,5},{5,4},{6,7},{7,6},{8,9},{9,8},{10,11... | collective-permute-start | bytes 1572872 | tf_op jit(solution)/shard_map/ppermute | solution.py:385
  36.1 1.7 %collective-permute-done = f32[4,128,256]{2,1,0:T(8,128)S(1)} collective-permute-done((f32[4,128,256]{2,1,0:T(8,128)}, f32[4,128,256]{2,1,0:T(8,128)S(1)}, u32[]{:S(2)}, u32[]{:S(2)}) %collective-permute-start) | collective-permute-done | bytes 524320 | tf_op jit(solution)/shard_map/ppermute | solution.py:385
  37.9 1.1 %add.33 = f32[4,128,256]{2,1,0:T(8,128)S(1)} add(f32[4,128,256]{2,1,0:T(8,128)} %get-tuple-element.18, f32[4,128,256]{2,1,0:T(8,128)S(1)} %collective-permute-done) | non-fusion elementwise | flops 131072 | bytes 1572864 | tf_op jit(solution)/shard_map/add | solution.py:408
  39.0 1.4 %collective-permute-start.1 = (f32[128,256]{1,0:T(8,128)S(1)}, f32[128,256]{1,0:T(8,128)S(1)}, u32[]{:S(2)}, u32[]{:S(2)}) collective-permute-start(f32[128,256]{1,0:T(8,128)S(1)} %get-tuple-element.36), channel_id=1, source_target_pairs={{0,2},{1,3},{2,4},{3,5},{4,6},{5,7},{6,0},{7,1},{8,10},{9,11},{10,... | collective-permute-start | bytes 393224 | tf_op jit(solution)/shard_map/ppermute | solution.py:391
  40.4 2.6 %collective-permute-start.2 = (f32[128,256]{1,0:T(8,128)S(1)}, f32[128,256]{1,0:T(8,128)S(1)}, u32[]{:S(2)}, u32[]{:S(2)}) collective-permute-start(f32[128,256]{1,0:T(8,128)S(1)} %get-tuple-element.38), channel_id=1, source_target_pairs={{0,4},{1,5},{2,6},{3,7},{4,0},{5,1},{6,2},{7,3},{8,12},{9,13},{10,... | collective-permute-start | bytes 393224 | tf_op jit(solution)/shard_map/ppermute | solution.py:391
  43.0 1.1 %collective-permute-start.3 = (f32[128,256]{1,0:T(8,128)S(1)}, f32[128,256]{1,0:T(8,128)S(1)}, u32[]{:S(2)}, u32[]{:S(2)}) collective-permute-start(f32[128,256]{1,0:T(8,128)S(1)} %get-tuple-element.37), channel_id=1, source_target_pairs={{0,6},{1,7},{2,0},{3,1},{4,2},{5,3},{6,4},{7,5},{8,14},{9,15},{10,... | collective-permute-start | bytes 393224 | tf_op jit(solution)/shard_map/ppermute | solution.py:391
  44.1 1.1 %collective-permute-done.1 = f32[128,256]{1,0:T(8,128)S(1)} collective-permute-done((f32[128,256]{1,0:T(8,128)S(1)}, f32[128,256]{1,0:T(8,128)S(1)}, u32[]{:S(2)}, u32[]{:S(2)}) %collective-permute-start.1) | collective-permute-done | bytes 131104 | tf_op jit(solution)/shard_map/ppermute | solution.py:391
  45.1 3.9 %collective-permute-done.2 = f32[128,256]{1,0:T(8,128)S(1)} collective-permute-done((f32[128,256]{1,0:T(8,128)S(1)}, f32[128,256]{1,0:T(8,128)S(1)}, u32[]{:S(2)}, u32[]{:S(2)}) %collective-permute-start.2) | collective-permute-done | bytes 131104 | tf_op jit(solution)/shard_map/ppermute | solution.py:391
  49.1 0.0 collective-permute-done.3
  49.1 0.0 all-to-all-done.in_ref
  49.1 0.0 copy-start
  49.2 0.2 scan.1
  49.3 34.1 %all_to_all.10.refs_1_.st_ref = f32[16,256,128]{2,1,0:T(8,128)S(1)} all-to-all(f32[16,256,128]{2,1,0:T(8,128)S(1)} %scan.1), channel_id=1, replica_groups=mesh['seq'=16,'head'=8] {'seq'}, dimensions={0} | all-to-all | bytes 4194304 | tf_op jit(solution)/shard_map/all_to_all | solution.py:410
  83.4 0.0 copy-done.1
  83.4 0.0 slice-start
  83.4 1.8 %meet_other.1 = (f32[4,128,256]{2,1,0:T(8,128)S(1)}, bf16[256,2048]{1,0:T(8,128)(2,1)S(1)}) custom-call(s32[2]{0:T(128)S(1)} %copy-done.4, bf16[1024,2048]{1,0:T(8,128)(2,1)S(1)} %copy-done, bf16[1024,2048]{1,0:T(8,128)(2,1)S(1)} %copy-done.1, f32[16,256,128]{2,1,0:T(8,128)S(1)} %all_to_all.10.refs_1_.st_ref), custom_call_target="tpu_custom_call" | custom-call | flops 1000000000 | bytes 4000000 | tf_op jit(solution)/shard_map/meet_other/pallas_call | solution.py:350
  85.3 2.4 %collective-permute-start.4 = (f32[4,128,256]{2,1,0:T(8,128)S(1)}, f32[4,128,256]{2,1,0:T(8,128)S(1)}, u32[]{:S(2)}, u32[]{:S(2)}) collective-permute-start(f32[4,128,256]{2,1,0:T(8,128)S(1)} %get-tuple-element.32), channel_id=1, source_target_pairs={{0,1},{1,0},{2,3},{3,2},{4,5},{5,4},{6,7},{7,6},{8,9},{9,8},{10,11... | collective-permute-start | bytes 1572872 | tf_op jit(solution)/shard_map/ppermute | solution.py:385
  87.7 1.8 %meet_mine.1 = f32[4,128,256]{2,1,0:T(8,128)S(1)} custom-call(s32[2]{0:T(128)S(1)} %copy-done.4, bf16[1024,2048]{1,0:T(8,128)(2,1)S(1)} %copy-done, bf16[1024,2048]{1,0:T(8,128)(2,1)S(1)} %copy-done.1, bf16[256,2048]{1,0:T(8,128)(2,1)S(1)} %get-tuple-element.31.states), custom_call_target="tpu_custom_call" | custom-call | flops 1000000000 | bytes 4000000 | tf_op jit(solution)/shard_map/meet_mine/pallas_call | solution.py:350
  89.5 0.0 collective-permute-done.4
  89.5 0.1 add.37
  89.6 1.0 %collective-permute-start.5 = (f32[128,256]{1,0:T(8,128)S(1)}, f32[128,256]{1,0:T(8,128)S(1)}, u32[]{:S(2)}, u32[]{:S(2)}) collective-permute-start(f32[128,256]{1,0:T(8,128)S(1)} %get-tuple-element.33), channel_id=1, source_target_pairs={{0,2},{1,3},{2,4},{3,5},{4,6},{5,7},{6,0},{7,1},{8,10},{9,11},{10,... | collective-permute-start | bytes 393224 | tf_op jit(solution)/shard_map/ppermute | solution.py:391
  90.6 2.2 %collective-permute-start.6 = (f32[128,256]{1,0:T(8,128)S(1)}, f32[128,256]{1,0:T(8,128)S(1)}, u32[]{:S(2)}, u32[]{:S(2)}) collective-permute-start(f32[128,256]{1,0:T(8,128)S(1)} %get-tuple-element.35), channel_id=1, source_target_pairs={{0,4},{1,5},{2,6},{3,7},{4,0},{5,1},{6,2},{7,3},{8,12},{9,13},{10,... | collective-permute-start | bytes 393224 | tf_op jit(solution)/shard_map/ppermute | solution.py:391
  92.8 1.1 %collective-permute-start.7 = (f32[128,256]{1,0:T(8,128)S(1)}, f32[128,256]{1,0:T(8,128)S(1)}, u32[]{:S(2)}, u32[]{:S(2)}) collective-permute-start(f32[128,256]{1,0:T(8,128)S(1)} %get-tuple-element.34), channel_id=1, source_target_pairs={{0,6},{1,7},{2,0},{3,1},{4,2},{5,3},{6,4},{7,5},{8,14},{9,15},{10,... | collective-permute-start | bytes 393224 | tf_op jit(solution)/shard_map/ppermute | solution.py:391
  93.9 3.3 %finish.1 = bf16[1024,2048]{1,0:T(8,128)(2,1)} custom-call(f32[1024,2048]{1,0:T(8,128)S(1)} %bitcast.35, f32[16,256,128]{2,1,0:T(8,128)S(1)} %all_to_all.10.refs_1_.st_ref, bf16[1024,128]{1,0:T(8,128)(2,1)S(1)} %copy-done.2, bf16[1024,128]{1,0:T(8,128)(2,1)S(1)} %copy-done.3), custom_call_target="tpu_custom_call" | custom-call | flops 2000000000 | bytes 13000000 | tf_op jit(solution)/shard_map/finish/pallas_call | solution.py:371
  97.2 0.0 collective-permute-done.5
  97.2 1.9 %collective-permute-done.6 = f32[128,256]{1,0:T(8,128)S(1)} collective-permute-done((f32[128,256]{1,0:T(8,128)S(1)}, f32[128,256]{1,0:T(8,128)S(1)}, u32[]{:S(2)}, u32[]{:S(2)}) %collective-permute-start.6) | collective-permute-done | bytes 131104 | tf_op jit(solution)/shard_map/ppermute | solution.py:391
  99.1 0.0 collective-permute-done.7
  99.2 0.6 fusion.8
  (16 shorter events, 0.2 us)
Async XLA Ops:
  7.6 41.5 %all-to-all-start = ((f32[16,264,128]{2,1,0:T(8,128)}), f32[16,264,128]{2,1,0:T(8,128)S(1)}, u32[]{:S(2)}, u32[]{:S(2)}) async-start(f32[16,264,128]{2,1,0:T(8,128)} %summary.1), calls=%async_computation | async-start | bytes 4325376 | tf_op jit(solution)/shard_map/all_to_all | solution.py:402
  35.1 2.8 %collective-permute-start = (f32[4,128,256]{2,1,0:T(8,128)}, f32[4,128,256]{2,1,0:T(8,128)S(1)}, u32[]{:S(2)}, u32[]{:S(2)}) collective-permute-start(f32[4,128,256]{2,1,0:T(8,128)} %get-tuple-element.19), channel_id=1, source_target_pairs={{0,1},{1,0},{2,3},{3,2},{4,5},{5,4},{6,7},{7,6},{8,9},{9,8},{10,11... | collective-permute-start | bytes 1572872 | tf_op jit(solution)/shard_map/ppermute | solution.py:385
  39.0 6.1 %collective-permute-start.1 = (f32[128,256]{1,0:T(8,128)S(1)}, f32[128,256]{1,0:T(8,128)S(1)}, u32[]{:S(2)}, u32[]{:S(2)}) collective-permute-start(f32[128,256]{1,0:T(8,128)S(1)} %get-tuple-element.36), channel_id=1, source_target_pairs={{0,2},{1,3},{2,4},{3,5},{4,6},{5,7},{6,0},{7,1},{8,10},{9,11},{10,... | collective-permute-start | bytes 393224 | tf_op jit(solution)/shard_map/ppermute | solution.py:391
  40.4 8.7 %collective-permute-start.2 = (f32[128,256]{1,0:T(8,128)S(1)}, f32[128,256]{1,0:T(8,128)S(1)}, u32[]{:S(2)}, u32[]{:S(2)}) collective-permute-start(f32[128,256]{1,0:T(8,128)S(1)} %get-tuple-element.38), channel_id=1, source_target_pairs={{0,4},{1,5},{2,6},{3,7},{4,0},{5,1},{6,2},{7,3},{8,12},{9,13},{10,... | collective-permute-start | bytes 393224 | tf_op jit(solution)/shard_map/ppermute | solution.py:391
  43.0 6.1 %collective-permute-start.3 = (f32[128,256]{1,0:T(8,128)S(1)}, f32[128,256]{1,0:T(8,128)S(1)}, u32[]{:S(2)}, u32[]{:S(2)}) collective-permute-start(f32[128,256]{1,0:T(8,128)S(1)} %get-tuple-element.37), channel_id=1, source_target_pairs={{0,6},{1,7},{2,0},{3,1},{4,2},{5,3},{6,4},{7,5},{8,14},{9,15},{10,... | collective-permute-start | bytes 393224 | tf_op jit(solution)/shard_map/ppermute | solution.py:391
  49.1 34.3 %copy-start = (bf16[1024,2048]{1,0:T(8,128)(2,1)S(1)}, bf16[1024,2048]{1,0:T(8,128)(2,1)}, u32[]{:S(2)}) copy-start(bf16[1024,2048]{1,0:T(8,128)(2,1)} %get-tuple-element.29.x1_ref) | copy-start | bytes 12582916
  49.1 34.3 %copy-start.1 = (bf16[1024,2048]{1,0:T(8,128)(2,1)S(1)}, bf16[1024,2048]{1,0:T(8,128)(2,1)}, u32[]{:S(2)}) copy-start(bf16[1024,2048]{1,0:T(8,128)(2,1)} %get-tuple-element.30.g1_ref) | copy-start | bytes 12582916
  49.1 34.3 %copy-start.4 = (s32[2]{0:T(128)S(1)}, s32[2]{0:T(128)}, u32[]{:S(2)}) copy-start(s32[2]{0:T(128)} %pad_add_fusion.place_ref) | copy-start | bytes 28
  83.4 10.4 %slice-start = ((s8[8388608]{0:T(1024)(128)(4,1)}), s8[4194304]{0:T(1024)(128)(4,1)S(1)}, s32[]{:S(2)}) async-start(s8[8388608]{0:T(1024)(128)(4,1)} %bitcast.34), calls=%async_computation.2 | async-start | bytes 8388608
  85.3 4.2 %collective-permute-start.4 = (f32[4,128,256]{2,1,0:T(8,128)S(1)}, f32[4,128,256]{2,1,0:T(8,128)S(1)}, u32[]{:S(2)}, u32[]{:S(2)}) collective-permute-start(f32[4,128,256]{2,1,0:T(8,128)S(1)} %get-tuple-element.32), channel_id=1, source_target_pairs={{0,1},{1,0},{2,3},{3,2},{4,5},{5,4},{6,7},{7,6},{8,9},{9,8},{10,11... | collective-permute-start | bytes 1572872 | tf_op jit(solution)/shard_map/ppermute | solution.py:385
  87.7 6.2 %slice-start.1 = ((s8[8388608]{0:T(1024)(128)(4,1)}), s8[4194304]{0:T(1024)(128)(4,1)S(1)}, s32[]{:S(2)}) async-start(s8[8388608]{0:T(1024)(128)(4,1)} %bitcast.34), calls=%async_computation.3 | async-start | bytes 8388608
  87.7 6.2 %copy-start.2 = (bf16[1024,128]{1,0:T(8,128)(2,1)S(1)}, bf16[1024,128]{1,0:T(8,128)(2,1)}, u32[]{:S(2)}) copy-start(bf16[1024,128]{1,0:T(8,128)(2,1)} %refs_2_.1) | copy-start | bytes 786436
  87.7 6.2 %copy-start.3 = (bf16[1024,128]{1,0:T(8,128)(2,1)S(1)}, bf16[1024,128]{1,0:T(8,128)(2,1)}, u32[]{:S(2)}) copy-start(bf16[1024,128]{1,0:T(8,128)(2,1)} %get-tuple-element.26.refs_3_) | copy-start | bytes 786436
  89.6 7.6 %collective-permute-start.5 = (f32[128,256]{1,0:T(8,128)S(1)}, f32[128,256]{1,0:T(8,128)S(1)}, u32[]{:S(2)}, u32[]{:S(2)}) collective-permute-start(f32[128,256]{1,0:T(8,128)S(1)} %get-tuple-element.33), channel_id=1, source_target_pairs={{0,2},{1,3},{2,4},{3,5},{4,6},{5,7},{6,0},{7,1},{8,10},{9,11},{10,... | collective-permute-start | bytes 393224 | tf_op jit(solution)/shard_map/ppermute | solution.py:391
  90.6 8.5 %collective-permute-start.6 = (f32[128,256]{1,0:T(8,128)S(1)}, f32[128,256]{1,0:T(8,128)S(1)}, u32[]{:S(2)}, u32[]{:S(2)}) collective-permute-start(f32[128,256]{1,0:T(8,128)S(1)} %get-tuple-element.35), channel_id=1, source_target_pairs={{0,4},{1,5},{2,6},{3,7},{4,0},{5,1},{6,2},{7,3},{8,12},{9,13},{10,... | collective-permute-start | bytes 393224 | tf_op jit(solution)/shard_map/ppermute | solution.py:391
  92.8 6.4 %collective-permute-start.7 = (f32[128,256]{1,0:T(8,128)S(1)}, f32[128,256]{1,0:T(8,128)S(1)}, u32[]{:S(2)}, u32[]{:S(2)}) collective-permute-start(f32[128,256]{1,0:T(8,128)S(1)} %get-tuple-element.34), channel_id=1, source_target_pairs={{0,6},{1,7},{2,0},{3,1},{4,2},{5,3},{6,4},{7,5},{8,14},{9,15},{10,... | collective-permute-start | bytes 393224 | tf_op jit(solution)/shard_map/ppermute | solution.py:391

commit v8 on v7

--- a/solution.py
+++ b/solution.py
@@ -385,13 +385,13 @@
     return lax.ppermute(other, "head", [(i, i ^ 1) for i in range(ranks)])
 
 
-def over_chips(terms, start):
+def over_chips(terms):
     ranks = lax.axis_size("head")
     arrived = [
         lax.ppermute(terms[d], "head", [(i, (i + 2 * d) % ranks) for i in range(ranks)])
         for d in range(1, terms.shape[0])
     ]
-    return sum(arrived, start + terms[0])
+    return sum(arrived, terms[0])
 
 
 def body(scaled_input, out_grad, write_proj, read_proj, log_decay):
@@ -405,13 +405,13 @@
     gi, other, mine, x1, g1, fx = local_gradients(
         place, scaled_input, out_grad, write_proj, read_proj, log_decay
     )
-    local = over_chips(mine + over_cores(other), 0.0)
+    local = mine + over_cores(other)
     every, place, local, gi, x1, g1, fx = lax.optimization_barrier((every, place, local, gi, x1, g1, fx))
     own = lax.all_to_all(scan_shards(every), "seq", 0, 0, tiled=True)
     other, states = meet(meet_other_kernel, place, x1, g1, own, True)
     arrived = over_cores(other)
     (mine,) = meet(meet_mine_kernel, place, x1, g1, states, False)
-    shared = over_chips(mine + arrived, local)
+    shared = over_chips(mine + arrived + local)
     grad_input = finish(gi, own, write_proj, fx, heads)
     return grad_input, shared[:, :state].astype(BF16), shared[:, state:].astype(BF16)
 

time: 100 us -> 96.7 us (0.967)
  starting transfers between devices: 21.2 us -> 17.2 us
  waiting for transfers between devices: 8.64 us -> 12.5 us
  blocking collectives: 34.1 us -> 30.9 us
    all_to_all x1, waiting for transfers between devices: 0.01 us -> 8.77 us  [body(): lax.all_to_all(summarise(scaled_input, out_grad, write_proj, read_proj, l...]
    ppermute x6 -> x3, waiting for transfers between devices: 6.89 us -> 1.93 us  [over_chips(): lax.ppermute(terms[d], 'head', [(i, (i + 2 * d) % ranks) for i in range(r...]
    ppermute x6 -> x3, starting transfers between devices: 9.32 us -> 5.08 us  [over_chips(): lax.ppermute(terms[d], 'head', [(i, (i + 2 * d) % ranks) for i in range(r...]
    all_to_all x1, blocking collectives: 34.1 us -> 30.9 us  [body(): own = lax.all_to_all(scan_shards(every), 'seq', 0, 0, tiled=True)]
  transfers between devices with their start and end apart: 9 -> 6, of which waited for: 4 -> 3; matrix products, arithmetic and copies ran while one was open for 2% -> 2% of each run, Pallas kernels for 24% -> 24%
where the time goes in v8:
time: 96.7 us; the launch traced here: 96.5 us
  Pallas kernels  32.5 us (34%)
  blocking collectives  30.9 us (32%)
  starting transfers between devices  17.2 us (18%)
  waiting for transfers between devices  12.5 us (13%)
  other arithmetic  1.91 us (2%)
    all_to_all x1, blocking collectives, body(): own = lax.all_to_all(scan_shards(every), 'seq', 0, 0, tiled=True)  30.9 us
    pallas_call x1, Pallas kernels, local_gradients(): pl.pallas_call(local_kernel, grid=(width // WIDE,), in_specs=[pl.BlockSpe...  18.4 us
    all_to_all x1, waiting for transfers between devices, body(): lax.all_to_all(summarise(scaled_input, out_grad, write_proj, read_proj, l...  8.77 us
    all_to_all x1, starting transfers between devices, body(): lax.all_to_all(summarise(scaled_input, out_grad, write_proj, read_proj, l...  8.44 us
    pallas_call x1, Pallas kernels, summarise(): pl.pallas_call(summary_kernel, in_specs=[there] * 5, out_specs=there, out...  6.98 us
    ppermute x3, starting transfers between devices, over_chips(): lax.ppermute(terms[d], 'head', [(i, (i + 2 * d) % ranks) for i in range(r...  5.08 us
    ppermute x2, starting transfers between devices, over_cores(): return lax.ppermute(other, 'head', [(i, i ^ 1) for i in range(ranks)])  3.71 us
    pallas_call x2, Pallas kernels, meet(): pl.pallas_call(kernel, in_specs=[pl.BlockSpec(memory_space=pltpu.SMEM)] +...  3.61 us
  transfers between devices with their start and end apart: 6, of which 3 were waited for; matrix products, arithmetic and copies ran while one was open for 2% of the time, Pallas kernels for 24%

profile of v8, /device:TPU:1, one launch (start us, length us, event | category | flops | bytes accessed | tf_op | source)
XLA Modules:
  0.0 96.5 jit_solution(1599117885985471735)
XLA Ops:
  0.6 7.0 %summary.1 = f32[16,264,128]{2,1,0:T(8,128)} custom-call(bf16[1024,2048]{1,0:T(8,128)(2,1)} %x_ref.1, bf16[1024,2048]{1,0:T(8,128)(2,1)} %g_ref.1, bf16[1024,128]{1,0:T(8,128)(2,1)} %refs_2_.1, bf16[1024,128]{1,0:T(8,128)(2,1)} %r_ref.1, f32[32,1024]{1,0:T(8,128)} %ld_ref.1), custom_call_target="tpu_custom_call" | custom-call | tf_op jit(solution)/shard_map/summary/pallas_call | solution.py:272
  7.6 8.4 %all-to-all-start = ((f32[16,264,128]{2,1,0:T(8,128)}), f32[16,264,128]{2,1,0:T(8,128)S(1)}, u32[]{:S(2)}, u32[]{:S(2)}) async-start(f32[16,264,128]{2,1,0:T(8,128)} %summary.1), calls=%async_computation | async-start | bytes 4325376 | tf_op jit(solution)/shard_map/all_to_all | solution.py:402
  16.1 0.7 pad_add_fusion.place_ref
  16.7 18.4 %local.1 = (f32[1024,2048]{1,0:T(8,128)}, f32[4,128,256]{2,1,0:T(8,128)}, f32[4,128,256]{2,1,0:T(8,128)}, bf16[1024,2048]{1,0:T(8,128)(2,1)}, bf16[1024,2048]{1,0:T(8,128)(2,1)}, /*index=5*/bf16[1024,128]{1,0:T(8,128)(2,1)}) custom-call(s32[2]{0:T(128)} %pad_add_fusion.place_ref, bf16[1024,2048]{1,0:T(8,128)(2,1)} %x_ref.1, bf16[1024,2048]{1,0:T(8,128)(2,1)} %g_ref.1, ...), custom_call_target="tpu_custom_call" | custom-call | flops 10000000000 | bytes 26000000 | tf_op jit(solution)/shard_map/local/pallas_call | solution.py:312
  35.1 1.0 %collective-permute-start = (f32[4,128,256]{2,1,0:T(8,128)}, f32[4,128,256]{2,1,0:T(8,128)S(1)}, u32[]{:S(2)}, u32[]{:S(2)}) collective-permute-start(f32[4,128,256]{2,1,0:T(8,128)} %get-tuple-element.19), channel_id=1, source_target_pairs={{0,1},{1,0},{2,3},{3,2},{4,5},{5,4},{6,7},{7,6},{8,9},{9,8},{10,11... | collective-permute-start | bytes 1572872 | tf_op jit(solution)/shard_map/ppermute | solution.py:385
  36.2 1.7 %collective-permute-done = f32[4,128,256]{2,1,0:T(8,128)S(1)} collective-permute-done((f32[4,128,256]{2,1,0:T(8,128)}, f32[4,128,256]{2,1,0:T(8,128)S(1)}, u32[]{:S(2)}, u32[]{:S(2)}) %collective-permute-start) | collective-permute-done | bytes 524320 | tf_op jit(solution)/shard_map/ppermute | solution.py:385
  37.9 1.1 %add.24 = f32[4,128,256]{2,1,0:T(8,128)S(1)} add(f32[4,128,256]{2,1,0:T(8,128)} %get-tuple-element.18, f32[4,128,256]{2,1,0:T(8,128)S(1)} %collective-permute-done) | non-fusion elementwise | flops 131072 | bytes 1572864 | tf_op jit(solution)/shard_map/add | solution.py:408
  39.0 8.8 %all-to-all-done.in_ref = f32[16,264,128]{2,1,0:T(8,128)S(1)} async-done(((f32[16,264,128]{2,1,0:T(8,128)}), f32[16,264,128]{2,1,0:T(8,128)S(1)}, u32[]{:S(2)}, u32[]{:S(2)}) %all-to-all-start) | async-done | bytes 2162720 | tf_op jit(solution)/shard_map/all_to_all | solution.py:402
  47.8 0.0 copy-start
  47.8 0.2 scan.1
  48.0 30.9 %all_to_all.10.refs_1_.st_ref = f32[16,256,128]{2,1,0:T(8,128)S(1)} all-to-all(f32[16,256,128]{2,1,0:T(8,128)S(1)} %scan.1), channel_id=1, replica_groups=mesh['seq'=16,'head'=8] {'seq'}, dimensions={0} | all-to-all | bytes 4194304 | tf_op jit(solution)/shard_map/all_to_all | solution.py:410
  78.9 0.0 copy-done
  78.9 0.0 copy-done.1
  78.9 0.0 copy-done.4
  78.9 0.0 slice-start
  78.9 1.8 %meet_other.1 = (f32[4,128,256]{2,1,0:T(8,128)S(1)}, bf16[256,2048]{1,0:T(8,128)(2,1)S(1)}) custom-call(s32[2]{0:T(128)S(1)} %copy-done.4, bf16[1024,2048]{1,0:T(8,128)(2,1)S(1)} %copy-done, bf16[1024,2048]{1,0:T(8,128)(2,1)S(1)} %copy-done.1, f32[16,256,128]{2,1,0:T(8,128)S(1)} %all_to_all.10.refs_1_.st_ref), custom_call_target="tpu_custom_call" | custom-call | flops 1000000000 | bytes 4000000 | tf_op jit(solution)/shard_map/meet_other/pallas_call | solution.py:350
  80.8 2.7 %collective-permute-start.1 = (f32[4,128,256]{2,1,0:T(8,128)S(1)}, f32[4,128,256]{2,1,0:T(8,128)S(1)}, u32[]{:S(2)}, u32[]{:S(2)}) collective-permute-start(f32[4,128,256]{2,1,0:T(8,128)S(1)} %get-tuple-element.31), channel_id=1, source_target_pairs={{0,1},{1,0},{2,3},{3,2},{4,5},{5,4},{6,7},{7,6},{8,9},{9,8},{10,11... | collective-permute-start | bytes 1572872 | tf_op jit(solution)/shard_map/ppermute | solution.py:385
  83.5 1.8 %meet_mine.1 = f32[4,128,256]{2,1,0:T(8,128)S(1)} custom-call(s32[2]{0:T(128)S(1)} %copy-done.4, bf16[1024,2048]{1,0:T(8,128)(2,1)S(1)} %copy-done, bf16[1024,2048]{1,0:T(8,128)(2,1)S(1)} %copy-done.1, bf16[256,2048]{1,0:T(8,128)(2,1)S(1)} %get-tuple-element.30.states), custom_call_target="tpu_custom_call" | custom-call | flops 1000000000 | bytes 4000000 | tf_op jit(solution)/shard_map/meet_mine/pallas_call | solution.py:350
  85.2 0.0 collective-permute-done.1
  85.3 0.1 add_add_fusion
  85.4 1.4 %collective-permute-start.2 = (f32[128,256]{1,0:T(8,128)S(1)}, f32[128,256]{1,0:T(8,128)S(1)}, u32[]{:S(2)}, u32[]{:S(2)}) collective-permute-start(f32[128,256]{1,0:T(8,128)S(1)} %get-tuple-element.33), channel_id=1, source_target_pairs={{0,2},{1,3},{2,4},{3,5},{4,6},{5,7},{6,0},{7,1},{8,10},{9,11},{10,... | collective-permute-start | bytes 393224 | tf_op jit(solution)/shard_map/ppermute | solution.py:391
  86.8 2.6 %collective-permute-start.3 = (f32[128,256]{1,0:T(8,128)S(1)}, f32[128,256]{1,0:T(8,128)S(1)}, u32[]{:S(2)}, u32[]{:S(2)}) collective-permute-start(f32[128,256]{1,0:T(8,128)S(1)} %get-tuple-element.35), channel_id=1, source_target_pairs={{0,4},{1,5},{2,6},{3,7},{4,0},{5,1},{6,2},{7,3},{8,12},{9,13},{10,... | collective-permute-start | bytes 393224 | tf_op jit(solution)/shard_map/ppermute | solution.py:391
  89.4 1.1 %collective-permute-start.4 = (f32[128,256]{1,0:T(8,128)S(1)}, f32[128,256]{1,0:T(8,128)S(1)}, u32[]{:S(2)}, u32[]{:S(2)}) collective-permute-start(f32[128,256]{1,0:T(8,128)S(1)} %get-tuple-element.34), channel_id=1, source_target_pairs={{0,6},{1,7},{2,0},{3,1},{4,2},{5,3},{6,4},{7,5},{8,14},{9,15},{10,... | collective-permute-start | bytes 393224 | tf_op jit(solution)/shard_map/ppermute | solution.py:391
  90.5 0.0 slice-done
  90.5 0.0 slice-done.1
  90.5 0.0 copy-done.2
  90.5 0.0 copy-done.3
  90.5 3.3 %finish.1 = bf16[1024,2048]{1,0:T(8,128)(2,1)} custom-call(f32[1024,2048]{1,0:T(8,128)S(1)} %bitcast.19, f32[16,256,128]{2,1,0:T(8,128)S(1)} %all_to_all.10.refs_1_.st_ref, bf16[1024,128]{1,0:T(8,128)(2,1)S(1)} %copy-done.2, bf16[1024,128]{1,0:T(8,128)(2,1)S(1)} %copy-done.3), custom_call_target="tpu_custom_call" | custom-call | flops 2000000000 | bytes 13000000 | tf_op jit(solution)/shard_map/finish/pallas_call | solution.py:371
  93.9 0.0 collective-permute-done.2
  93.9 1.9 %collective-permute-done.3 = f32[128,256]{1,0:T(8,128)S(1)} collective-permute-done((f32[128,256]{1,0:T(8,128)S(1)}, f32[128,256]{1,0:T(8,128)S(1)}, u32[]{:S(2)}, u32[]{:S(2)}) %collective-permute-start.3) | collective-permute-done | bytes 131104 | tf_op jit(solution)/shard_map/ppermute | solution.py:391
  95.8 0.0 collective-permute-done.4
  95.8 0.6 fusion.4
  (8 shorter events, 0.1 us)
Async XLA Ops:
  7.6 40.2 %all-to-all-start = ((f32[16,264,128]{2,1,0:T(8,128)}), f32[16,264,128]{2,1,0:T(8,128)S(1)}, u32[]{:S(2)}, u32[]{:S(2)}) async-start(f32[16,264,128]{2,1,0:T(8,128)} %summary.1), calls=%async_computation | async-start | bytes 4325376 | tf_op jit(solution)/shard_map/all_to_all | solution.py:402
  35.1 2.8 %collective-permute-start = (f32[4,128,256]{2,1,0:T(8,128)}, f32[4,128,256]{2,1,0:T(8,128)S(1)}, u32[]{:S(2)}, u32[]{:S(2)}) collective-permute-start(f32[4,128,256]{2,1,0:T(8,128)} %get-tuple-element.19), channel_id=1, source_target_pairs={{0,1},{1,0},{2,3},{3,2},{4,5},{5,4},{6,7},{7,6},{8,9},{9,8},{10,11... | collective-permute-start | bytes 1572872 | tf_op jit(solution)/shard_map/ppermute | solution.py:385
  47.8 31.1 %copy-start = (bf16[1024,2048]{1,0:T(8,128)(2,1)S(1)}, bf16[1024,2048]{1,0:T(8,128)(2,1)}, u32[]{:S(2)}) copy-start(bf16[1024,2048]{1,0:T(8,128)(2,1)} %get-tuple-element.28.x1_ref) | copy-start | bytes 12582916
  47.8 31.1 %copy-start.1 = (bf16[1024,2048]{1,0:T(8,128)(2,1)S(1)}, bf16[1024,2048]{1,0:T(8,128)(2,1)}, u32[]{:S(2)}) copy-start(bf16[1024,2048]{1,0:T(8,128)(2,1)} %get-tuple-element.29.g1_ref) | copy-start | bytes 12582916
  47.8 31.1 %copy-start.4 = (s32[2]{0:T(128)S(1)}, s32[2]{0:T(128)}, u32[]{:S(2)}) copy-start(s32[2]{0:T(128)} %pad_add_fusion.place_ref) | copy-start | bytes 28
  78.9 11.6 %slice-start = ((s8[8388608]{0:T(1024)(128)(4,1)}), s8[4194304]{0:T(1024)(128)(4,1)S(1)}, s32[]{:S(2)}) async-start(s8[8388608]{0:T(1024)(128)(4,1)} %bitcast.18), calls=%async_computation.2 | async-start | bytes 8388608
  80.8 4.5 %collective-permute-start.1 = (f32[4,128,256]{2,1,0:T(8,128)S(1)}, f32[4,128,256]{2,1,0:T(8,128)S(1)}, u32[]{:S(2)}, u32[]{:S(2)}) collective-permute-start(f32[4,128,256]{2,1,0:T(8,128)S(1)} %get-tuple-element.31), channel_id=1, source_target_pairs={{0,1},{1,0},{2,3},{3,2},{4,5},{5,4},{6,7},{7,6},{8,9},{9,8},{10,11... | collective-permute-start | bytes 1572872 | tf_op jit(solution)/shard_map/ppermute | solution.py:385
  83.4 7.0 %slice-start.1 = ((s8[8388608]{0:T(1024)(128)(4,1)}), s8[4194304]{0:T(1024)(128)(4,1)S(1)}, s32[]{:S(2)}) async-start(s8[8388608]{0:T(1024)(128)(4,1)} %bitcast.18), calls=%async_computation.3 | async-start | bytes 8388608
  83.5 7.0 %copy-start.2 = (bf16[1024,128]{1,0:T(8,128)(2,1)S(1)}, bf16[1024,128]{1,0:T(8,128)(2,1)}, u32[]{:S(2)}) copy-start(bf16[1024,128]{1,0:T(8,128)(2,1)} %refs_2_.1) | copy-start | bytes 786436
  83.5 7.0 %copy-start.3 = (bf16[1024,128]{1,0:T(8,128)(2,1)S(1)}, bf16[1024,128]{1,0:T(8,128)(2,1)}, u32[]{:S(2)}) copy-start(bf16[1024,128]{1,0:T(8,128)(2,1)} %get-tuple-element.26.refs_3_) | copy-start | bytes 786436
  85.4 8.5 %collective-permute-start.2 = (f32[128,256]{1,0:T(8,128)S(1)}, f32[128,256]{1,0:T(8,128)S(1)}, u32[]{:S(2)}, u32[]{:S(2)}) collective-permute-start(f32[128,256]{1,0:T(8,128)S(1)} %get-tuple-element.33), channel_id=1, source_target_pairs={{0,2},{1,3},{2,4},{3,5},{4,6},{5,7},{6,0},{7,1},{8,10},{9,11},{10,... | collective-permute-start | bytes 393224 | tf_op jit(solution)/shard_map/ppermute | solution.py:391
  86.8 9.0 %collective-permute-start.3 = (f32[128,256]{1,0:T(8,128)S(1)}, f32[128,256]{1,0:T(8,128)S(1)}, u32[]{:S(2)}, u32[]{:S(2)}) collective-permute-start(f32[128,256]{1,0:T(8,128)S(1)} %get-tuple-element.35), channel_id=1, source_target_pairs={{0,4},{1,5},{2,6},{3,7},{4,0},{5,1},{6,2},{7,3},{8,12},{9,13},{10,... | collective-permute-start | bytes 393224 | tf_op jit(solution)/shard_map/ppermute | solution.py:391
  89.4 6.4 %collective-permute-start.4 = (f32[128,256]{1,0:T(8,128)S(1)}, f32[128,256]{1,0:T(8,128)S(1)}, u32[]{:S(2)}, u32[]{:S(2)}) collective-permute-start(f32[128,256]{1,0:T(8,128)S(1)} %get-tuple-element.34), channel_id=1, source_target_pairs={{0,6},{1,7},{2,0},{3,1},{4,2},{5,3},{6,4},{7,5},{8,14},{9,15},{10,... | collective-permute-start | bytes 393224 | tf_op jit(solution)/shard_map/ppermute | solution.py:391

commit v9 on v8

--- a/solution.py
+++ b/solution.py
@@ -387,11 +387,10 @@
 
 def over_chips(terms):
     ranks = lax.axis_size("head")
-    arrived = [
-        lax.ppermute(terms[d], "head", [(i, (i + 2 * d) % ranks) for i in range(ranks)])
-        for d in range(1, terms.shape[0])
-    ]
-    return sum(arrived, terms[0])
+    total = [terms[0]]
+    for d in sorted(range(1, terms.shape[0]), key=lambda d: -min(d, terms.shape[0] - d)):
+        total.append(lax.ppermute(terms[d], "head", [(i, (i + 2 * d) % ranks) for i in range(ranks)]))
+    return total
 
 
 def body(scaled_input, out_grad, write_proj, read_proj, log_decay):
@@ -413,7 +412,9 @@
     (mine,) = meet(meet_mine_kernel, place, x1, g1, states, False)
     shared = over_chips(mine + arrived + local)
     grad_input = finish(gi, own, write_proj, fx, heads)
-    return grad_input, shared[:, :state].astype(BF16), shared[:, state:].astype(BF16)
+    grad_write = sum(part[:, :state] for part in shared).astype(BF16)
+    grad_read = sum(part[:, state:] for part in shared).astype(BF16)
+    return grad_input, grad_write, grad_read
 
 
 def solution(mesh):

time: 96.7 us -> 96.1 us (level)
  waiting for transfers between devices: 12.5 us -> 11.2 us
    ppermute x3, waiting for transfers between devices: 1.93 us -> 0.72 us  [over_chips(): lax.ppermute(terms[d], 'head', [(i, (i + 2 * d) % ranks) for i in range(r...]
  transfers between devices with their start and end apart: 6 -> 6, of which waited for: 3 -> 4; matrix products, arithmetic and copies ran while one was open for 2% -> 2% of each run, Pallas kernels for 24% -> 25%
where the time goes in v9:
time: 96.1 us; the launch traced here: 95.9 us
  Pallas kernels  32.5 us (34%)
  blocking collectives  30.9 us (32%)
  starting transfers between devices  17.8 us (19%)
  waiting for transfers between devices  11.2 us (12%)
  other arithmetic  2.52 us (3%)
    all_to_all x1, blocking collectives, body(): own = lax.all_to_all(scan_shards(every), 'seq', 0, 0, tiled=True)  30.9 us
    pallas_call x1, Pallas kernels, local_gradients(): pl.pallas_call(local_kernel, grid=(width // WIDE,), in_specs=[pl.BlockSpe...  18.4 us
    all_to_all x1, waiting for transfers between devices, body(): lax.all_to_all(summarise(scaled_input, out_grad, write_proj, read_proj, l...  8.77 us
    all_to_all x1, starting transfers between devices, body(): lax.all_to_all(summarise(scaled_input, out_grad, write_proj, read_proj, l...  8.44 us
    pallas_call x1, Pallas kernels, summarise(): pl.pallas_call(summary_kernel, in_specs=[there] * 5, out_specs=there, out...  6.98 us
    ppermute x3, starting transfers between devices, over_chips(): lax.ppermute(terms[d], 'head', [(i, (i + 2 * d) % ranks) for i in range(r...  5.69 us
    ppermute x2, starting transfers between devices, over_cores(): return lax.ppermute(other, 'head', [(i, i ^ 1) for i in range(ranks)])  3.71 us
    pallas_call x2, Pallas kernels, meet(): pl.pallas_call(kernel, in_specs=[pl.BlockSpec(memory_space=pltpu.SMEM)] +...  3.61 us
  transfers between devices with their start and end apart: 6, of which 4 were waited for; matrix products, arithmetic and copies ran while one was open for 2% of the time, Pallas kernels for 25%

profile of v9, /device:TPU:1, one launch (start us, length us, event | category | flops | bytes accessed | tf_op | source)
XLA Modules:
  0.0 95.9 jit_solution(12901250876458983422)
XLA Ops:
  0.6 7.0 %summary.1 = f32[16,264,128]{2,1,0:T(8,128)} custom-call(bf16[1024,2048]{1,0:T(8,128)(2,1)} %x_ref.1, bf16[1024,2048]{1,0:T(8,128)(2,1)} %g_ref.1, bf16[1024,128]{1,0:T(8,128)(2,1)} %refs_2_.1, bf16[1024,128]{1,0:T(8,128)(2,1)} %r_ref.1, f32[32,1024]{1,0:T(8,128)} %ld_ref.1), custom_call_target="tpu_custom_call" | custom-call | tf_op jit(solution)/shard_map/summary/pallas_call | solution.py:272
  7.6 8.4 %all-to-all-start = ((f32[16,264,128]{2,1,0:T(8,128)}), f32[16,264,128]{2,1,0:T(8,128)S(1)}, u32[]{:S(2)}, u32[]{:S(2)}) async-start(f32[16,264,128]{2,1,0:T(8,128)} %summary.1), calls=%async_computation | async-start | bytes 4325376 | tf_op jit(solution)/shard_map/all_to_all | solution.py:401
  16.1 0.7 pad_add_fusion.place_ref
  16.7 18.4 %local.1 = (f32[1024,2048]{1,0:T(8,128)}, f32[4,128,256]{2,1,0:T(8,128)}, f32[4,128,256]{2,1,0:T(8,128)}, bf16[1024,2048]{1,0:T(8,128)(2,1)}, bf16[1024,2048]{1,0:T(8,128)(2,1)}, /*index=5*/bf16[1024,128]{1,0:T(8,128)(2,1)}) custom-call(s32[2]{0:T(128)} %pad_add_fusion.place_ref, bf16[1024,2048]{1,0:T(8,128)(2,1)} %x_ref.1, bf16[1024,2048]{1,0:T(8,128)(2,1)} %g_ref.1, ...), custom_call_target="tpu_custom_call" | custom-call | flops 10000000000 | bytes 26000000 | tf_op jit(solution)/shard_map/local/pallas_call | solution.py:312
  35.1 1.0 %collective-permute-start = (f32[4,128,256]{2,1,0:T(8,128)}, f32[4,128,256]{2,1,0:T(8,128)S(1)}, u32[]{:S(2)}, u32[]{:S(2)}) collective-permute-start(f32[4,128,256]{2,1,0:T(8,128)} %get-tuple-element.19), channel_id=1, source_target_pairs={{0,1},{1,0},{2,3},{3,2},{4,5},{5,4},{6,7},{7,6},{8,9},{9,8},{10,11... | collective-permute-start | bytes 1572872 | tf_op jit(solution)/shard_map/ppermute | solution.py:385
  36.2 1.7 %collective-permute-done = f32[4,128,256]{2,1,0:T(8,128)S(1)} collective-permute-done((f32[4,128,256]{2,1,0:T(8,128)}, f32[4,128,256]{2,1,0:T(8,128)S(1)}, u32[]{:S(2)}, u32[]{:S(2)}) %collective-permute-start) | collective-permute-done | bytes 524320 | tf_op jit(solution)/shard_map/ppermute | solution.py:385
  37.9 1.1 %add.33 = f32[4,128,256]{2,1,0:T(8,128)S(1)} add(f32[4,128,256]{2,1,0:T(8,128)} %get-tuple-element.18, f32[4,128,256]{2,1,0:T(8,128)S(1)} %collective-permute-done) | non-fusion elementwise | flops 131072 | bytes 1572864 | tf_op jit(solution)/shard_map/add | solution.py:407
  39.0 8.8 %all-to-all-done.in_ref = f32[16,264,128]{2,1,0:T(8,128)S(1)} async-done(((f32[16,264,128]{2,1,0:T(8,128)}), f32[16,264,128]{2,1,0:T(8,128)S(1)}, u32[]{:S(2)}, u32[]{:S(2)}) %all-to-all-start) | async-done | bytes 2162720 | tf_op jit(solution)/shard_map/all_to_all | solution.py:401
  47.8 0.0 copy-start
  47.8 0.2 scan.1
  48.0 30.9 %all_to_all.10.refs_1_.st_ref = f32[16,256,128]{2,1,0:T(8,128)S(1)} all-to-all(f32[16,256,128]{2,1,0:T(8,128)S(1)} %scan.1), channel_id=1, replica_groups=mesh['seq'=16,'head'=8] {'seq'}, dimensions={0} | all-to-all | bytes 4194304 | tf_op jit(solution)/shard_map/all_to_all | solution.py:409
  78.9 0.0 copy-done
  78.9 0.0 copy-done.1
  78.9 0.0 copy-done.4
  78.9 0.0 slice-start
  78.9 1.8 %meet_other.1 = (f32[4,128,256]{2,1,0:T(8,128)S(1)}, bf16[256,2048]{1,0:T(8,128)(2,1)S(1)}) custom-call(s32[2]{0:T(128)S(1)} %copy-done.4, bf16[1024,2048]{1,0:T(8,128)(2,1)S(1)} %copy-done, bf16[1024,2048]{1,0:T(8,128)(2,1)S(1)} %copy-done.1, f32[16,256,128]{2,1,0:T(8,128)S(1)} %all_to_all.10.refs_1_.st_ref), custom_call_target="tpu_custom_call" | custom-call | flops 1000000000 | bytes 4000000 | tf_op jit(solution)/shard_map/meet_other/pallas_call | solution.py:350
  80.8 2.7 %collective-permute-start.1 = (f32[4,128,256]{2,1,0:T(8,128)S(1)}, f32[4,128,256]{2,1,0:T(8,128)S(1)}, u32[]{:S(2)}, u32[]{:S(2)}) collective-permute-start(f32[4,128,256]{2,1,0:T(8,128)S(1)} %get-tuple-element.31), channel_id=1, source_target_pairs={{0,1},{1,0},{2,3},{3,2},{4,5},{5,4},{6,7},{7,6},{8,9},{9,8},{10,11... | collective-permute-start | bytes 1572872 | tf_op jit(solution)/shard_map/ppermute | solution.py:385
  83.5 1.8 %meet_mine.1 = f32[4,128,256]{2,1,0:T(8,128)S(1)} custom-call(s32[2]{0:T(128)S(1)} %copy-done.4, bf16[1024,2048]{1,0:T(8,128)(2,1)S(1)} %copy-done, bf16[1024,2048]{1,0:T(8,128)(2,1)S(1)} %copy-done.1, bf16[256,2048]{1,0:T(8,128)(2,1)S(1)} %get-tuple-element.30.states), custom_call_target="tpu_custom_call" | custom-call | flops 1000000000 | bytes 4000000 | tf_op jit(solution)/shard_map/meet_mine/pallas_call | solution.py:350
  85.2 0.0 collective-permute-done.1
  85.3 0.1 add_add_fusion
  85.4 3.0 %collective-permute-start.2 = (f32[128,256]{1,0:T(8,128)S(1)}, f32[128,256]{1,0:T(8,128)S(1)}, u32[]{:S(2)}, u32[]{:S(2)}) collective-permute-start(f32[128,256]{1,0:T(8,128)S(1)} %get-tuple-element.38), channel_id=1, source_target_pairs={{0,4},{1,5},{2,6},{3,7},{4,0},{5,1},{6,2},{7,3},{8,12},{9,13},{10,... | collective-permute-start | bytes 393224 | tf_op jit(solution)/shard_map/ppermute | solution.py:392
  88.4 0.4 collective-permute-start.3
  88.8 2.3 %collective-permute-start.4 = (f32[128,256]{1,0:T(8,128)S(1)}, f32[128,256]{1,0:T(8,128)S(1)}, u32[]{:S(2)}, u32[]{:S(2)}) collective-permute-start(f32[128,256]{1,0:T(8,128)S(1)} %get-tuple-element.36), channel_id=1, source_target_pairs={{0,6},{1,7},{2,0},{3,1},{4,2},{5,3},{6,4},{7,5},{8,14},{9,15},{10,... | collective-permute-start | bytes 393224 | tf_op jit(solution)/shard_map/ppermute | solution.py:392
  91.1 0.0 slice-done
  91.1 0.0 slice-done.1
  91.1 0.0 copy-done.2
  91.1 0.0 copy-done.3
  91.1 3.3 %finish.1 = bf16[1024,2048]{1,0:T(8,128)(2,1)} custom-call(f32[1024,2048]{1,0:T(8,128)S(1)} %bitcast.11, f32[16,256,128]{2,1,0:T(8,128)S(1)} %all_to_all.10.refs_1_.st_ref, bf16[1024,128]{1,0:T(8,128)(2,1)S(1)} %copy-done.2, bf16[1024,128]{1,0:T(8,128)(2,1)S(1)} %copy-done.3), custom_call_target="tpu_custom_call" | custom-call | flops 2000000000 | bytes 13000000 | tf_op jit(solution)/shard_map/finish/pallas_call | solution.py:371
  94.5 0.0 collective-permute-done.2
  94.5 0.5 collective-permute-done.3
  95.0 0.2 collective-permute-done.4
  95.2 0.7 fusion
  (7 shorter events, 0.0 us)
Async XLA Ops:
  7.6 40.2 %all-to-all-start = ((f32[16,264,128]{2,1,0:T(8,128)}), f32[16,264,128]{2,1,0:T(8,128)S(1)}, u32[]{:S(2)}, u32[]{:S(2)}) async-start(f32[16,264,128]{2,1,0:T(8,128)} %summary.1), calls=%async_computation | async-start | bytes 4325376 | tf_op jit(solution)/shard_map/all_to_all | solution.py:401
  35.1 2.8 %collective-permute-start = (f32[4,128,256]{2,1,0:T(8,128)}, f32[4,128,256]{2,1,0:T(8,128)S(1)}, u32[]{:S(2)}, u32[]{:S(2)}) collective-permute-start(f32[4,128,256]{2,1,0:T(8,128)} %get-tuple-element.19), channel_id=1, source_target_pairs={{0,1},{1,0},{2,3},{3,2},{4,5},{5,4},{6,7},{7,6},{8,9},{9,8},{10,11... | collective-permute-start | bytes 1572872 | tf_op jit(solution)/shard_map/ppermute | solution.py:385
  47.8 31.1 %copy-start = (bf16[1024,2048]{1,0:T(8,128)(2,1)S(1)}, bf16[1024,2048]{1,0:T(8,128)(2,1)}, u32[]{:S(2)}) copy-start(bf16[1024,2048]{1,0:T(8,128)(2,1)} %get-tuple-element.28.x1_ref) | copy-start | bytes 12582916
  47.8 31.1 %copy-start.1 = (bf16[1024,2048]{1,0:T(8,128)(2,1)S(1)}, bf16[1024,2048]{1,0:T(8,128)(2,1)}, u32[]{:S(2)}) copy-start(bf16[1024,2048]{1,0:T(8,128)(2,1)} %get-tuple-element.29.g1_ref) | copy-start | bytes 12582916
  47.8 31.1 %copy-start.4 = (s32[2]{0:T(128)S(1)}, s32[2]{0:T(128)}, u32[]{:S(2)}) copy-start(s32[2]{0:T(128)} %pad_add_fusion.place_ref) | copy-start | bytes 28
  78.9 12.2 %slice-start = ((s8[8388608]{0:T(1024)(128)(4,1)}), s8[4194304]{0:T(1024)(128)(4,1)S(1)}, s32[]{:S(2)}) async-start(s8[8388608]{0:T(1024)(128)(4,1)} %bitcast.10), calls=%async_computation.2 | async-start | bytes 8388608
  80.8 4.5 %collective-permute-start.1 = (f32[4,128,256]{2,1,0:T(8,128)S(1)}, f32[4,128,256]{2,1,0:T(8,128)S(1)}, u32[]{:S(2)}, u32[]{:S(2)}) collective-permute-start(f32[4,128,256]{2,1,0:T(8,128)S(1)} %get-tuple-element.31), channel_id=1, source_target_pairs={{0,1},{1,0},{2,3},{3,2},{4,5},{5,4},{6,7},{7,6},{8,9},{9,8},{10,11... | collective-permute-start | bytes 1572872 | tf_op jit(solution)/shard_map/ppermute | solution.py:385
  83.4 7.7 %slice-start.1 = ((s8[8388608]{0:T(1024)(128)(4,1)}), s8[4194304]{0:T(1024)(128)(4,1)S(1)}, s32[]{:S(2)}) async-start(s8[8388608]{0:T(1024)(128)(4,1)} %bitcast.10), calls=%async_computation.3 | async-start | bytes 8388608
  83.5 7.7 %copy-start.2 = (bf16[1024,128]{1,0:T(8,128)(2,1)S(1)}, bf16[1024,128]{1,0:T(8,128)(2,1)}, u32[]{:S(2)}) copy-start(bf16[1024,128]{1,0:T(8,128)(2,1)} %refs_2_.1) | copy-start | bytes 786436
  83.5 7.7 %copy-start.3 = (bf16[1024,128]{1,0:T(8,128)(2,1)S(1)}, bf16[1024,128]{1,0:T(8,128)(2,1)}, u32[]{:S(2)}) copy-start(bf16[1024,128]{1,0:T(8,128)(2,1)} %get-tuple-element.26.refs_3_) | copy-start | bytes 786436
  85.4 9.1 %collective-permute-start.2 = (f32[128,256]{1,0:T(8,128)S(1)}, f32[128,256]{1,0:T(8,128)S(1)}, u32[]{:S(2)}, u32[]{:S(2)}) collective-permute-start(f32[128,256]{1,0:T(8,128)S(1)} %get-tuple-element.38), channel_id=1, source_target_pairs={{0,4},{1,5},{2,6},{3,7},{4,0},{5,1},{6,2},{7,3},{8,12},{9,13},{10,... | collective-permute-start | bytes 393224 | tf_op jit(solution)/shard_map/ppermute | solution.py:392
  88.4 6.6 %collective-permute-start.3 = (f32[128,256]{1,0:T(8,128)S(1)}, f32[128,256]{1,0:T(8,128)S(1)}, u32[]{:S(2)}, u32[]{:S(2)}) collective-permute-start(f32[128,256]{1,0:T(8,128)S(1)} %get-tuple-element.37), channel_id=1, source_target_pairs={{0,2},{1,3},{2,4},{3,5},{4,6},{5,7},{6,0},{7,1},{8,10},{9,11},{10,... | collective-permute-start | bytes 393224 | tf_op jit(solution)/shard_map/ppermute | solution.py:392
  88.8 6.4 %collective-permute-start.4 = (f32[128,256]{1,0:T(8,128)S(1)}, f32[128,256]{1,0:T(8,128)S(1)}, u32[]{:S(2)}, u32[]{:S(2)}) collective-permute-start(f32[128,256]{1,0:T(8,128)S(1)} %get-tuple-element.36), channel_id=1, source_target_pairs={{0,6},{1,7},{2,0},{3,1},{4,2},{5,3},{6,4},{7,5},{8,14},{9,15},{10,... | collective-permute-start | bytes 393224 | tf_op jit(solution)/shard_map/ppermute | solution.py:392

commit v10 on v9

--- a/solution.py
+++ b/solution.py
@@ -201,9 +201,13 @@
             for slot in range(count // 2):
                 k = block_of(place_ref, slot, count // 2, core)
                 tok = pl.ds(pl.multiple_of(k * SUB, SUB), SUB)
-                weights = jnp.where(upper, acc[k, :SUB, :SUB], 0.0).astype(BF16)
-                out_ref[slot, :, :state] = dot(weights, r_ref[tok]) + acc[k, :SUB, SUB:]
-                out_ref[slot, :, state:] = (dot(wt[k], weights) + acc[k, SUB:, :SUB]).T
+                weights = jnp.where(upper, acc[k, :SUB, :SUB], 0.0)
+                high = weights.astype(BF16)
+                rest = (weights - high.astype(F32)).astype(BF16)
+                to_write = dot(high, r_ref[tok]) + dot(rest, r_ref[tok])
+                to_read = dot(wt[k], high) + dot(wt[k], rest)
+                out_ref[slot, :, :state] = to_write + acc[k, :SUB, SUB:]
+                out_ref[slot, :, state:] = (to_read + acc[k, SUB:, :SUB]).T
 
 
 def meet_half(place_ref, away, x1_ref, g1_ref, states, out_ref):

time: 96.1 us -> 96.1 us (level)
  no operation moved by 1% of the time
where the time goes in v10:
time: 96.1 us; the launch traced here: 95.9 us
  Pallas kernels  32.6 us (34%)
  blocking collectives  30.9 us (32%)
  starting transfers between devices  17.8 us (19%)
  waiting for transfers between devices  11.1 us (12%)
  other arithmetic  2.52 us (3%)
    all_to_all x1, blocking collectives, body(): own = lax.all_to_all(scan_shards(every), 'seq', 0, 0, tiled=True)  30.9 us
    pallas_call x1, Pallas kernels, local_gradients(): pl.pallas_call(local_kernel, grid=(width // WIDE,), in_specs=[pl.BlockSpe...  18.5 us
    all_to_all x1, waiting for transfers between devices, body(): lax.all_to_all(summarise(scaled_input, out_grad, write_proj, read_proj, l...  8.64 us
    all_to_all x1, starting transfers between devices, body(): lax.all_to_all(summarise(scaled_input, out_grad, write_proj, read_proj, l...  8.44 us
    pallas_call x1, Pallas kernels, summarise(): pl.pallas_call(summary_kernel, in_specs=[there] * 5, out_specs=there, out...  6.98 us
    ppermute x3, starting transfers between devices, over_chips(): lax.ppermute(terms[d], 'head', [(i, (i + 2 * d) % ranks) for i in range(r...  5.69 us
    ppermute x2, starting transfers between devices, over_cores(): return lax.ppermute(other, 'head', [(i, i ^ 1) for i in range(ranks)])  3.7 us
    pallas_call x2, Pallas kernels, meet(): pl.pallas_call(kernel, in_specs=[pl.BlockSpec(memory_space=pltpu.SMEM)] +...  3.61 us
  transfers between devices with their start and end apart: 6, of which 4 were waited for; matrix products, arithmetic and copies ran while one was open for 2% of the time, Pallas kernels for 25%

profile of v10, /device:TPU:1, one launch (start us, length us, event | category | flops | bytes accessed | tf_op | source)
XLA Modules:
  0.0 95.9 jit_solution(12346616907526676642)
XLA Ops:
  0.6 7.0 %summary.1 = f32[16,264,128]{2,1,0:T(8,128)} custom-call(bf16[1024,2048]{1,0:T(8,128)(2,1)} %x_ref.1, bf16[1024,2048]{1,0:T(8,128)(2,1)} %g_ref.1, bf16[1024,128]{1,0:T(8,128)(2,1)} %refs_2_.1, bf16[1024,128]{1,0:T(8,128)(2,1)} %r_ref.1, f32[32,1024]{1,0:T(8,128)} %ld_ref.1), custom_call_target="tpu_custom_call" | custom-call | tf_op jit(solution)/shard_map/summary/pallas_call | solution.py:276
  7.6 8.4 %all-to-all-start = ((f32[16,264,128]{2,1,0:T(8,128)}), f32[16,264,128]{2,1,0:T(8,128)S(1)}, u32[]{:S(2)}, u32[]{:S(2)}) async-start(f32[16,264,128]{2,1,0:T(8,128)} %summary.1), calls=%async_computation | async-start | bytes 4325376 | tf_op jit(solution)/shard_map/all_to_all | solution.py:405
  16.1 0.7 pad_add_fusion.place_ref
  16.7 18.5 %local.1 = (f32[1024,2048]{1,0:T(8,128)}, f32[4,128,256]{2,1,0:T(8,128)}, f32[4,128,256]{2,1,0:T(8,128)}, bf16[1024,2048]{1,0:T(8,128)(2,1)}, bf16[1024,2048]{1,0:T(8,128)(2,1)}, /*index=5*/bf16[1024,128]{1,0:T(8,128)(2,1)}) custom-call(s32[2]{0:T(128)} %pad_add_fusion.place_ref, bf16[1024,2048]{1,0:T(8,128)(2,1)} %x_ref.1, bf16[1024,2048]{1,0:T(8,128)(2,1)} %g_ref.1, ...), custom_call_target="tpu_custom_call" | custom-call | flops 10000000000 | bytes 26000000 | tf_op jit(solution)/shard_map/local/pallas_call | solution.py:316
  35.3 1.0 %collective-permute-start = (f32[4,128,256]{2,1,0:T(8,128)}, f32[4,128,256]{2,1,0:T(8,128)S(1)}, u32[]{:S(2)}, u32[]{:S(2)}) collective-permute-start(f32[4,128,256]{2,1,0:T(8,128)} %get-tuple-element.19), channel_id=1, source_target_pairs={{0,1},{1,0},{2,3},{3,2},{4,5},{5,4},{6,7},{7,6},{8,9},{9,8},{10,11... | collective-permute-start | bytes 1572872 | tf_op jit(solution)/shard_map/ppermute | solution.py:389
  36.3 1.7 %collective-permute-done = f32[4,128,256]{2,1,0:T(8,128)S(1)} collective-permute-done((f32[4,128,256]{2,1,0:T(8,128)}, f32[4,128,256]{2,1,0:T(8,128)S(1)}, u32[]{:S(2)}, u32[]{:S(2)}) %collective-permute-start) | collective-permute-done | bytes 524320 | tf_op jit(solution)/shard_map/ppermute | solution.py:389
  38.1 1.1 %add.33 = f32[4,128,256]{2,1,0:T(8,128)S(1)} add(f32[4,128,256]{2,1,0:T(8,128)} %get-tuple-element.18, f32[4,128,256]{2,1,0:T(8,128)S(1)} %collective-permute-done) | non-fusion elementwise | flops 131072 | bytes 1572864 | tf_op jit(solution)/shard_map/add | solution.py:411
  39.2 8.6 %all-to-all-done.in_ref = f32[16,264,128]{2,1,0:T(8,128)S(1)} async-done(((f32[16,264,128]{2,1,0:T(8,128)}), f32[16,264,128]{2,1,0:T(8,128)S(1)}, u32[]{:S(2)}, u32[]{:S(2)}) %all-to-all-start) | async-done | bytes 2162720 | tf_op jit(solution)/shard_map/all_to_all | solution.py:405
  47.8 0.0 copy-start
  47.8 0.2 scan.1
  48.0 30.9 %all_to_all.10.refs_1_.st_ref = f32[16,256,128]{2,1,0:T(8,128)S(1)} all-to-all(f32[16,256,128]{2,1,0:T(8,128)S(1)} %scan.1), channel_id=1, replica_groups=mesh['seq'=16,'head'=8] {'seq'}, dimensions={0} | all-to-all | bytes 4194304 | tf_op jit(solution)/shard_map/all_to_all | solution.py:413
  78.9 0.0 copy-done
  78.9 0.0 copy-done.1
  78.9 0.0 copy-done.4
  78.9 0.0 slice-start
  78.9 1.8 %meet_other.1 = (f32[4,128,256]{2,1,0:T(8,128)S(1)}, bf16[256,2048]{1,0:T(8,128)(2,1)S(1)}) custom-call(s32[2]{0:T(128)S(1)} %copy-done.4, bf16[1024,2048]{1,0:T(8,128)(2,1)S(1)} %copy-done, bf16[1024,2048]{1,0:T(8,128)(2,1)S(1)} %copy-done.1, f32[16,256,128]{2,1,0:T(8,128)S(1)} %all_to_all.10.refs_1_.st_ref), custom_call_target="tpu_custom_call" | custom-call | flops 1000000000 | bytes 4000000 | tf_op jit(solution)/shard_map/meet_other/pallas_call | solution.py:354
  80.8 2.7 %collective-permute-start.1 = (f32[4,128,256]{2,1,0:T(8,128)S(1)}, f32[4,128,256]{2,1,0:T(8,128)S(1)}, u32[]{:S(2)}, u32[]{:S(2)}) collective-permute-start(f32[4,128,256]{2,1,0:T(8,128)S(1)} %get-tuple-element.31), channel_id=1, source_target_pairs={{0,1},{1,0},{2,3},{3,2},{4,5},{5,4},{6,7},{7,6},{8,9},{9,8},{10,11... | collective-permute-start | bytes 1572872 | tf_op jit(solution)/shard_map/ppermute | solution.py:389
  83.5 1.8 %meet_mine.1 = f32[4,128,256]{2,1,0:T(8,128)S(1)} custom-call(s32[2]{0:T(128)S(1)} %copy-done.4, bf16[1024,2048]{1,0:T(8,128)(2,1)S(1)} %copy-done, bf16[1024,2048]{1,0:T(8,128)(2,1)S(1)} %copy-done.1, bf16[256,2048]{1,0:T(8,128)(2,1)S(1)} %get-tuple-element.30.states), custom_call_target="tpu_custom_call" | custom-call | flops 1000000000 | bytes 4000000 | tf_op jit(solution)/shard_map/meet_mine/pallas_call | solution.py:354
  85.2 0.0 collective-permute-done.1
  85.3 0.1 add_add_fusion
  85.4 3.0 %collective-permute-start.2 = (f32[128,256]{1,0:T(8,128)S(1)}, f32[128,256]{1,0:T(8,128)S(1)}, u32[]{:S(2)}, u32[]{:S(2)}) collective-permute-start(f32[128,256]{1,0:T(8,128)S(1)} %get-tuple-element.38), channel_id=1, source_target_pairs={{0,4},{1,5},{2,6},{3,7},{4,0},{5,1},{6,2},{7,3},{8,12},{9,13},{10,... | collective-permute-start | bytes 393224 | tf_op jit(solution)/shard_map/ppermute | solution.py:396
  88.4 0.4 collective-permute-start.3
  88.8 2.3 %collective-permute-start.4 = (f32[128,256]{1,0:T(8,128)S(1)}, f32[128,256]{1,0:T(8,128)S(1)}, u32[]{:S(2)}, u32[]{:S(2)}) collective-permute-start(f32[128,256]{1,0:T(8,128)S(1)} %get-tuple-element.36), channel_id=1, source_target_pairs={{0,6},{1,7},{2,0},{3,1},{4,2},{5,3},{6,4},{7,5},{8,14},{9,15},{10,... | collective-permute-start | bytes 393224 | tf_op jit(solution)/shard_map/ppermute | solution.py:396
  91.1 0.0 slice-done
  91.1 0.0 slice-done.1
  91.1 0.0 copy-done.2
  91.1 0.0 copy-done.3
  91.1 3.3 %finish.1 = bf16[1024,2048]{1,0:T(8,128)(2,1)} custom-call(f32[1024,2048]{1,0:T(8,128)S(1)} %bitcast.11, f32[16,256,128]{2,1,0:T(8,128)S(1)} %all_to_all.10.refs_1_.st_ref, bf16[1024,128]{1,0:T(8,128)(2,1)S(1)} %copy-done.2, bf16[1024,128]{1,0:T(8,128)(2,1)S(1)} %copy-done.3), custom_call_target="tpu_custom_call" | custom-call | flops 2000000000 | bytes 13000000 | tf_op jit(solution)/shard_map/finish/pallas_call | solution.py:375
  94.5 0.0 collective-permute-done.2
  94.5 0.5 collective-permute-done.3
  95.0 0.2 collective-permute-done.4
  95.2 0.7 fusion
  (7 shorter events, 0.0 us)
Async XLA Ops:
  7.6 40.2 %all-to-all-start = ((f32[16,264,128]{2,1,0:T(8,128)}), f32[16,264,128]{2,1,0:T(8,128)S(1)}, u32[]{:S(2)}, u32[]{:S(2)}) async-start(f32[16,264,128]{2,1,0:T(8,128)} %summary.1), calls=%async_computation | async-start | bytes 4325376 | tf_op jit(solution)/shard_map/all_to_all | solution.py:405
  35.3 2.8 %collective-permute-start = (f32[4,128,256]{2,1,0:T(8,128)}, f32[4,128,256]{2,1,0:T(8,128)S(1)}, u32[]{:S(2)}, u32[]{:S(2)}) collective-permute-start(f32[4,128,256]{2,1,0:T(8,128)} %get-tuple-element.19), channel_id=1, source_target_pairs={{0,1},{1,0},{2,3},{3,2},{4,5},{5,4},{6,7},{7,6},{8,9},{9,8},{10,11... | collective-permute-start | bytes 1572872 | tf_op jit(solution)/shard_map/ppermute | solution.py:389
  47.8 31.1 %copy-start = (bf16[1024,2048]{1,0:T(8,128)(2,1)S(1)}, bf16[1024,2048]{1,0:T(8,128)(2,1)}, u32[]{:S(2)}) copy-start(bf16[1024,2048]{1,0:T(8,128)(2,1)} %get-tuple-element.28.x1_ref) | copy-start | bytes 12582916
  47.8 31.1 %copy-start.1 = (bf16[1024,2048]{1,0:T(8,128)(2,1)S(1)}, bf16[1024,2048]{1,0:T(8,128)(2,1)}, u32[]{:S(2)}) copy-start(bf16[1024,2048]{1,0:T(8,128)(2,1)} %get-tuple-element.29.g1_ref) | copy-start | bytes 12582916
  47.8 31.1 %copy-start.4 = (s32[2]{0:T(128)S(1)}, s32[2]{0:T(128)}, u32[]{:S(2)}) copy-start(s32[2]{0:T(128)} %pad_add_fusion.place_ref) | copy-start | bytes 28
  78.9 12.2 %slice-start = ((s8[8388608]{0:T(1024)(128)(4,1)}), s8[4194304]{0:T(1024)(128)(4,1)S(1)}, s32[]{:S(2)}) async-start(s8[8388608]{0:T(1024)(128)(4,1)} %bitcast.10), calls=%async_computation.2 | async-start | bytes 8388608
  80.8 4.5 %collective-permute-start.1 = (f32[4,128,256]{2,1,0:T(8,128)S(1)}, f32[4,128,256]{2,1,0:T(8,128)S(1)}, u32[]{:S(2)}, u32[]{:S(2)}) collective-permute-start(f32[4,128,256]{2,1,0:T(8,128)S(1)} %get-tuple-element.31), channel_id=1, source_target_pairs={{0,1},{1,0},{2,3},{3,2},{4,5},{5,4},{6,7},{7,6},{8,9},{9,8},{10,11... | collective-permute-start | bytes 1572872 | tf_op jit(solution)/shard_map/ppermute | solution.py:389
  83.4 7.7 %slice-start.1 = ((s8[8388608]{0:T(1024)(128)(4,1)}), s8[4194304]{0:T(1024)(128)(4,1)S(1)}, s32[]{:S(2)}) async-start(s8[8388608]{0:T(1024)(128)(4,1)} %bitcast.10), calls=%async_computation.3 | async-start | bytes 8388608
  83.5 7.7 %copy-start.2 = (bf16[1024,128]{1,0:T(8,128)(2,1)S(1)}, bf16[1024,128]{1,0:T(8,128)(2,1)}, u32[]{:S(2)}) copy-start(bf16[1024,128]{1,0:T(8,128)(2,1)} %refs_2_.1) | copy-start | bytes 786436
  83.5 7.7 %copy-start.3 = (bf16[1024,128]{1,0:T(8,128)(2,1)S(1)}, bf16[1024,128]{1,0:T(8,128)(2,1)}, u32[]{:S(2)}) copy-start(bf16[1024,128]{1,0:T(8,128)(2,1)} %get-tuple-element.26.refs_3_) | copy-start | bytes 786436
  85.4 9.1 %collective-permute-start.2 = (f32[128,256]{1,0:T(8,128)S(1)}, f32[128,256]{1,0:T(8,128)S(1)}, u32[]{:S(2)}, u32[]{:S(2)}) collective-permute-start(f32[128,256]{1,0:T(8,128)S(1)} %get-tuple-element.38), channel_id=1, source_target_pairs={{0,4},{1,5},{2,6},{3,7},{4,0},{5,1},{6,2},{7,3},{8,12},{9,13},{10,... | collective-permute-start | bytes 393224 | tf_op jit(solution)/shard_map/ppermute | solution.py:396
  88.4 6.6 %collective-permute-start.3 = (f32[128,256]{1,0:T(8,128)S(1)}, f32[128,256]{1,0:T(8,128)S(1)}, u32[]{:S(2)}, u32[]{:S(2)}) collective-permute-start(f32[128,256]{1,0:T(8,128)S(1)} %get-tuple-element.37), channel_id=1, source_target_pairs={{0,2},{1,3},{2,4},{3,5},{4,6},{5,7},{6,0},{7,1},{8,10},{9,11},{10,... | collective-permute-start | bytes 393224 | tf_op jit(solution)/shard_map/ppermute | solution.py:396
  88.8 6.4 %collective-permute-start.4 = (f32[128,256]{1,0:T(8,128)S(1)}, f32[128,256]{1,0:T(8,128)S(1)}, u32[]{:S(2)}, u32[]{:S(2)}) collective-permute-start(f32[128,256]{1,0:T(8,128)S(1)} %get-tuple-element.36), channel_id=1, source_target_pairs={{0,6},{1,7},{2,0},{3,1},{4,2},{5,3},{6,4},{7,5},{8,14},{9,15},{10,... | collective-permute-start | bytes 393224 | tf_op jit(solution)/shard_map/ppermute | solution.py:396
